TPU v7x, 32 devices: a whole 2x2x4 slice. The times are simulated.
32 devices in a mesh: narrow: 4 (over z), wide: 8 (over y, x, core).
Axes of the slice: x: 2, y: 2, z: 4, core: 2. Of those that a mesh axis runs over, the one named last changes fastest.
Arguments:
- tokens: bfloat16 [64, 512, 768], P(('narrow', 'wide')), may hold values from -6 to 6
- w_query: bfloat16 [768, 768], P(('narrow', 'wide')), may hold values from -0.109375 to 0.109375
- w_key: bfloat16 [768, 768], P(('narrow', 'wide')), may hold values from -0.109375 to 0.109375
- w_value: bfloat16 [768, 768], P(('narrow', 'wide')), may hold values from -0.21875 to 0.21875
- w_output: bfloat16 [768, 768], P(('narrow', 'wide')), may hold values from -0.625 to 0.625
- w_router: bfloat16 [768, 32], P(('narrow', 'wide')), may hold values from -0.15625 to 0.15625
- gain_attn: bfloat16 [768], P(('narrow', 'wide')), may hold values from 0.25 to 1.75
- gain_ffn: bfloat16 [768], P(('narrow', 'wide')), may hold values from 0.25 to 1.75
- rel_bias: bfloat16 [384], P(('narrow', 'wide')), may hold values from -4 to 4
- router_bias: bfloat16 [32], P(('narrow', 'wide')), may hold values from -0.59765625 to 0.59765625
- w_in: bfloat16 [32, 768, 3072], P(('narrow', 'wide')), may hold values from -0.21875 to 0.21875
- w_out: bfloat16 [32, 3072, 768], P(('narrow', 'wide')), may hold values from -4.96875 to 4.96875
- routes: int32 [64, 512, 1], P(('narrow', 'wide')), may hold values from 0 to 31
- fill_rank: int32 [64, 512], P(('narrow', 'wide')), may hold values from 0 to 511, each once within a row
- bucket_map: int32 [1023], replicated, may hold values from 0 to 31
- upstream_grad: bfloat16 [64, 512, 768], P(('narrow', 'wide')), may hold values from -6 to 6
Outputs:
- layer_out: bfloat16 [64, 512, 768], P(('narrow', 'wide'))
- grad_tokens: bfloat16 [64, 512, 768], P(('narrow', 'wide'))
- grad_query_w: float32 [768, 768], P(('narrow', 'wide'))
- grad_key_w: float32 [768, 768], P(('narrow', 'wide'))
- grad_value_w: float32 [768, 768], P(('narrow', 'wide'))
- grad_output_w: float32 [768, 768], P(('narrow', 'wide'))
- grad_router_w: float32 [768, 32], P(('narrow', 'wide'))
- grad_gain_attn: float32 [768], P(('narrow', 'wide'))
- grad_gain_ffn: float32 [768], P(('narrow', 'wide'))
- grad_rel_bias: float32 [384], P(('narrow', 'wide'))
- grad_router_bias: float32 [32], P(('narrow', 'wide'))
- grad_w_in: float32 [32, 768, 3072], P(('narrow', 'wide'))
- grad_w_out: float32 [32, 3072, 768], P(('narrow', 'wide'))
Inputs may be any that keep to these rules, and one draw needn't show every extreme that they name: `routes`: each token's single expert. `fill_rank`: in each sequence a permutation of 0 to 511.
All inputs are finite; a program needn't handle non-finite values.
Results may differ from a plain program's by a relative error of at most 0.025.
Values may be sent and summed in bfloat16 or wider, within the bound.
No kernel may reach another device: no remote copies, remote signals or barrier semaphores. Data moves between devices by JAX's collectives and lax.ppermute only.
A program may use at most 256 MiB of HBM per device.

v0:
```python
import functools
import jax
import jax.numpy as jnp
from jax import lax
from jax.experimental import pallas as pl
from jax.experimental.pallas import tpu as pltpu
from jax.sharding import PartitionSpec as P

HEADS = 12
HEAD = 64
BUCKETS = 32
PAIR = 2 * HEAD
GROUP = 4
BLOCK = 128
LANES = 128
AXES = ("narrow", "wide")
MIB = 1024 * 1024

epsilon = 1e-06
f32 = jnp.float32
bf16 = jnp.bfloat16


def mm(a, b):
    return lax.dot_general(a, b, (((1,), (0,)), ((), ())), preferred_element_type=f32)


def mm_nt(a, b):
    return lax.dot_general(a, b, (((1,), (1,)), ((), ())), preferred_element_type=f32)


def mm_tn(a, b):
    return lax.dot_general(a, b, (((0,), (0,)), ((), ())), preferred_element_type=f32)


def norm_scale(values):
    return lax.rsqrt(jnp.mean(values * values, axis=-1, keepdims=True) + epsilon)


def softmax_rows(logits):
    shifted = jnp.exp(logits - jnp.max(logits, axis=-1, keepdims=True))
    return shifted / jnp.sum(shifted, axis=-1, keepdims=True)


def pair_mask(shape, half):
    lane = lax.broadcasted_iota(jnp.int32, shape, 1)
    return (lane < HEAD) if half == 0 else (lane >= HEAD)


def params(size):
    return pltpu.CompilerParams(vmem_limit_bytes=size * MIB)


def front_kernel(
    tokens_ref, wq_ref, wk_ref, wv_ref, wo_ref, skew_ref, gain_one_ref, gain_two_ref, spots_ref,
    q_ref, k_ref, v_ref, mixed_ref, lse_ref, sent_ref, normed_ref, resid_ref,
):
    step = pl.program_id(0)
    length, width = tokens_ref.shape

    @pl.when(step == 0)
    def start():
        acts = tokens_ref[...].astype(f32)
        normed_ref[...] = (acts * norm_scale(acts) * gain_one_ref[...]).astype(bf16)
        resid_ref[...] = acts

    normed = normed_ref[...]
    q_ref[...] = mm(normed, wq_ref[...]).astype(bf16)
    k_ref[...] = mm(normed, wk_ref[...]).astype(bf16)
    v_ref[...] = mm(normed, wv_ref[...]).astype(bf16)
    for pair in range(GROUP // 2):
        cols = slice(PAIR * pair, PAIR * (pair + 1))
        query, key, value = q_ref[:, cols], k_ref[:, cols], v_ref[:, cols]
        out = None
        for half in range(2):
            head = 2 * pair + half
            mask = pair_mask(query.shape, half)
            scores = mm_nt(jnp.where(mask, query, jnp.zeros_like(query)), key)
            parts = []
            for at in range(length // BLOCK):
                rows = slice(BLOCK * at, BLOCK * (at + 1))
                low = length - BLOCK * (at + 1)
                part = scores[rows, :] + skew_ref[head, :, low : low + length].astype(f32)
                peak = jnp.max(part, axis=-1, keepdims=True)
                part = jnp.exp(part - peak)
                total = jnp.sum(part, axis=-1, keepdims=True)
                lse_ref[0, rows, head : head + 1] = peak + jnp.log(total)
                parts.append((part * (1.0 / total)).astype(bf16))
            probs = jnp.concatenate(parts, axis=0)
            term = mm(probs, jnp.where(mask, value, jnp.zeros_like(value)))
            out = term if out is None else out + term
        mixed_ref[:, cols] = out.astype(bf16)
    resid_ref[...] += mm(mixed_ref[...], wo_ref[...])

    @pl.when(step == pl.num_programs(0) - 1)
    def finish():
        resid = resid_ref[...]
        normed_two = (resid * norm_scale(resid) * gain_two_ref[...]).astype(bf16)
        rows = lax.broadcasted_iota(jnp.int32, (sent_ref.shape[0], length), 0)
        left = mm((rows == spots_ref[0:1, :]).astype(bf16), normed_two[:, : width // 2])
        right = mm((rows == spots_ref[1:2, :]).astype(bf16), normed_two[:, width // 2 :])
        sent_ref[...] = (left + right).astype(bf16)


def front_call(tokens, wq, wk, wv, wo, skewed, gain_one, gain_two, spots, slots):
    length, width = tokens.shape
    part = GROUP * HEAD
    groups = HEADS // GROUP
    whole = lambda *shape: pl.BlockSpec(shape, lambda g: (0,) * len(shape))
    columns = lambda rows: pl.BlockSpec((rows, part), lambda g: (0, g))
    shape = jax.ShapeDtypeStruct
    return pl.pallas_call(
        front_kernel,
        grid=(groups,),
        in_specs=[
            whole(length, width), columns(width), columns(width), columns(width),
            pl.BlockSpec((part, width), lambda g: (g, 0)),
            pl.BlockSpec((GROUP, BLOCK, skewed.shape[2]), lambda g: (g, 0, 0)),
            whole(1, width), whole(1, width), whole(2, length),
        ],
        out_specs=[
            columns(length), columns(length), columns(length), columns(length),
            pl.BlockSpec((1, length, GROUP), lambda g: (g, 0, 0)),
            whole(2 * slots, width // 2),
        ],
        out_shape=[
            *(4 * [shape((length, width), bf16)]), shape((groups, length, GROUP), f32),
            shape((2 * slots, width // 2), bf16),
        ],
        scratch_shapes=[pltpu.VMEM((length, width), bf16), pltpu.VMEM((length, width), f32)],
        compiler_params=params(60),
        cost_estimate=pl.CostEstimate(
            flops=2 * length * width * width * 4 + 4 * length * length * width * 4,
            bytes_accessed=14 * MIB, transcendentals=HEADS * length * length,
        ),
        name="front",
    )(tokens, wq, wk, wv, wo, skewed, gain_one, gain_two, spots)


def bell(values):
    size = jnp.abs(values)
    t = 1.0 / (1.0 + (0.3275911 * 0.7071067811865476) * size)
    falling = jnp.exp(-0.5 * values * values)
    poly = t * (
        0.127414796
        + t * (-0.142248368 + t * (0.7107068705 + t * (-0.7265760135 + t * 0.5307027145)))
    )
    tail = poly * falling
    return jnp.where(values < 0, tail, 1.0 - tail), falling * 0.3989422804014327


def expert_kernel(
    own_ref, arrived_ref, raw_ref, wr_ref, rbias_ref, place_ref, placed_ref, win_ref, wout_ref,
    sent_ref, rows_ref, active_ref, gradinner_ref, gradresult_ref, result_acc, rows_acc,
):
    step = pl.program_id(0)
    last = pl.num_programs(0) - 1
    count = rows_ref.shape[0]
    unit = place_ref.shape[0]

    @pl.when(step == 0)
    def start():
        half = arrived_ref.shape[1]
        ids = lax.broadcasted_iota(jnp.int32, (unit, 2 * unit), 1)
        for side in range(2):
            pick = (ids == place_ref[:, side : side + 1]).astype(bf16)
            for at in range(0, count, unit):
                rows_ref[at : at + unit, half * side : half * (side + 1)] = mm(
                    pick, arrived_ref[2 * at : 2 * (at + unit), :]
                ).astype(bf16)
        probs = softmax_rows(mm(rows_ref[...], wr_ref[...]) + rbias_ref[...])
        mine = lax.broadcasted_iota(jnp.int32, probs.shape, 1) == own_ref[0]
        gate = jnp.sum(jnp.where(mine, probs, 0.0), axis=-1, keepdims=True)
        gradresult_ref[...] = (gate * raw_ref[...].astype(f32)).astype(bf16)

    inner = mm(rows_ref[...], win_ref[...])
    grad_active = mm_nt(gradresult_ref[...], wout_ref[...])
    share, density = bell(inner)
    active = (inner * share).astype(bf16)
    grad_inner = (grad_active * (share + inner * density)).astype(bf16)
    active_ref[...] = active
    gradinner_ref[...] = grad_inner
    result = mm(active, wout_ref[...])
    grad_rows = mm_nt(grad_inner, win_ref[...])

    @pl.when(step == 0)
    def first():
        result_acc[...] = result
        rows_acc[...] = grad_rows

    @pl.when(step > 0)
    def more():
        result_acc[...] += result
        rows_acc[...] += grad_rows

    @pl.when(step == last)
    def finish():
        ids = lax.broadcasted_iota(jnp.int32, (2 * unit, unit), 0)
        picks = [(ids == placed_ref[side : side + 1, :]).astype(bf16) for side in range(2)]
        for at in range(0, count, unit):
            sent_ref[2 * at : 2 * (at + unit), :] = (
                mm(picks[0], result_acc[at : at + unit, :].astype(bf16))
                + mm(picks[1], rows_acc[at : at + unit, :].astype(bf16))
            ).astype(bf16)


def expert_call(own, arrived, raw, wr, rbias, place, w_in, w_out, part=1024):
    count, width = raw.shape
    hidden = w_in.shape[1]
    experts = wr.shape[1]
    whole = lambda *shape: pl.BlockSpec(shape, lambda g, own: (0,) * len(shape))
    columns = lambda n: pl.BlockSpec((n, part), lambda g, own: (0, g))
    return pl.pallas_call(
        expert_kernel,
        grid_spec=pltpu.PrefetchScalarGridSpec(
            num_scalar_prefetch=1,
            grid=(hidden // part,),
            in_specs=[
                whole(2 * count, width // 2), whole(count, width), whole(width, experts),
                whole(1, experts), whole(*place.shape), whole(*place.shape[::-1]),
                columns(width), pl.BlockSpec((part, width), lambda g, own: (g, 0)),
            ],
            out_specs=[
                whole(2 * count, width), whole(count, width), columns(count), columns(count),
                whole(count, width),
            ],
            scratch_shapes=[pltpu.VMEM((count, width), f32), pltpu.VMEM((count, width), f32)],
        ),
        out_shape=[
            jax.ShapeDtypeStruct((2 * count, width), bf16),
            jax.ShapeDtypeStruct((count, width), bf16),
            jax.ShapeDtypeStruct((count, hidden), bf16),
            jax.ShapeDtypeStruct((count, hidden), bf16),
            jax.ShapeDtypeStruct((count, width), bf16),
        ],
        compiler_params=params(60),
        cost_estimate=pl.CostEstimate(
            flops=8 * count * width * hidden, bytes_accessed=20 * MIB,
            transcendentals=count * hidden,
        ),
        name="expert",
    )(own, arrived, raw, wr, rbias, place, place.T, w_in, w_out)


def back_rows_kernel(
    target_ref, route_ref, returned_ref, up_ref, tokens_ref, mixed_ref, gain_ref, wr_ref,
    rbias_ref, wo_ref, *refs,
):
    output_ref, gradresid_ref, gradmixed_ref, go_ref, grw_ref, ggain_ref, gbias_ref = refs[-7:]
    length = up_ref.shape[0]
    experts = wr_ref.shape[1]
    mixed = mixed_ref[...]
    resid = tokens_ref[...].astype(f32) + mm(mixed, wo_ref[...])
    scale = norm_scale(resid)
    normed_two = (resid * scale * gain_ref[...]).astype(bf16)
    router = softmax_rows(mm(normed_two, wr_ref[...]) + rbias_ref[...])
    returned = returned_ref[...]
    ids = lax.broadcasted_iota(jnp.int32, (length, returned.shape[0]), 1)
    expert_rows = mm((ids == target_ref[:, 0:1]).astype(bf16), returned)
    grad_back = mm((ids == target_ref[:, 1:2]).astype(bf16), returned)
    up = up_ref[...].astype(f32)
    hot = lax.broadcasted_iota(jnp.int32, (length, experts), 1) == route_ref[...]
    gate = jnp.sum(jnp.where(hot, router, 0.0), axis=-1, keepdims=True)
    output_ref[...] = (resid + gate * expert_rows).astype(bf16)
    grad_gate = jnp.sum(up * expert_rows, axis=-1, keepdims=True)
    grad_logits = (router * (jnp.where(hot, grad_gate, 0.0) - gate * grad_gate)).astype(bf16)
    gbias_ref[...] = jnp.sum(grad_logits.astype(f32), axis=0, keepdims=True)
    grw_ref[...] = mm_tn(normed_two, grad_logits)
    grad_normed = mm_nt(grad_logits, wr_ref[...]) + grad_back
    ggain_ref[...] = jnp.sum(grad_normed * resid * scale, axis=0, keepdims=True)
    weighted = grad_normed * gain_ref[...]
    slope = scale * scale * scale * jnp.mean(weighted * resid, axis=-1, keepdims=True)
    grad_resid = up + (scale * weighted - resid * slope)
    gradresid_ref[...] = grad_resid
    grad_branch = grad_resid.astype(bf16)
    go = mm_tn(mixed, grad_branch)
    if len(refs) > 7:
        go = go + refs[0][...].astype(f32)
    go_ref[...] = go.astype(bf16)
    gradmixed_ref[...] = mm_nt(grad_branch, wo_ref[...]).astype(bf16)


def back_rows_call(target, route, returned, up, tokens, mixed, gain, wr, rbias, wo, prior):
    length, width = up.shape
    experts = wr.shape[1]
    shape = jax.ShapeDtypeStruct
    return pl.pallas_call(
        back_rows_kernel,
        out_shape=[
            shape((length, width), bf16), shape((length, width), f32),
            shape((length, width), bf16), shape((width, width), bf16),
            shape((width, experts), f32), shape((1, width), f32), shape((1, experts), f32),
        ],
        compiler_params=params(60),
        cost_estimate=pl.CostEstimate(
            flops=2 * length * width * (3 * width + 2 * returned.shape[0]),
            bytes_accessed=12 * MIB, transcendentals=0,
        ),
        name="back_rows",
    )(
        target, route, returned, up, tokens, mixed, gain, wr, rbias, wo,
        *([] if prior is None else [prior]),
    )


def back_heads_kernel(
    tokens_ref, gain_ref, gradmixed_ref, mixed_ref, wq_ref, wk_ref, wv_ref, q_ref, k_ref, v_ref,
    skew_ref, lse_ref, gradresid_ref, *refs,
):
    prior_ref = refs[0] if len(refs) > 7 else None
    line_ref, gw_ref, gradacts_ref, ggain_ref, normedt_ref, acc_ref, fold_ref = refs[-7:]
    step = pl.program_id(0)
    last = pl.num_programs(0) - 1
    length, width = tokens_ref.shape
    span = 2 * length

    @pl.when(step == 0)
    def start():
        acts = tokens_ref[...].astype(f32)
        normed = (acts * norm_scale(acts) * gain_ref[...]).astype(bf16)
        normedt_ref[...] = normed.T
        acc_ref[...] = jnp.zeros_like(acc_ref)

    dq, dk, dv = [], [], []
    for pair in range(GROUP // 2):
        cols = slice(PAIR * pair, PAIR * (pair + 1))
        query, key, value = q_ref[:, cols], k_ref[:, cols], v_ref[:, cols]
        grad = gradmixed_ref[:, cols]
        product = grad.astype(f32) * mixed_ref[:, cols].astype(f32)
        gq = gk = gv = None
        for half in range(2):
            head = 2 * pair + half
            mask = pair_mask(query.shape, half)
            clear = lambda a: jnp.where(mask, a, jnp.zeros_like(a))
            own, asked = clear(grad), clear(query)
            center = jnp.sum(clear(product), axis=-1, keepdims=True)
            scores = mm_nt(asked, key)
            grad_probs = mm_nt(own, value)
            all_probs, all_grads = [], []
            for at in range(length // BLOCK):
                rows = slice(BLOCK * at, BLOCK * (at + 1))
                low = length - BLOCK * (at + 1)
                part = scores[rows, :] + skew_ref[head, :, low : low + length].astype(f32)
                probs = jnp.exp(part - lse_ref[0, rows, head : head + 1])
                piece = probs * (grad_probs[rows, :] - center[rows, :])
                if at == 0:
                    fold_ref[:, :low] = jnp.zeros((BLOCK, low), f32)
                    fold_ref[:, low : low + length] = piece
                    fold_ref[:, low + length :] = jnp.zeros((BLOCK, length - low), f32)
                else:
                    fold_ref[:, low : low + length] += piece
                all_probs.append(probs.astype(bf16))
                all_grads.append(piece.astype(bf16))
            rows = fold_ref[...]
            size = BLOCK
            while size > 1:
                size //= 2
                rows = rows[:size] + pltpu.roll(rows[size:], span - size, 1)
            line_ref[0, head : head + 1, :] = pltpu.roll(rows, BLOCK - 1, 1)
            probs = jnp.concatenate(all_probs, axis=0)
            grad_scores = jnp.concatenate(all_grads, axis=0)
            a = mm(grad_scores, clear(key))
            b = mm_tn(grad_scores, asked)
            c = mm_tn(probs, own)
            gq = a if gq is None else gq + a
            gk = b if gk is None else gk + b
            gv = c if gv is None else gv + c
        dq.append(gq.astype(bf16))
        dk.append(gk.astype(bf16))
        dv.append(gv.astype(bf16))
    dq, dk, dv = (jnp.concatenate(x, axis=1) for x in (dq, dk, dv))
    normedt = normedt_ref[...]
    for i, grad in enumerate((dq, dk, dv)):
        total = mm(normedt, grad)
        if prior_ref is not None:
            total = total + prior_ref[i].astype(f32)
        gw_ref[i] = total.astype(bf16)
    acc_ref[...] += mm_nt(dq, wq_ref[...]) + mm_nt(dk, wk_ref[...]) + mm_nt(dv, wv_ref[...])

    @pl.when(step == last)
    def finish():
        grad_normed = acc_ref[...]
        acts = tokens_ref[...].astype(f32)
        scale = norm_scale(acts)
        ggain_ref[...] = jnp.sum(grad_normed * acts * scale, axis=0, keepdims=True)
        weighted = grad_normed * gain_ref[...]
        slope = scale * scale * scale * jnp.mean(weighted * acts, axis=-1, keepdims=True)
        grad_acts = gradresid_ref[...] + (scale * weighted - acts * slope)
        gradacts_ref[...] = grad_acts.astype(bf16)


def back_heads_call(
    tokens, gain, grad_mixed, mixed, wq, wk, wv, q, k, v, skewed, lse, grad_resid, prior
):
    length, width = tokens.shape
    part = GROUP * HEAD
    groups = HEADS // GROUP
    whole = lambda *shape: pl.BlockSpec(shape, lambda g: (0,) * len(shape))
    columns = lambda size: pl.BlockSpec((size, part), lambda g: (0, g))
    shape = jax.ShapeDtypeStruct
    weights = pl.BlockSpec((3, width, part), lambda g: (0, 0, g))
    return pl.pallas_call(
        back_heads_kernel,
        grid=(groups,),
        in_specs=[
            whole(length, width), whole(1, width), columns(length), columns(length),
            columns(width), columns(width), columns(width),
            columns(length), columns(length), columns(length),
            pl.BlockSpec((GROUP, BLOCK, skewed.shape[2]), lambda g: (g, 0, 0)),
            pl.BlockSpec((1, length, GROUP), lambda g: (g, 0, 0)), whole(length, width),
            *([] if prior is None else [weights]),
        ],
        out_specs=[
            pl.BlockSpec((1, GROUP, 2 * length), lambda g: (g, 0, 0)), weights,
            whole(length, width), whole(1, width),
        ],
        out_shape=[
            shape((groups, GROUP, 2 * length), f32), shape((3, width, width), bf16),
            shape((length, width), bf16), shape((1, width), f32),
        ],
        scratch_shapes=[
            pltpu.VMEM((width, length), bf16), pltpu.VMEM((length, width), f32),
            pltpu.VMEM((BLOCK, 2 * length), f32),
        ],
        compiler_params=params(60),
        cost_estimate=pl.CostEstimate(
            flops=groups * (2 * length * width * part * 6 + 8 * length * length * part * 4),
            bytes_accessed=21 * MIB, transcendentals=HEADS * length * length,
        ),
        name="back_heads",
    )(
        tokens, gain, grad_mixed, mixed, wq, wk, wv, q, k, v, skewed, lse, grad_resid,
        *([] if prior is None else [prior]),
    )


def pack_kernel(*refs):
    for at, ref in enumerate(refs[:-1]):
        refs[-1][at] = ref[...]


def pack_call(*parts):
    return pl.pallas_call(
        pack_kernel,
        out_shape=jax.ShapeDtypeStruct((len(parts), *parts[0].shape), parts[0].dtype),
        compiler_params=params(8),
        name="pack",
    )(*parts)


def skew_kernel(lines_ref, out_ref):
    heads, block, span = out_ref.shape
    full = lines_ref.shape[1]
    for head in range(heads):
        row = jnp.broadcast_to(lines_ref[head : head + 1, :], (16, full))
        base = pltpu.roll(row, full - (block - 1), 1, stride=1, stride_axis=0)
        for at in range(0, block, 16):
            turned = base if at == 0 else pltpu.roll(base, at, 1)
            out_ref[head, at : at + 16, :] = turned[:, :span].astype(bf16)


def skew_call(lines, block):
    heads, span = lines.shape
    return pl.pallas_call(
        skew_kernel,
        out_shape=jax.ShapeDtypeStruct((heads, block, span - block), bf16),
        compiler_params=params(16),
        name="skew",
    )(lines)


def exchange(buffer):
    return lax.all_to_all(buffer, AXES, split_axis=0, concat_axis=0, tiled=True)


def swap(value, bit):
    devices = lax.axis_size(AXES)
    return lax.ppermute(value, AXES, [(at, at ^ (1 << bit)) for at in range(devices)])


def own_bit(bit):
    return ((lax.axis_index(AXES) >> bit) & 1) == 1


def gather_step(held, bit):
    value, done = held
    theirs = swap(value, bit)
    upper = own_bit(bit)
    place = sum(1 for other in done if other > bit)
    value = jnp.stack(
        [jnp.where(upper, theirs, value), jnp.where(upper, value, theirs)], axis=place
    )
    return value, done + [bit]


def gather_all(value, order):
    held = (value, [])
    for bit in order:
        held = gather_step(held, bit)
    return held[0].reshape((-1,) + value.shape)


def scatter_step(held, bit):
    value, left = held
    place = 1 + left.index(bit)
    low = lax.index_in_dim(value, 0, place, keepdims=False)
    high = lax.index_in_dim(value, 1, place, keepdims=False)
    upper = own_bit(bit)
    sent = jnp.where(upper, low, high).astype(bf16)
    value = jnp.where(upper, high, low).astype(f32) + swap(sent, bit).astype(f32)
    return value, [other for other in left if other != bit]


def pack_rows(parts, width):
    lead = parts[0].shape[0]
    flat = jnp.concatenate([part.reshape(lead, -1) for part in parts], axis=1)
    short = -flat.shape[1] % width
    return jnp.pad(flat, ((0, 0), (0, short))).reshape(lead, -1, width)


def unpack_rows(packed, sizes):
    flat = packed.reshape(packed.shape[0], -1)
    out, at = [], 0
    for size in sizes:
        out.append(flat[:, at : at + size])
        at += size
    return out


def body(
    tokens,
    w_query,
    w_key,
    w_value,
    w_output,
    w_router,
    gain_attn,
    gain_ffn,
    rel_bias,
    router_bias,
    w_in,
    w_out,
    routes,
    fill_rank,
    bucket_map,
    upstream_grad,
):
    batches, length, width = tokens.shape
    devices = lax.axis_size(AXES)
    wide_bits = lax.axis_size("wide").bit_length() - 1
    bits = devices.bit_length() - 1
    local_experts = w_in.shape[0]
    experts = local_experts * devices
    capacity = max(2, 5 * length // (4 * experts))
    slots = experts * capacity
    span = 2 * length
    far = list(range(wide_bits, bits))
    near = list(range(1, wide_bits))
    turned = near[1:] + near[:1]

    expert_ids = jnp.arange(experts, dtype=jnp.int32)

    def plan(route, order):
        route_hot = (route[:, None] == expert_ids[None, :]).astype(f32)
        earlier = (order[None, :] < order[:, None]).astype(bf16)
        counts = jnp.dot(earlier, route_hot.astype(bf16), preferred_element_type=f32)
        slot = jnp.sum(counts * route_hot, axis=-1).astype(jnp.int32)
        first = jnp.where(slot < capacity, route * (2 * capacity) + slot, -1)
        second = jnp.where(first >= 0, first + capacity, -1)
        return jnp.stack([first, second], axis=0)

    small_parts = [w_router, gain_attn, gain_ffn, rel_bias, router_bias]
    small = pack_rows([part.reshape(1, -1) for part in small_parts], 8 * LANES)
    square = (pack_call(w_query, w_key, w_value, w_output), [])
    small = (small.reshape(8, LANES), [])
    for bit in far[::-1]:
        square, small = gather_step(square, bit), gather_step(small, bit)
    value, ahead = lax.optimization_barrier((square[0], small[0]))
    small = (ahead, small[1])
    done = far[::-1]
    value = value.reshape((2,) * len(far) + (4, -1, width))
    low, high = ((lax.slice_in_dim(value, i, i + 2, axis=len(far)), done) for i in (0, 2))
    raw_inputs = (routes, fill_rank, upstream_grad)
    for number, (one, two) in enumerate(zip(near[::-1], turned[::-1])):
        low, high = gather_step(low, one), gather_step(high, two)
        if number == 0:
            for bit in near[::-1]:
                small = gather_step(small, bit)
            first, second, ahead = lax.optimization_barrier((low[0], high[0], small[0]))
            low, high = (first, low[1]), (second, high[1])
            small_all = gather_step((ahead, small[1]), 0)[0]
            small_all, *raw_inputs = lax.optimization_barrier((small_all, *raw_inputs))

    raw_routes, raw_ranks, raw_upstream = raw_inputs
    spots = [plan(raw_routes[at, :, 0], raw_ranks[at]) for at in range(batches)]
    raw_spots = jnp.concatenate([spots[at][at] for at in range(batches)], axis=0)
    raw_ids = jnp.arange(2 * slots, dtype=jnp.int32)
    raw_sent = jnp.dot(
        (raw_ids[:, None] == raw_spots[None, :]).astype(bf16),
        raw_upstream.reshape(batches * length, width),
        preferred_element_type=f32,
    ).astype(bf16)
    raw_arrived = exchange(raw_sent.reshape(devices, 2 * capacity, width))

    wr_all, gain_one, gain_two, rel_flat, bias_all = unpack_rows(
        small_all.reshape(devices, 1, -1), [part.size for part in small_parts]
    )
    wr_all = wr_all.reshape(width, experts)
    gain_one = gain_one.reshape(1, width).astype(f32)
    gain_two = gain_two.reshape(1, width).astype(f32)
    bias_all = bias_all.reshape(1, experts).astype(f32)
    table = rel_flat.reshape(BUCKETS, HEADS).T
    bucket_hot = (
        jnp.arange(BUCKETS, dtype=jnp.int32)[:, None]
        == jnp.pad(bucket_map, (0, 1), constant_values=-1)[None, :]
    ).astype(bf16)
    skewed = skew_call(jnp.dot(table, bucket_hot, preferred_element_type=f32), BLOCK)
    first, second, skewed = lax.optimization_barrier((low[0], high[0], skewed))
    low, high = gather_step((first, low[1]), 0), gather_step((second, high[1]), 0)
    wq, wk, wv, wo = (
        lax.index_in_dim(part[0].reshape(devices, 2, -1, width), i, 1).reshape(width, width)
        for part in (low, high)
        for i in range(2)
    )

    own = lax.axis_index(AXES).astype(jnp.int32).reshape(1)
    count = 8 if 8 * capacity % 16 == 0 else 16
    row = jnp.arange(count * capacity, dtype=jnp.int32)
    place = row + (row // capacity) * capacity
    place = jnp.stack([place, place + capacity], axis=1)

    fronts, arrived, returned = [], [], []
    for at in range(batches):
        acts = tokens[at]
        if at == 1:
            acts, raw_arrived = lax.optimization_barrier((acts, raw_arrived))
        front = front_call(
            acts, wq, wk, wv, wo, skewed, gain_one, gain_two, spots[at], slots
        )
        fronts.append(front)
        arrived.append(exchange(front[-1].reshape(devices, 2 * capacity, width // 2)))
    raw = raw_arrived.reshape(devices, 2, capacity, width)
    grad_in = grad_out = 0.0
    for at in range(batches):
        sent, rows, active, grad_inner, grad_result = expert_call(
            own,
            arrived[at].reshape(2 * slots, width // 2),
            raw[:, at].reshape(slots, width),
            wr_all,
            bias_all,
            place,
            w_in[0],
            w_out[0],
        )
        grad_in += jnp.einsum("rd,rf->df", rows, grad_inner, preferred_element_type=f32)
        grad_out += jnp.einsum("rf,rd->fd", active, grad_result, preferred_element_type=f32)
        back = exchange(sent.reshape(devices, 2 * capacity, width))
        back, grad_in, grad_out = lax.optimization_barrier((back, grad_in, grad_out))
        returned.append(back)

    row_parts, head_parts = [], []
    g_output = g_heads = None
    for at in range(batches):
        q, k, v, mixed, lse, sent = fronts[at]
        row_part = back_rows_call(
            spots[at].T, routes[at], returned[at].reshape(2 * slots, width), upstream_grad[at],
            tokens[at], mixed, gain_two, wr_all, bias_all, wo, g_output,
        )
        g_output = row_part[3]
        head_part = back_heads_call(
            tokens[at], gain_one, row_part[2], mixed, wq, wk, wv, q, k, v, skewed, lse,
            row_part[1], g_heads,
        )
        g_heads = head_part[1]
        row_parts.append(row_part)
        head_parts.append(head_part)

    parts = jnp.concatenate([g_heads, g_output[None]], axis=0)
    held = scatter_step((parts.reshape((4,) + (2,) * bits + (-1, width)), list(range(bits))[::-1]), 0)
    low, high = ((held[0][i : i + 2], held[1]) for i in (0, 2))
    for one, two in zip(near, turned):
        low, high = scatter_step(low, one), scatter_step(high, two)
    held = (jnp.concatenate([low[0], high[0]], axis=0), low[1])
    for bit in far:
        held = scatter_step(held, bit)
    r_query, r_key, r_value, r_output = (held[0][i] for i in range(4))

    g_router, g_gain_two, g_bias = (
        sum(row_part[i] for row_part in row_parts) for i in range(4, 7)
    )
    lines, g_gain_one = (sum(part[i] for part in head_parts) for i in (0, 3))
    g_rel = jnp.einsum(
        "hn,bn->bh",
        lines.reshape(HEADS, span),
        bucket_hot.astype(f32),
        precision=lax.Precision.HIGHEST,
    )
    small_grads = [g_router, g_gain_one, g_gain_two, g_rel, g_bias]
    small_pack = pack_rows([part.reshape(devices, -1) for part in small_grads], 8 * LANES)
    held = (
        small_pack.reshape((1,) + (2,) * bits + (-1, LANES)), list(range(bits))[::-1]
    )
    for bit in [0] + near + far:
        held = scatter_step(held, bit)
    small_sum = held[0]
    tail = unpack_rows(small_sum.reshape(1, 1, -1), [part.size // devices for part in small_grads])
    r_router, r_gain_one, r_gain_two, r_rel, r_bias = (
        part.reshape(shape)
        for part, shape in zip(
            tail,
            (w_router.shape, gain_attn.shape, gain_ffn.shape, rel_bias.shape, router_bias.shape),
        )
    )
    return (
        jnp.stack([row_part[0] for row_part in row_parts], axis=0),
        jnp.stack([part[2] for part in head_parts], axis=0),
        r_query,
        r_key,
        r_value,
        r_output,
        r_router,
        r_gain_one,
        r_gain_two,
        r_rel,
        r_bias,
        grad_in[None],
        grad_out[None],
    )


def solution(mesh):
    both = P(AXES)
    in_specs = (both,) * 14 + (P(), both)
    out_specs = (both,) * 13
    return jax.shard_map(body, mesh=mesh, in_specs=in_specs, out_specs=out_specs, check_vma=False)
```

profile of v0, /device:TPU:0, one launch (start us, length us, event | category | flops | bytes accessed | tf_op | source)
XLA Modules:
  0.0 368.6 jit_solution(17915232440679044861)
XLA Ops:
  12.1 7.4 %collective-permute-done = bf16[4,24,768]{2,1,0:T(8,128)(2,1)S(1)} collective-permute-done((bf16[4,24,768]{2,1,0:T(8,128)(2,1)S(1)}, bf16[4,24,768]{2,1,0:T(8,128)(2,1)S(1)}, u32[]{:S(2)}, u32[]{:S(2)}) %collective-permute-start) | collective-permute-done | bytes 147488 | tf_op jit(solution)/shard_map/ppermute | solution.py:478
  19.7 7.8 %collective-permute-done.1 = bf16[2,4,24,768]{3,2,1,0:T(8,128)(2,1)S(1)} collective-permute-done((bf16[2,4,24,768]{3,2,1,0:T(8,128)(2,1)S(1)}, bf16[2,4,24,768]{3,2,1,0:T(8,128)(2,1)S(1)}, u32[]{:S(2)}, u32[]{:S(2)}) %collective-permute-start.1) | collective-permute-done | bytes 294944 | tf_op jit(solution)/shard_map/ppermute | solution.py:478
  35.4 4.3 %collective-permute-done.5 = bf16[2,2,2,24,768]{4,3,2,0,1:T(8,128)(2,1)S(1)} collective-permute-done((bf16[2,2,2,24,768]{4,3,2,0,1:T(8,128)(2,1)S(1)}, bf16[2,2,2,24,768]{4,3,2,0,1:T(8,128)(2,1)S(1)}, u32[]{:S(2)}, u32[]{:S(2)}) %collective-permute-start.5) | collective-permute-done | bytes 294944 | tf_op jit(solution)/shard_map/ppermute | solution.py:478
  75.9 15.5 %front.2 = (bf16[512,768]{1,0:T(8,128)(2,1)}, bf16[512,768]{1,0:T(8,128)(2,1)}, bf16[512,768]{1,0:T(8,128)(2,1)}, bf16[512,768]{1,0:T(8,128)(2,1)}, f32[3,512,4]{2,1,0:T(8,128)}, /*index=5*/bf16[1280,384]{1,0:T(8,128)(2,1)}) custom-call(bf16[512,768]{1,0:T(8,128)(2,1)} %get-tuple-element.161.tokens_ref, bf16[768,768]{1,0:T(8,128)(2,1)} %bitcast.308, ...), custom_call_target="tpu_custom_call" | custom-call | flops 5637144576 | bytes 14680064 | tf_op jit(solution)/shard_map/front/pallas_call | solution.py:112
  91.4 5.8 %all-to-all-done.1 = bf16[32,40,768]{2,1,0:T(8,128)(2,1)S(1)} async-done(((bf16[32,40,768]{2,1,0:T(8,128)(2,1)}), bf16[32,40,768]{2,1,0:T(8,128)(2,1)S(1)}, u32[]{:S(2)}, u32[]{:S(2)}) %all-to-all-start.1) | async-done | bytes 1966112 | tf_op jit(solution)/shard_map/all_to_all | solution.py:473
  97.2 4.2 %all-to-all-start = ((bf16[32,40,384]{2,1,0:T(8,128)(2,1)}), bf16[32,40,384]{2,1,0:T(8,128)(2,1)S(1)}, u32[]{:S(2)}, u32[]{:S(2)}) async-start(bf16[32,40,384]{2,1,0:T(8,128)(2,1)} %bitcast.323), calls=%async_computation | async-start | bytes 1966080 | tf_op jit(solution)/shard_map/all_to_all | solution.py:473
  102.0 15.5 %front.3 = (bf16[512,768]{1,0:T(8,128)(2,1)}, bf16[512,768]{1,0:T(8,128)(2,1)}, bf16[512,768]{1,0:T(8,128)(2,1)}, bf16[512,768]{1,0:T(8,128)(2,1)}, f32[3,512,4]{2,1,0:T(8,128)}, /*index=5*/bf16[1280,384]{1,0:T(8,128)(2,1)}) custom-call(bf16[512,768]{1,0:T(8,128)(2,1)} %get-tuple-element.99.tokens_ref, bf16[768,768]{1,0:T(8,128)(2,1)} %bitcast.309, ...), custom_call_target="tpu_custom_call" | custom-call | flops 5637144576 | bytes 14680064 | tf_op jit(solution)/shard_map/front/pallas_call | solution.py:112
  117.5 8.7 %all-to-all-done = bf16[32,40,384]{2,1,0:T(8,128)(2,1)S(1)} async-done(((bf16[32,40,384]{2,1,0:T(8,128)(2,1)}), bf16[32,40,384]{2,1,0:T(8,128)(2,1)S(1)}, u32[]{:S(2)}, u32[]{:S(2)}) %all-to-all-start) | async-done | bytes 983072 | tf_op jit(solution)/shard_map/all_to_all | solution.py:473
  137.5 22.8 %expert.2 = (bf16[1280,768]{1,0:T(8,128)(2,1)}, bf16[640,768]{1,0:T(8,128)(2,1)}, bf16[640,3072]{1,0:T(8,128)(2,1)}, bf16[640,3072]{1,0:T(8,128)(2,1)}, bf16[640,768]{1,0:T(8,128)(2,1)}) custom-call(s32[1]{0:T(128)} %bitcast.28.own_ref, bf16[1280,384]{1,0:T(8,128)(2,1)} %bitcast.321, bf16[640,768]{1,0:T(8,128)(2,1)} %reshape_squeeze.6.raw_ref, ...), custom_call_target="tpu_custom_call" | custom-call | flops 12079595520 | bytes 20971520 | tf_op jit(solution)/shard_map/expert/pallas_call | solution.py:213
  161.2 6.4 %all-to-all-start.2 = ((bf16[32,40,768]{2,1,0:T(8,128)(2,1)}), bf16[32,40,768]{2,1,0:T(8,128)(2,1)}, u32[]{:S(2)}, u32[]{:S(2)}) async-start(bf16[32,40,768]{2,1,0:T(8,128)(2,1)} %bitcast.301), calls=%async_computation.2 | async-start | bytes 3932160 | tf_op jit(solution)/shard_map/all_to_all | solution.py:473
  174.0 8.4 %fusion.49 = f32[768,3072]{1,0:T(8,128)} fusion(bf16[640,768]{1,0:T(8,128)(2,1)S(1)} %copy-done.16, bf16[640,3072]{1,0:T(8,128)(2,1)} %get-tuple-element.93), kind=kOutput, calls=%fused_computation.172 | convolution fusion | flops 3019898880 | bytes 14352384 | tf_op jit(solution)/shard_map/rd,rf->df/dot_general | solution.py:655
  182.4 22.8 %expert.3 = (bf16[1280,768]{1,0:T(8,128)(2,1)}, bf16[640,768]{1,0:T(8,128)(2,1)}, bf16[640,3072]{1,0:T(8,128)(2,1)}, bf16[640,3072]{1,0:T(8,128)(2,1)}, bf16[640,768]{1,0:T(8,128)(2,1)}) custom-call(s32[1]{0:T(128)} %bitcast.28.own_ref, bf16[1280,384]{1,0:T(8,128)(2,1)} %bitcast.320, bf16[640,768]{1,0:T(8,128)(2,1)} %reshape_squeeze.7.raw_ref, ...), custom_call_target="tpu_custom_call" | custom-call | flops 12079595520 | bytes 20971520 | tf_op jit(solution)/shard_map/expert/pallas_call | solution.py:213
  205.2 8.4 %all-to-all-done.2 = bf16[32,40,768]{2,1,0:T(8,128)(2,1)} async-done(((bf16[32,40,768]{2,1,0:T(8,128)(2,1)}), bf16[32,40,768]{2,1,0:T(8,128)(2,1)}, u32[]{:S(2)}, u32[]{:S(2)}) %all-to-all-start.2) | async-done | bytes 1966112 | tf_op jit(solution)/shard_map/all_to_all | solution.py:473
  213.6 4.3 %all-to-all-start.4 = ((bf16[32,40,768]{2,1,0:T(8,128)(2,1)}), bf16[32,40,768]{2,1,0:T(8,128)(2,1)}, u32[]{:S(2)}, u32[]{:S(2)}) async-start(bf16[32,40,768]{2,1,0:T(8,128)(2,1)} %bitcast.300), calls=%async_computation.4 | async-start | bytes 3932160 | tf_op jit(solution)/shard_map/all_to_all | solution.py:473
  217.9 8.5 %fusion.50 = f32[3072,768]{1,0:T(8,128)} fusion(bf16[640,3072]{1,0:T(8,128)(2,1)} %get-tuple-element.94, bf16[640,768]{1,0:T(8,128)(2,1)S(1)} %copy-done.33), kind=kOutput, calls=%fused_computation.173 | convolution fusion | flops 3019898880 | bytes 14352384 | tf_op jit(solution)/shard_map/rf,rd->fd/dot_general | solution.py:656
  226.4 9.3 %back_rows.2 = (bf16[512,768]{1,0:T(8,128)(2,1)}, f32[512,768]{1,0:T(8,128)}, bf16[512,768]{1,0:T(8,128)(2,1)}, bf16[768,768]{1,0:T(8,128)(2,1)}, f32[768,32]{1,...) custom-call(s32[512,2]{1,0:T(8,128)} %bitcast.335, s32[512,1]{1,0:T(8,128)} %copy.164.route_ref, ...), custom_call_target="tpu_custom_call" | custom-call | flops 3825205248 | bytes 12582912 | tf_op jit(solution)/shard_map/back_rows/pallas_call | solution.py:287
  235.7 21.3 %back_heads.2 = (f32[3,4,1024]{2,1,0:T(4,128)}, bf16[3,768,768]{2,1,0:T(8,128)(2,1)}, bf16[512,768]{1,0:T(8,128)(2,1)}, f32[1,768]{1,0:T(1,128)}) custom-call(bf16[512,768]{1,0:T(8,128)(2,1)} %get-tuple-element.161.tokens_ref, f32[1,768]{1,0:T(1,128)} %reshape.639.gain_one_ref.gain_ref, bf16[512,768]{1,0:T(8,128)(2,1)} %get-tuple-element.112.gradmixed_ref, ...), custom_call_target="tpu_custom_call" | custom-call | flops 10066329600 | bytes 22020096 | tf_op jit(solution)/shard_map/back_heads/pallas_call | solution.py:402
  257.0 9.1 %convolution_add_fusion.1 = f32[768,3072]{1,0:T(8,128)} fusion(f32[768,3072]{1,0:T(8,128)} %fusion.49, bf16[640,768]{1,0:T(8,128)(2,1)} %get-tuple-element.103, bf16[640,3072]{1,0:T(8,128)(2,1)S(1)} %copy-done.8), kind=kOutput, calls=%fused_computation.3 | convolution fusion | flops 3022258176 | bytes 23789568 | tf_op jit(solution)/shard_map/rd,rf->df/dot_general | solution.py:655
  266.1 9.0 %convolution_add_fusion = f32[3072,768]{1,0:T(8,128)} fusion(f32[3072,768]{1,0:T(8,128)} %fusion.50, bf16[640,3072]{1,0:T(8,128)(2,1)S(1)} %copy-done.7, bf16[640,768]{1,0:T(8,128)(2,1)S(1)} %copy-done.15), kind=kOutput, calls=%fused_computation.2 | convolution fusion | flops 3022258176 | bytes 23789568 | tf_op jit(solution)/shard_map/rf,rd->fd/dot_general | solution.py:656
  275.1 9.6 %back_rows.3 = (bf16[512,768]{1,0:T(8,128)(2,1)}, f32[512,768]{1,0:T(8,128)}, bf16[512,768]{1,0:T(8,128)(2,1)}, bf16[768,768]{1,0:T(8,128)(2,1)}, f32[768,32]{1,...) custom-call(s32[512,2]{1,0:T(8,128)} %bitcast.334, s32[512,1]{1,0:T(8,128)} %copy.168.route_ref, ...), custom_call_target="tpu_custom_call" | custom-call | flops 3825205248 | bytes 12582912 | tf_op jit(solution)/shard_map/back_rows/pallas_call | solution.py:287
  284.7 21.4 %back_heads.3 = (f32[3,4,1024]{2,1,0:T(4,128)}, bf16[3,768,768]{2,1,0:T(8,128)(2,1)}, bf16[512,768]{1,0:T(8,128)(2,1)}, f32[1,768]{1,0:T(1,128)}) custom-call(bf16[512,768]{1,0:T(8,128)(2,1)} %get-tuple-element.99.tokens_ref, f32[1,768]{1,0:T(1,128)} %reshape.639.gain_one_ref.gain_ref, bf16[512,768]{1,0:T(8,128)(2,1)} %get-tuple-element.119.gradmixed_ref, ...), custom_call_target="tpu_custom_call" | custom-call | flops 10066329600 | bytes 22020096 | tf_op jit(solution)/shard_map/back_heads/pallas_call | solution.py:402
  335.4 7.4 %collective-permute-done.14 = bf16[2,2,2,2,24,768]{5,4,0,1,2,3:T(8,128)(2,1)S(1)} collective-permute-done((bf16[2,2,2,2,24,768]{5,4,0,1,2,3:T(8,128)(2,1)S(1)}, bf16[2,2,2,2,24,768]{5,4,0,1,2,3:T(8,128)(2,1)S(1)}, u32[]{:S(2)}, u32[]{:S(2)}) %collective-permute-start.14) | collective-permute-done | bytes 589856 | tf_op jit(solution)/shard_map/ppermute | solution.py:478
  346.4 4.9 %collective-permute-done.17 = bf16[2,2,2,24,768]{4,3,0,1,2:T(8,128)(2,1)S(1)} collective-permute-done((bf16[2,2,2,24,768]{4,3,0,1,2:T(8,128)(2,1)S(1)}, bf16[2,2,2,24,768]{4,3,0,1,2:T(8,128)(2,1)S(1)}, u32[]{:S(2)}, u32[]{:S(2)}) %collective-permute-start.17) | collective-permute-done | bytes 294944 | tf_op jit(solution)/shard_map/ppermute | solution.py:478
  354.0 6.1 %collective-permute-done.18 = bf16[4,2,24,768]{3,2,0,1:T(8,128)(2,1)S(1)} collective-permute-done((bf16[4,2,24,768]{3,2,0,1:T(8,128)(2,1)S(1)}, bf16[4,2,24,768]{3,2,0,1:T(8,128)(2,1)S(1)}, u32[]{:S(2)}, u32[]{:S(2)}) %collective-permute-start.18) | collective-permute-done | bytes 294944 | tf_op jit(solution)/shard_map/ppermute | solution.py:478
  (235 shorter events, 117.3 us)
Async XLA Ops:
  2.9 7.3 %collective-permute-start.2 = (bf16[8,128]{1,0:T(8,128)(2,1)S(1)}, bf16[8,128]{1,0:T(8,128)(2,1)S(1)}, u32[]{:S(2)}, u32[]{:S(2)}) collective-permute-start(bf16[8,128]{1,0:T(8,128)(2,1)S(1)} %bitcast.341), channel_id=1, source_target_pairs={{0,16},{1,17},{2,18},{3,19},{4,20},{5,21},{6,22},{7,23},{8,24},{9,... | collective-permute-start | bytes 6152 | tf_op jit(solution)/shard_map/ppermute | solution.py:478
  10.1 9.4 %collective-permute-start = (bf16[4,24,768]{2,1,0:T(8,128)(2,1)S(1)}, bf16[4,24,768]{2,1,0:T(8,128)(2,1)S(1)}, u32[]{:S(2)}, u32[]{:S(2)}) collective-permute-start(bf16[4,24,768]{2,1,0:T(8,128)(2,1)S(1)} %pack.1), channel_id=1, source_target_pairs={{0,16},{1,17},{2,18},{3,19},{4,20},{5,21},{6,22},{7,23},{8,24},{9,... | collective-permute-start | bytes 442376 | tf_op jit(solution)/shard_map/ppermute | solution.py:478
  10.2 9.5 %collective-permute-start.3 = (bf16[2,8,128]{2,1,0:T(8,128)(2,1)S(1)}, bf16[2,8,128]{2,1,0:T(8,128)(2,1)S(1)}, u32[]{:S(2)}, u32[]{:S(2)}) collective-permute-start(bf16[2,8,128]{2,1,0:T(8,128)(2,1)S(1)} %pad_maximum_fusion.16), channel_id=1, source_target_pairs={{0,8},{1,9},{2,10},{3,11},{4,12},{5,13},{6,14},{7,15},{8,0},{9,1},... | collective-permute-start | bytes 12296 | tf_op jit(solution)/shard_map/ppermute | solution.py:478
  19.6 7.9 %collective-permute-start.1 = (bf16[2,4,24,768]{3,2,1,0:T(8,128)(2,1)S(1)}, bf16[2,4,24,768]{3,2,1,0:T(8,128)(2,1)S(1)}, u32[]{:S(2)}, u32[]{:S(2)}) collective-permute-start(bf16[2,4,24,768]{3,2,1,0:T(8,128)(2,1)S(1)} %pad_maximum_fusion.11), channel_id=1, source_target_pairs={{0,8},{1,9},{2,10},{3,11},{4,12},{5,13},{6,14},{7,15},{8,0},{9,1},... | collective-permute-start | bytes 884744 | tf_op jit(solution)/shard_map/ppermute | solution.py:478
  32.9 6.8 %collective-permute-start.5 = (bf16[2,2,2,24,768]{4,3,2,0,1:T(8,128)(2,1)S(1)}, bf16[2,2,2,24,768]{4,3,2,0,1:T(8,128)(2,1)S(1)}, u32[]{:S(2)}, u32[]{:S(2)}) collective-permute-start(bf16[2,2,2,24,768]{4,3,2,0,1:T(8,128)(2,1)S(1)} %get-tuple-element.173), channel_id=1, source_target_pairs={{0,2},{1,3},{2,0},{3,1},{4,6},{5,7},{6,4},{7,5},{8,10},{9,11},{10,... | collective-permute-start | bytes 884744 | tf_op jit(solution)/shard_map/ppermute | solution.py:478
  33.5 6.7 %collective-permute-start.4 = (bf16[2,2,2,24,768]{4,3,2,0,1:T(8,128)(2,1)S(1)}, bf16[2,2,2,24,768]{4,3,2,0,1:T(8,128)(2,1)S(1)}, u32[]{:S(2)}, u32[]{:S(2)}) collective-permute-start(bf16[2,2,2,24,768]{4,3,2,0,1:T(8,128)(2,1)S(1)} %get-tuple-element.174), channel_id=1, source_target_pairs={{0,4},{1,5},{2,6},{3,7},{4,0},{5,1},{6,2},{7,3},{8,12},{9,13},{10,... | collective-permute-start | bytes 884744 | tf_op jit(solution)/shard_map/ppermute | solution.py:478
  40.6 16.3 %collective-permute-start.9 = (bf16[2,2,2,2,24,768]{5,4,3,0,1,2:T(8,128)(2,1)S(1)}, bf16[2,2,2,2,24,768]{5,4,3,0,1,2:T(8,128)(2,1)}, u32[]{:S(2)}, u32[]{:S(2)}) collective-permute-start(bf16[2,2,2,2,24,768]{5,4,3,0,1,2:T(8,128)(2,1)S(1)} %get-tuple-element.82), channel_id=1, source_target_pairs={{0,2},{1,3},{2,0},{3,1},{4,6},{5,7},{6,4},{7,5},{8,10},{9,11},{10,... | collective-permute-start | bytes 1769480 | tf_op jit(solution)/shard_map/ppermute | solution.py:478
  42.1 20.9 %collective-permute-start.10 = (bf16[2,2,2,2,24,768]{5,4,3,0,1,2:T(8,128)(2,1)S(1)}, bf16[2,2,2,2,24,768]{5,4,3,0,1,2:T(8,128)(2,1)}, u32[]{:S(2)}, u32[]{:S(2)}) collective-permute-start(bf16[2,2,2,2,24,768]{5,4,3,0,1,2:T(8,128)(2,1)S(1)} %get-tuple-element.83), channel_id=1, source_target_pairs={{0,4},{1,5},{2,6},{3,7},{4,0},{5,1},{6,2},{7,3},{8,12},{9,13},{10,... | collective-permute-start | bytes 1769480 | tf_op jit(solution)/shard_map/ppermute | solution.py:478
  48.3 48.9 %all-to-all-start.1 = ((bf16[32,40,768]{2,1,0:T(8,128)(2,1)}), bf16[32,40,768]{2,1,0:T(8,128)(2,1)S(1)}, u32[]{:S(2)}, u32[]{:S(2)}) async-start(bf16[32,40,768]{2,1,0:T(8,128)(2,1)} %bitcast.299), calls=%async_computation.1 | async-start | bytes 3932160 | tf_op jit(solution)/shard_map/all_to_all | solution.py:473
  64.4 6.4 %collective-permute-start.12 = (bf16[2,2,2,2,2,24,768]{6,5,4,0,1,3,2:T(8,128)(2,1)S(1)}, bf16[2,2,2,2,2,24,768]{6,5,4,0,1,3,2:T(8,128)(2,1)}, u32[]{:S(2)}, u32[]{:S(2)}) collective-permute-start(bf16[2,2,2,2,2,24,768]{6,5,4,0,1,3,2:T(8,128)(2,1)S(1)} %pad_maximum_fusion.6), channel_id=1, source_target_pairs={{0,1},{1,0},{2,3},{3,2},{4,5},{5,4},{6,7},{7,6},{8,9},{9,8},{10,11... | collective-permute-start | bytes 3538952 | tf_op jit(solution)/shard_map/ppermute | solution.py:478
  97.2 29.0 %all-to-all-start = ((bf16[32,40,384]{2,1,0:T(8,128)(2,1)}), bf16[32,40,384]{2,1,0:T(8,128)(2,1)S(1)}, u32[]{:S(2)}, u32[]{:S(2)}) async-start(bf16[32,40,384]{2,1,0:T(8,128)(2,1)} %bitcast.323), calls=%async_computation | async-start | bytes 1966080 | tf_op jit(solution)/shard_map/all_to_all | solution.py:473
  127.2 33.1 %all-to-all-start.3 = ((bf16[32,40,384]{2,1,0:T(8,128)(2,1)}), bf16[32,40,384]{2,1,0:T(8,128)(2,1)S(1)}, u32[]{:S(2)}, u32[]{:S(2)}) async-start(bf16[32,40,384]{2,1,0:T(8,128)(2,1)} %bitcast.322), calls=%async_computation.3 | async-start | bytes 1966080 | tf_op jit(solution)/shard_map/all_to_all | solution.py:473
  161.2 52.4 %all-to-all-start.2 = ((bf16[32,40,768]{2,1,0:T(8,128)(2,1)}), bf16[32,40,768]{2,1,0:T(8,128)(2,1)}, u32[]{:S(2)}, u32[]{:S(2)}) async-start(bf16[32,40,768]{2,1,0:T(8,128)(2,1)} %bitcast.301), calls=%async_computation.2 | async-start | bytes 3932160 | tf_op jit(solution)/shard_map/all_to_all | solution.py:473
  213.6 61.5 %all-to-all-start.4 = ((bf16[32,40,768]{2,1,0:T(8,128)(2,1)}), bf16[32,40,768]{2,1,0:T(8,128)(2,1)}, u32[]{:S(2)}, u32[]{:S(2)}) async-start(bf16[32,40,768]{2,1,0:T(8,128)(2,1)} %bitcast.300), calls=%async_computation.4 | async-start | bytes 3932160 | tf_op jit(solution)/shard_map/all_to_all | solution.py:473
  310.8 15.2 %collective-permute-start.13 = (bf16[4,2,2,2,2,24,768]{6,5,0,1,2,4,3:T(8,128)(2,1)}, bf16[4,2,2,2,2,24,768]{6,5,0,1,2,4,3:T(8,128)(2,1)}, u32[]{:S(2)}, u32[]{:S(2)}) collective-permute-start(bf16[4,2,2,2,2,24,768]{6,5,0,1,2,4,3:T(8,128)(2,1)} %select_bitcast_fusion), channel_id=1, source_target_pairs={{0,1},{1,0},{2,3},{3,2},{4,5},{5,4},{6,7},{7,6},{8,9},{9,8},{10,11... | collective-permute-start | bytes 7077896 | tf_op jit(solution)/shard_map/ppermute | solution.py:478
  320.3 4.2 %collective-permute-start.22 = (bf16[1,2,2,8,128]{4,3,2,1,0:T(8,128)(2,1)S(1)}, bf16[1,2,2,8,128]{4,3,2,1,0:T(8,128)(2,1)S(1)}, u32[]{:S(2)}, u32[]{:S(2)}) collective-permute-start(bf16[1,2,2,8,128]{4,3,2,1,0:T(8,128)(2,1)S(1)} %fusion.35), channel_id=1, source_target_pairs={{0,4},{1,5},{2,6},{3,7},{4,0},{5,1},{6,2},{7,3},{8,12},{9,13},{10,... | collective-permute-start | bytes 24584 | tf_op jit(solution)/shard_map/ppermute | solution.py:478
  324.5 8.4 %collective-permute-start.23 = (bf16[1,2,8,128]{3,2,1,0:T(8,128)(2,1)S(1)}, bf16[1,2,8,128]{3,2,1,0:T(8,128)(2,1)S(1)}, u32[]{:S(2)}, u32[]{:S(2)}) collective-permute-start(bf16[1,2,8,128]{3,2,1,0:T(8,128)(2,1)S(1)} %fusion.39), channel_id=1, source_target_pairs={{0,8},{1,9},{2,10},{3,11},{4,12},{5,13},{6,14},{7,15},{8,0},{9,1},... | collective-permute-start | bytes 12296 | tf_op jit(solution)/shard_map/ppermute | solution.py:478
  328.8 13.9 %collective-permute-start.14 = (bf16[2,2,2,2,24,768]{5,4,0,1,2,3:T(8,128)(2,1)S(1)}, bf16[2,2,2,2,24,768]{5,4,0,1,2,3:T(8,128)(2,1)S(1)}, u32[]{:S(2)}, u32[]{:S(2)}) collective-permute-start(bf16[2,2,2,2,24,768]{5,4,0,1,2,3:T(8,128)(2,1)S(1)} %fusion.10), channel_id=1, source_target_pairs={{0,2},{1,3},{2,0},{3,1},{4,6},{5,7},{6,4},{7,5},{8,10},{9,11},{10,... | collective-permute-start | bytes 1769480 | tf_op jit(solution)/shard_map/ppermute | solution.py:478
  330.3 13.6 %collective-permute-start.16 = (bf16[2,2,2,2,24,768]{5,4,0,1,2,3:T(8,128)(2,1)S(1)}, bf16[2,2,2,2,24,768]{5,4,0,1,2,3:T(8,128)(2,1)S(1)}, u32[]{:S(2)}, u32[]{:S(2)}) collective-permute-start(bf16[2,2,2,2,24,768]{5,4,0,1,2,3:T(8,128)(2,1)S(1)} %fusion.11), channel_id=1, source_target_pairs={{0,4},{1,5},{2,6},{3,7},{4,0},{5,1},{6,2},{7,3},{8,12},{9,13},{10,... | collective-permute-start | bytes 1769480 | tf_op jit(solution)/shard_map/ppermute | solution.py:478
  332.9 12.9 %collective-permute-start.24 = (bf16[1,8,128]{2,1,0:T(8,128)(2,1)S(1)}, bf16[1,8,128]{2,1,0:T(8,128)(2,1)S(1)}, u32[]{:S(2)}, u32[]{:S(2)}) collective-permute-start(bf16[1,8,128]{2,1,0:T(8,128)(2,1)S(1)} %fusion.40), channel_id=1, source_target_pairs={{0,16},{1,17},{2,18},{3,19},{4,20},{5,21},{6,22},{7,23},{8,24},{9,... | collective-permute-start | bytes 6152 | tf_op jit(solution)/shard_map/ppermute | solution.py:478
  344.5 6.8 %collective-permute-start.17 = (bf16[2,2,2,24,768]{4,3,0,1,2:T(8,128)(2,1)S(1)}, bf16[2,2,2,24,768]{4,3,0,1,2:T(8,128)(2,1)S(1)}, u32[]{:S(2)}, u32[]{:S(2)}) collective-permute-start(bf16[2,2,2,24,768]{4,3,0,1,2:T(8,128)(2,1)S(1)} %fusion.18), channel_id=1, source_target_pairs={{0,2},{1,3},{2,0},{3,1},{4,6},{5,7},{6,4},{7,5},{8,10},{9,11},{10,... | collective-permute-start | bytes 884744 | tf_op jit(solution)/shard_map/ppermute | solution.py:478
  345.1 6.8 %collective-permute-start.15 = (bf16[2,2,2,24,768]{4,3,0,1,2:T(8,128)(2,1)S(1)}, bf16[2,2,2,24,768]{4,3,0,1,2:T(8,128)(2,1)S(1)}, u32[]{:S(2)}, u32[]{:S(2)}) collective-permute-start(bf16[2,2,2,24,768]{4,3,0,1,2:T(8,128)(2,1)S(1)} %fusion.17), channel_id=1, source_target_pairs={{0,4},{1,5},{2,6},{3,7},{4,0},{5,1},{6,2},{7,3},{8,12},{9,13},{10,... | collective-permute-start | bytes 884744 | tf_op jit(solution)/shard_map/ppermute | solution.py:478
  352.1 8.0 %collective-permute-start.18 = (bf16[4,2,24,768]{3,2,0,1:T(8,128)(2,1)S(1)}, bf16[4,2,24,768]{3,2,0,1:T(8,128)(2,1)S(1)}, u32[]{:S(2)}, u32[]{:S(2)}) collective-permute-start(bf16[4,2,24,768]{3,2,0,1:T(8,128)(2,1)S(1)} %fusion.19), channel_id=1, source_target_pairs={{0,8},{1,9},{2,10},{3,11},{4,12},{5,13},{6,14},{7,15},{8,0},{9,1},... | collective-permute-start | bytes 884744 | tf_op jit(solution)/shard_map/ppermute | solution.py:478
  360.2 7.2 %collective-permute-start.19 = (bf16[4,24,768]{2,1,0:T(8,128)(2,1)S(1)}, bf16[4,24,768]{2,1,0:T(8,128)(2,1)S(1)}, u32[]{:S(2)}, u32[]{:S(2)}) collective-permute-start(bf16[4,24,768]{2,1,0:T(8,128)(2,1)S(1)} %fusion.20), channel_id=1, source_target_pairs={{0,16},{1,17},{2,18},{3,19},{4,20},{5,21},{6,22},{7,23},{8,24},{9,... | collective-permute-start | bytes 442376 | tf_op jit(solution)/shard_map/ppermute | solution.py:478
  (40 other events, 203.8 us)
where the time goes:
time: 374 us; the launch traced here: 369 us
  Pallas kernels  140 us (37%)
  waiting for transfers between devices  78.6 us (21%)
  starting transfers between devices  52.2 us (14%)
  matrix products  39.8 us (11%)
  local copies, waits for them, and re-layouts  31.2 us (8%)
  other arithmetic  24.1 us (6%)
    ppermute x25, waiting for transfers between devices, swap(): lax.ppermute(value, AXES, [(at, at ^ 1 << bit) for at in range(devices)])  55.7 us
    pallas_call x2, Pallas kernels, expert_call(): pl.pallas_call(expert_kernel, grid_spec=pltpu.PrefetchScalarGridSpec(num_...  45.6 us
    pallas_call x2, Pallas kernels, back_heads_call(): pl.pallas_call(back_heads_kernel, grid=(groups,), in_specs=[whole(length,...  42.7 us
    pallas_call x2, Pallas kernels, front_call(): pl.pallas_call(front_kernel, grid=(groups,), in_specs=[whole(length, widt...  30.9 us
    ppermute x25, starting transfers between devices, swap(): lax.ppermute(value, AXES, [(at, at ^ 1 << bit) for at in range(devices)])  30.9 us
    all_to_all x5, waiting for transfers between devices, exchange(): return lax.all_to_all(buffer, AXES, split_axis=0, concat_axis=0, tiled=True)  23 us
    all_to_all x5, starting transfers between devices, exchange(): return lax.all_to_all(buffer, AXES, split_axis=0, concat_axis=0, tiled=True)  21.4 us
    pallas_call x2, Pallas kernels, back_rows_call(): pl.pallas_call(back_rows_kernel, out_shape=[shape((length, width), bf16),...  18.9 us
  transfers between devices with their start and end apart: 30, of which 20 were waited for; matrix products, arithmetic and copies ran while one was open for 22% of the time, Pallas kernels for 30%

commit v1 on v0

--- a/solution.py
+++ b/solution.py
@@ -1,6 +1,7 @@
 import functools
 import jax
 import jax.numpy as jnp
+import numpy as np
 from jax import lax
 from jax.experimental import pallas as pl
 from jax.experimental.pallas import tpu as pltpu
@@ -264,19 +265,21 @@
     output_ref[...] = (resid + gate * expert_rows).astype(bf16)
     grad_gate = jnp.sum(up * expert_rows, axis=-1, keepdims=True)
     grad_logits = (router * (jnp.where(hot, grad_gate, 0.0) - gate * grad_gate)).astype(bf16)
-    gbias_ref[...] = jnp.sum(grad_logits.astype(f32), axis=0, keepdims=True)
-    grw_ref[...] = mm_tn(normed_two, grad_logits)
     grad_normed = mm_nt(grad_logits, wr_ref[...]) + grad_back
-    ggain_ref[...] = jnp.sum(grad_normed * resid * scale, axis=0, keepdims=True)
+    gbias = jnp.sum(grad_logits.astype(f32), axis=0, keepdims=True)
+    grw = mm_tn(normed_two, grad_logits)
+    ggain = jnp.sum(grad_normed * resid * scale, axis=0, keepdims=True)
     weighted = grad_normed * gain_ref[...]
     slope = scale * scale * scale * jnp.mean(weighted * resid, axis=-1, keepdims=True)
     grad_resid = up + (scale * weighted - resid * slope)
     gradresid_ref[...] = grad_resid
     grad_branch = grad_resid.astype(bf16)
     go = mm_tn(mixed, grad_branch)
+    sums = [go, grw, ggain, gbias]
     if len(refs) > 7:
-        go = go + refs[0][...].astype(f32)
-    go_ref[...] = go.astype(bf16)
+        sums = [one + prior[...].astype(f32) for one, prior in zip(sums, refs)]
+    for ref, one in zip((go_ref, grw_ref, ggain_ref, gbias_ref), sums):
+        ref[...] = one.astype(ref.dtype)
     gradmixed_ref[...] = mm_nt(grad_branch, wo_ref[...]).astype(bf16)
 
 
@@ -298,8 +301,7 @@
         ),
         name="back_rows",
     )(
-        target, route, returned, up, tokens, mixed, gain, wr, rbias, wo,
-        *([] if prior is None else [prior]),
+        target, route, returned, up, tokens, mixed, gain, wr, rbias, wo, *prior
     )
 
 
@@ -307,7 +309,7 @@
     tokens_ref, gain_ref, gradmixed_ref, mixed_ref, wq_ref, wk_ref, wv_ref, q_ref, k_ref, v_ref,
     skew_ref, lse_ref, gradresid_ref, *refs,
 ):
-    prior_ref = refs[0] if len(refs) > 7 else None
+    prior_refs = refs[:-7]
     line_ref, gw_ref, gradacts_ref, ggain_ref, normedt_ref, acc_ref, fold_ref = refs[-7:]
     step = pl.program_id(0)
     last = pl.num_programs(0) - 1
@@ -356,24 +358,27 @@
             while size > 1:
                 size //= 2
                 rows = rows[:size] + pltpu.roll(rows[size:], span - size, 1)
-            line_ref[0, head : head + 1, :] = pltpu.roll(rows, BLOCK - 1, 1)
+            line = pltpu.roll(rows, BLOCK - 1, 1)
+            if prior_refs:
+                line = line + prior_refs[1][0, head : head + 1, :]
+            line_ref[0, head : head + 1, :] = line
             probs = jnp.concatenate(all_probs, axis=0)
             grad_scores = jnp.concatenate(all_grads, axis=0)
             a = mm(grad_scores, clear(key))
-            b = mm_tn(grad_scores, asked)
-            c = mm_tn(probs, own)
+            b = mm(asked.T, grad_scores)
+            c = mm(own.T, probs)
             gq = a if gq is None else gq + a
             gk = b if gk is None else gk + b
             gv = c if gv is None else gv + c
         dq.append(gq.astype(bf16))
-        dk.append(gk.astype(bf16))
-        dv.append(gv.astype(bf16))
+        dk.append(gk.T.astype(bf16))
+        dv.append(gv.T.astype(bf16))
     dq, dk, dv = (jnp.concatenate(x, axis=1) for x in (dq, dk, dv))
     normedt = normedt_ref[...]
     for i, grad in enumerate((dq, dk, dv)):
         total = mm(normedt, grad)
-        if prior_ref is not None:
-            total = total + prior_ref[i].astype(f32)
+        if prior_refs:
+            total = total + prior_refs[0][i].astype(f32)
         gw_ref[i] = total.astype(bf16)
     acc_ref[...] += mm_nt(dq, wq_ref[...]) + mm_nt(dk, wk_ref[...]) + mm_nt(dv, wv_ref[...])
 
@@ -382,7 +387,10 @@
         grad_normed = acc_ref[...]
         acts = tokens_ref[...].astype(f32)
         scale = norm_scale(acts)
-        ggain_ref[...] = jnp.sum(grad_normed * acts * scale, axis=0, keepdims=True)
+        ggain = jnp.sum(grad_normed * acts * scale, axis=0, keepdims=True)
+        if prior_refs:
+            ggain = ggain + prior_refs[2][...]
+        ggain_ref[...] = ggain
         weighted = grad_normed * gain_ref[...]
         slope = scale * scale * scale * jnp.mean(weighted * acts, axis=-1, keepdims=True)
         grad_acts = gradresid_ref[...] + (scale * weighted - acts * slope)
@@ -399,6 +407,7 @@
     columns = lambda size: pl.BlockSpec((size, part), lambda g: (0, g))
     shape = jax.ShapeDtypeStruct
     weights = pl.BlockSpec((3, width, part), lambda g: (0, 0, g))
+    lines = pl.BlockSpec((1, GROUP, 2 * length), lambda g: (g, 0, 0))
     return pl.pallas_call(
         back_heads_kernel,
         grid=(groups,),
@@ -408,10 +417,10 @@
             columns(length), columns(length), columns(length),
             pl.BlockSpec((GROUP, BLOCK, skewed.shape[2]), lambda g: (g, 0, 0)),
             pl.BlockSpec((1, length, GROUP), lambda g: (g, 0, 0)), whole(length, width),
-            *([] if prior is None else [weights]),
+            *([weights, lines, whole(1, width)] if prior else []),
         ],
         out_specs=[
-            pl.BlockSpec((1, GROUP, 2 * length), lambda g: (g, 0, 0)), weights,
+            lines, weights,
             whole(length, width), whole(1, width),
         ],
         out_shape=[
@@ -430,7 +439,7 @@
         name="back_heads",
     )(
         tokens, gain, grad_mixed, mixed, wq, wk, wv, q, k, v, skewed, lse, grad_resid,
-        *([] if prior is None else [prior]),
+        *prior,
     )
 
 
@@ -443,7 +452,7 @@
     return pl.pallas_call(
         pack_kernel,
         out_shape=jax.ShapeDtypeStruct((len(parts), *parts[0].shape), parts[0].dtype),
-        compiler_params=params(8),
+        compiler_params=params(60),
         name="pack",
     )(*parts)
 
@@ -554,6 +563,7 @@
     capacity = max(2, 5 * length // (4 * experts))
     slots = experts * capacity
     span = 2 * length
+    shard = w_query.shape[0]
     far = list(range(wide_bits, bits))
     near = list(range(1, wide_bits))
     turned = near[1:] + near[:1]
@@ -571,8 +581,10 @@
 
     small_parts = [w_router, gain_attn, gain_ffn, rel_bias, router_bias]
     small = pack_rows([part.reshape(1, -1) for part in small_parts], 8 * LANES)
-    square = (pack_call(w_query, w_key, w_value, w_output), [])
-    small = (small.reshape(8, LANES), [])
+    packed, small = lax.optimization_barrier(
+        (pack_call(w_query, w_key, w_value, w_output), small)
+    )
+    square, small = (packed, []), (small.reshape(8, LANES), [])
     for bit in far[::-1]:
         square, small = gather_step(square, bit), gather_step(small, bit)
     value, ahead = lax.optimization_barrier((square[0], small[0]))
@@ -580,7 +592,6 @@
     done = far[::-1]
     value = value.reshape((2,) * len(far) + (4, -1, width))
     low, high = ((lax.slice_in_dim(value, i, i + 2, axis=len(far)), done) for i in (0, 2))
-    raw_inputs = (routes, fill_rank, upstream_grad)
     for number, (one, two) in enumerate(zip(near[::-1], turned[::-1])):
         low, high = gather_step(low, one), gather_step(high, two)
         if number == 0:
@@ -589,17 +600,16 @@
             first, second, ahead = lax.optimization_barrier((low[0], high[0], small[0]))
             low, high = (first, low[1]), (second, high[1])
             small_all = gather_step((ahead, small[1]), 0)[0]
-            small_all, *raw_inputs = lax.optimization_barrier((small_all, *raw_inputs))
-
-    raw_routes, raw_ranks, raw_upstream = raw_inputs
-    spots = [plan(raw_routes[at, :, 0], raw_ranks[at]) for at in range(batches)]
+
+    spots = [plan(routes[at, :, 0], fill_rank[at]) for at in range(batches)]
     raw_spots = jnp.concatenate([spots[at][at] for at in range(batches)], axis=0)
     raw_ids = jnp.arange(2 * slots, dtype=jnp.int32)
     raw_sent = jnp.dot(
         (raw_ids[:, None] == raw_spots[None, :]).astype(bf16),
-        raw_upstream.reshape(batches * length, width),
+        upstream_grad.reshape(batches * length, width),
         preferred_element_type=f32,
     ).astype(bf16)
+    small_all, raw_sent = lax.optimization_barrier((small_all, raw_sent))
     raw_arrived = exchange(raw_sent.reshape(devices, 2 * capacity, width))
 
     wr_all, gain_one, gain_two, rel_flat, bias_all = unpack_rows(
@@ -615,7 +625,14 @@
         == jnp.pad(bucket_map, (0, 1), constant_values=-1)[None, :]
     ).astype(bf16)
     skewed = skew_call(jnp.dot(table, bucket_hot, preferred_element_type=f32), BLOCK)
-    first, second, skewed = lax.optimization_barrier((low[0], high[0], skewed))
+    own = lax.axis_index(AXES).astype(jnp.int32).reshape(1)
+    count = 8 if 8 * capacity % 16 == 0 else 16
+    row = np.arange(count * capacity, dtype=np.int32)
+    row = row + (row // capacity) * capacity
+    place = jnp.asarray(np.stack([row, row + capacity], axis=1))
+    first, second, skewed, wr_all, gain_one, gain_two, bias_all = lax.optimization_barrier(
+        (low[0], high[0], skewed, wr_all, gain_one, gain_two, bias_all)
+    )
     low, high = gather_step((first, low[1]), 0), gather_step((second, high[1]), 0)
     wq, wk, wv, wo = (
         lax.index_in_dim(part[0].reshape(devices, 2, -1, width), i, 1).reshape(width, width)
@@ -623,35 +640,34 @@
         for i in range(2)
     )
 
-    own = lax.axis_index(AXES).astype(jnp.int32).reshape(1)
-    count = 8 if 8 * capacity % 16 == 0 else 16
-    row = jnp.arange(count * capacity, dtype=jnp.int32)
-    place = row + (row // capacity) * capacity
-    place = jnp.stack([place, place + capacity], axis=1)
-
     fronts, arrived, returned = [], [], []
     for at in range(batches):
         acts = tokens[at]
         if at == 1:
-            acts, raw_arrived = lax.optimization_barrier((acts, raw_arrived))
+            raw = raw_arrived.reshape(devices, batches, capacity, width)
+            raw = [raw[:, i].reshape(slots, width) for i in range(batches)]
+            acts, raw, targets = lax.optimization_barrier(
+                (acts, raw, [(spots[i].T, routes[i]) for i in range(batches)])
+            )
         front = front_call(
             acts, wq, wk, wv, wo, skewed, gain_one, gain_two, spots[at], slots
         )
         fronts.append(front)
         arrived.append(exchange(front[-1].reshape(devices, 2 * capacity, width // 2)))
-    raw = raw_arrived.reshape(devices, 2, capacity, width)
     grad_in = grad_out = 0.0
     for at in range(batches):
         sent, rows, active, grad_inner, grad_result = expert_call(
             own,
             arrived[at].reshape(2 * slots, width // 2),
-            raw[:, at].reshape(slots, width),
+            raw[at],
             wr_all,
             bias_all,
             place,
             w_in[0],
             w_out[0],
         )
+        if at == batches - 1:
+            sent, grad_in, grad_out = lax.optimization_barrier((sent, grad_in, grad_out))
         grad_in += jnp.einsum("rd,rf->df", rows, grad_inner, preferred_element_type=f32)
         grad_out += jnp.einsum("rf,rd->fd", active, grad_result, preferred_element_type=f32)
         back = exchange(sent.reshape(devices, 2 * capacity, width))
@@ -659,56 +675,65 @@
         returned.append(back)
 
     row_parts, head_parts = [], []
-    g_output = g_heads = None
+    row_prior, head_prior = [], []
     for at in range(batches):
         q, k, v, mixed, lse, sent = fronts[at]
         row_part = back_rows_call(
-            spots[at].T, routes[at], returned[at].reshape(2 * slots, width), upstream_grad[at],
-            tokens[at], mixed, gain_two, wr_all, bias_all, wo, g_output,
+            *targets[at], returned[at].reshape(2 * slots, width), upstream_grad[at],
+            tokens[at], mixed, gain_two, wr_all, bias_all, wo, row_prior,
         )
-        g_output = row_part[3]
+        row_prior = row_part[3:]
         head_part = back_heads_call(
             tokens[at], gain_one, row_part[2], mixed, wq, wk, wv, q, k, v, skewed, lse,
-            row_part[1], g_heads,
+            row_part[1], head_prior,
         )
-        g_heads = head_part[1]
+        head_prior = [head_part[1], head_part[0], head_part[3]]
         row_parts.append(row_part)
         head_parts.append(head_part)
 
-    parts = jnp.concatenate([g_heads, g_output[None]], axis=0)
-    held = scatter_step((parts.reshape((4,) + (2,) * bits + (-1, width)), list(range(bits))[::-1]), 0)
-    low, high = ((held[0][i : i + 2], held[1]) for i in (0, 2))
+    def halved(value):
+        value = value.reshape((-1,) + (2,) * bits + (shard, width))
+        return scatter_step((value, list(range(bits))[::-1]), 0)
+
+    g_output, g_router, g_gain_two, g_bias = row_prior
+    g_heads, lines, g_gain_one = head_prior
+    outer, inner = halved(g_output[None]), halved(g_heads)
+    low, high = inner[0][:2], jnp.concatenate([inner[0][2:], outer[0]], axis=0)
+    low, high, g_router, g_gain_two, g_bias, lines, g_gain_one = lax.optimization_barrier(
+        (low, high, g_router, g_gain_two, g_bias, lines, g_gain_one)
+    )
+    low, high = (low, inner[1]), (high, inner[1])
+    g_rel = jnp.einsum(
+        "hn,bn->bh",
+        lines.reshape(HEADS, span),
+        bucket_hot.astype(f32),
+        precision=lax.Precision.HIGHEST,
+    )
+    short = [part.reshape(devices, -1) for part in (g_gain_one, g_gain_two, g_rel, g_bias)]
+    sizes = [part.shape[1] for part in short]
+    short_pack = pack_rows(short, 8 * LANES).reshape(devices, -1, LANES).astype(bf16)
+    lanes = -(-experts // LANES) * LANES
+    router_pack = jnp.pad(g_router.astype(bf16), ((0, 0), (0, lanes - experts)))
+    router_pack = router_pack.reshape(devices, -1, LANES)
+    small = jnp.concatenate([router_pack, short_pack], axis=1)
+    small = (small.reshape((1,) + (2,) * bits + small.shape[1:]), list(range(bits))[::-1])
+    small_bits = [0] + near + far
     for one, two in zip(near, turned):
         low, high = scatter_step(low, one), scatter_step(high, two)
     held = (jnp.concatenate([low[0], high[0]], axis=0), low[1])
     for bit in far:
         held = scatter_step(held, bit)
+    for bit in small_bits:
+        small = scatter_step(small, bit)
     r_query, r_key, r_value, r_output = (held[0][i] for i in range(4))
-
-    g_router, g_gain_two, g_bias = (
-        sum(row_part[i] for row_part in row_parts) for i in range(4, 7)
-    )
-    lines, g_gain_one = (sum(part[i] for part in head_parts) for i in (0, 3))
-    g_rel = jnp.einsum(
-        "hn,bn->bh",
-        lines.reshape(HEADS, span),
-        bucket_hot.astype(f32),
-        precision=lax.Precision.HIGHEST,
-    )
-    small_grads = [g_router, g_gain_one, g_gain_two, g_rel, g_bias]
-    small_pack = pack_rows([part.reshape(devices, -1) for part in small_grads], 8 * LANES)
-    held = (
-        small_pack.reshape((1,) + (2,) * bits + (-1, LANES)), list(range(bits))[::-1]
-    )
-    for bit in [0] + near + far:
-        held = scatter_step(held, bit)
-    small_sum = held[0]
-    tail = unpack_rows(small_sum.reshape(1, 1, -1), [part.size // devices for part in small_grads])
-    r_router, r_gain_one, r_gain_two, r_rel, r_bias = (
+    cut = router_pack.shape[1]
+    r_router = small[0][0, :cut].reshape(shard, lanes)[:, :experts]
+    tail = unpack_rows(small[0][:, cut:], sizes)
+    r_gain_one, r_gain_two, r_rel, r_bias = (
         part.reshape(shape)
         for part, shape in zip(
             tail,
-            (w_router.shape, gain_attn.shape, gain_ffn.shape, rel_bias.shape, router_bias.shape),
+            (gain_attn.shape, gain_ffn.shape, rel_bias.shape, router_bias.shape),
         )
     )
     return (

time: 374 us -> 357 us (0.955)
  other arithmetic: 24.1 us -> 12.7 us
    all_to_all x5, waiting for transfers between devices: 23 us -> 14 us  [exchange(): return lax.all_to_all(buffer, AXES, split_axis=0, concat_axis=0, tiled=True)]
    ppermute x25 -> x26, waiting for transfers between devices: 55.7 us -> 62.8 us  [swap(): lax.ppermute(value, AXES, [(at, at ^ 1 << bit) for at in range(devices)])]
    pallas_call x2, Pallas kernels: 42.7 us -> 38.4 us  [back_heads_call(): pl.pallas_call(back_heads_kernel, grid=(groups,), in_specs=[whole(length,...]
    ppermute x25 -> x26, starting transfers between devices: 30.9 us -> 33.7 us  [swap(): lax.ppermute(value, AXES, [(at, at ^ 1 << bit) for at in range(devices)])]
  transfers between devices with their start and end apart: 30 -> 31, of which waited for: 20 -> 22; matrix products, arithmetic and copies ran while one was open for 22% -> 19% of each run, Pallas kernels for 30% -> 30%
where the time goes in v1:
time: 357 us; the launch traced here: 352 us
  Pallas kernels  137 us (38%)
  waiting for transfers between devices  76.7 us (21%)
  starting transfers between devices  54.1 us (15%)
  matrix products  37.9 us (11%)
  local copies, waits for them, and re-layouts  30.7 us (9%)
  other arithmetic  12.7 us (4%)
    ppermute x26, waiting for transfers between devices, swap(): lax.ppermute(value, AXES, [(at, at ^ 1 << bit) for at in range(devices)])  62.8 us
    pallas_call x2, Pallas kernels, expert_call(): pl.pallas_call(expert_kernel, grid_spec=pltpu.PrefetchScalarGridSpec(num_...  45.6 us
    pallas_call x2, Pallas kernels, back_heads_call(): pl.pallas_call(back_heads_kernel, grid=(groups,), in_specs=[whole(length,...  38.4 us
    ppermute x26, starting transfers between devices, swap(): lax.ppermute(value, AXES, [(at, at ^ 1 << bit) for at in range(devices)])  33.7 us
    pallas_call x2, Pallas kernels, front_call(): pl.pallas_call(front_kernel, grid=(groups,), in_specs=[whole(length, widt...  30.9 us
    all_to_all x5, starting transfers between devices, exchange(): return lax.all_to_all(buffer, AXES, split_axis=0, concat_axis=0, tiled=True)  20.4 us
    pallas_call x2, Pallas kernels, back_rows_call(): pl.pallas_call(back_rows_kernel, out_shape=[shape((length, width), bf16),...  19.1 us
    dot_general x2, matrix products, body(): jnp.einsum('rd,rf->df', rows, grad_inner, preferred_element_type=f32)  17.9 us
  transfers between devices with their start and end apart: 31, of which 22 were waited for; matrix products, arithmetic and copies ran while one was open for 19% of the time, Pallas kernels for 30%

profile of v1, /device:TPU:0, one launch (start us, length us, event | category | flops | bytes accessed | tf_op | source)
XLA Modules:
  0.0 351.8 jit_solution(239019937912336030)
XLA Ops:
  4.4 4.1 %collective-permute-start.2 = (bf16[8,128]{1,0:T(8,128)(2,1)S(1)}, bf16[8,128]{1,0:T(8,128)(2,1)S(1)}, u32[]{:S(2)}, u32[]{:S(2)}) collective-permute-start(bf16[8,128]{1,0:T(8,128)(2,1)S(1)} %bitcast.286), channel_id=1, source_target_pairs={{0,16},{1,17},{2,18},{3,19},{4,20},{5,21},{6,22},{7,23},{8,24},{9,... | collective-permute-start | bytes 6152 | tf_op jit(solution)/shard_map/ppermute | solution.py:487
  12.8 5.3 %collective-permute-done = bf16[4,24,768]{2,1,0:T(8,128)(2,1)S(1)} collective-permute-done((bf16[4,24,768]{2,1,0:T(8,128)(2,1)}, bf16[4,24,768]{2,1,0:T(8,128)(2,1)S(1)}, u32[]{:S(2)}, u32[]{:S(2)}) %collective-permute-start) | collective-permute-done | bytes 147488 | tf_op jit(solution)/shard_map/ppermute | solution.py:487
  19.2 7.8 %collective-permute-done.1 = bf16[2,4,24,768]{3,2,1,0:T(8,128)(2,1)S(1)} collective-permute-done((bf16[2,4,24,768]{3,2,1,0:T(8,128)(2,1)S(1)}, bf16[2,4,24,768]{3,2,1,0:T(8,128)(2,1)S(1)}, u32[]{:S(2)}, u32[]{:S(2)}) %collective-permute-start.1) | collective-permute-done | bytes 294944 | tf_op jit(solution)/shard_map/ppermute | solution.py:487
  34.9 4.3 %collective-permute-done.5 = bf16[2,2,2,24,768]{4,3,2,0,1:T(8,128)(2,1)S(1)} collective-permute-done((bf16[2,2,2,24,768]{4,3,2,0,1:T(8,128)(2,1)S(1)}, bf16[2,2,2,24,768]{4,3,2,0,1:T(8,128)(2,1)S(1)}, u32[]{:S(2)}, u32[]{:S(2)}) %collective-permute-start.5) | collective-permute-done | bytes 294944 | tf_op jit(solution)/shard_map/ppermute | solution.py:487
  57.7 10.5 %collective-permute-done.9 = bf16[2,2,2,2,24,768]{5,4,3,0,1,2:T(8,128)(2,1)} collective-permute-done((bf16[2,2,2,2,24,768]{5,4,3,0,1,2:T(8,128)(2,1)S(1)}, bf16[2,2,2,2,24,768]{5,4,3,0,1,2:T(8,128)(2,1)}, u32[]{:S(2)}, u32[]{:S(2)}) %collective-permute-start.9) | collective-permute-done | bytes 589856 | tf_op jit(solution)/shard_map/ppermute | solution.py:487
  82.5 15.5 %front.2 = (bf16[512,768]{1,0:T(8,128)(2,1)}, bf16[512,768]{1,0:T(8,128)(2,1)}, bf16[512,768]{1,0:T(8,128)(2,1)}, bf16[512,768]{1,0:T(8,128)(2,1)}, f32[3,512,4]{2,1,0:T(8,128)}, /*index=5*/bf16[1280,384]{1,0:T(8,128)(2,1)}) custom-call(bf16[512,768]{1,0:T(8,128)(2,1)} %get-tuple-element.252.tokens_ref, bf16[768,768]{1,0:T(8,128)(2,1)} %bitcast.256, ...), custom_call_target="tpu_custom_call" | custom-call | flops 5637144576 | bytes 14680064 | tf_op jit(solution)/shard_map/front/pallas_call | solution.py:113
  98.0 4.6 %all-to-all-start.1 = ((bf16[32,40,384]{2,1,0:T(8,128)(2,1)}), bf16[32,40,384]{2,1,0:T(8,128)(2,1)S(1)}, u32[]{:S(2)}, u32[]{:S(2)}) async-start(bf16[32,40,384]{2,1,0:T(8,128)(2,1)} %bitcast.269), calls=%async_computation.1 | async-start | bytes 1966080 | tf_op jit(solution)/shard_map/all_to_all | solution.py:482
  108.2 15.5 %front.3 = (bf16[512,768]{1,0:T(8,128)(2,1)}, bf16[512,768]{1,0:T(8,128)(2,1)}, bf16[512,768]{1,0:T(8,128)(2,1)}, bf16[512,768]{1,0:T(8,128)(2,1)}, f32[3,512,4]{2,1,0:T(8,128)}, /*index=5*/bf16[1280,384]{1,0:T(8,128)(2,1)}) custom-call(bf16[512,768]{1,0:T(8,128)(2,1)} %get-tuple-element.126.tokens_ref, bf16[768,768]{1,0:T(8,128)(2,1)} %bitcast.257, ...), custom_call_target="tpu_custom_call" | custom-call | flops 5637144576 | bytes 14680064 | tf_op jit(solution)/shard_map/front/pallas_call | solution.py:113
  127.4 3.8 %all-to-all-start.3 = ((bf16[32,40,384]{2,1,0:T(8,128)(2,1)}), bf16[32,40,384]{2,1,0:T(8,128)(2,1)S(1)}, u32[]{:S(2)}, u32[]{:S(2)}) async-start(bf16[32,40,384]{2,1,0:T(8,128)(2,1)} %bitcast.271), calls=%async_computation.3 | async-start | bytes 1966080 | tf_op jit(solution)/shard_map/all_to_all | solution.py:482
  131.3 22.8 %expert.2 = (bf16[1280,768]{1,0:T(8,128)(2,1)}, bf16[640,768]{1,0:T(8,128)(2,1)}, bf16[640,3072]{1,0:T(8,128)(2,1)}, bf16[640,3072]{1,0:T(8,128)(2,1)}, bf16[640,768]{1,0:T(8,128)(2,1)}) custom-call(s32[1]{0:T(128)} %bitcast.39.own_ref, bf16[1280,384]{1,0:T(8,128)(2,1)} %bitcast.268, bf16[640,768]{1,0:T(8,128)(2,1)} %reshape_squeeze.6.raw_ref, ...), custom_call_target="tpu_custom_call" | custom-call | flops 12079595520 | bytes 20971520 | tf_op jit(solution)/shard_map/expert/pallas_call | solution.py:214
  157.0 4.4 %all-to-all-start.2 = ((bf16[32,40,768]{2,1,0:T(8,128)(2,1)}), bf16[32,40,768]{2,1,0:T(8,128)(2,1)S(1)}, u32[]{:S(2)}, u32[]{:S(2)}) async-start(bf16[32,40,768]{2,1,0:T(8,128)(2,1)} %bitcast.249), calls=%async_computation.2 | async-start | bytes 3932160 | tf_op jit(solution)/shard_map/all_to_all | solution.py:482
  161.5 8.6 %fusion.45 = f32[768,3072]{1,0:T(8,128)} fusion(bf16[640,768]{1,0:T(8,128)(2,1)S(1)} %copy-done.12, bf16[640,3072]{1,0:T(8,128)(2,1)} %get-tuple-element.118), kind=kOutput, calls=%fused_computation.166 | convolution fusion | flops 3019898880 | bytes 14352384 | tf_op jit(solution)/shard_map/rd,rf->df/dot_general | solution.py:671
  170.1 6.4 %fusion.46 = f32[3072,768]{1,0:T(8,128)} fusion(bf16[640,3072]{1,0:T(8,128)(2,1)S(1)} %copy-done.26, bf16[640,768]{1,0:T(8,128)(2,1)S(1)} %copy-done.27), kind=kOutput, calls=%fused_computation.167 | convolution fusion | flops 3019898880 | bytes 14352384 | tf_op jit(solution)/shard_map/rf,rd->fd/dot_general | solution.py:672
  176.5 22.8 %expert.3 = (bf16[1280,768]{1,0:T(8,128)(2,1)}, bf16[640,768]{1,0:T(8,128)(2,1)}, bf16[640,3072]{1,0:T(8,128)(2,1)}, bf16[640,3072]{1,0:T(8,128)(2,1)}, bf16[640,768]{1,0:T(8,128)(2,1)}) custom-call(s32[1]{0:T(128)} %bitcast.39.own_ref, bf16[1280,384]{1,0:T(8,128)(2,1)} %bitcast.270, bf16[640,768]{1,0:T(8,128)(2,1)} %reshape_squeeze.7.raw_ref, ...), custom_call_target="tpu_custom_call" | custom-call | flops 12079595520 | bytes 20971520 | tf_op jit(solution)/shard_map/expert/pallas_call | solution.py:214
  199.3 8.2 %all-to-all-done.2 = bf16[32,40,768]{2,1,0:T(8,128)(2,1)S(1)} async-done(((bf16[32,40,768]{2,1,0:T(8,128)(2,1)}), bf16[32,40,768]{2,1,0:T(8,128)(2,1)S(1)}, u32[]{:S(2)}, u32[]{:S(2)}) %all-to-all-start.2) | async-done | bytes 1966112 | tf_op jit(solution)/shard_map/all_to_all | solution.py:482
  208.8 4.3 %all-to-all-start.4 = ((bf16[32,40,768]{2,1,0:T(8,128)(2,1)}), bf16[32,40,768]{2,1,0:T(8,128)(2,1)}, u32[]{:S(2)}, u32[]{:S(2)}) async-start(bf16[32,40,768]{2,1,0:T(8,128)(2,1)} %bitcast.247), calls=%async_computation.4 | async-start | bytes 3932160 | tf_op jit(solution)/shard_map/all_to_all | solution.py:482
  214.8 9.2 %back_rows.2 = (bf16[512,768]{1,0:T(8,128)(2,1)}, f32[512,768]{1,0:T(8,128)}, bf16[512,768]{1,0:T(8,128)(2,1)}, bf16[768,768]{1,0:T(8,128)(2,1)}, f32[768,32]{1,...) custom-call(s32[512,2]{1,0:T(8,128)} %bitcast.282, s32[512,1]{1,0:T(8,128)} %copy.140.route_ref, ...), custom_call_target="tpu_custom_call" | custom-call | flops 3825205248 | bytes 12582912 | tf_op jit(solution)/shard_map/back_rows/pallas_call | solution.py:290
  224.0 18.9 %back_heads.2 = (f32[3,4,1024]{2,1,0:T(4,128)}, bf16[3,768,768]{2,1,0:T(8,128)(2,1)}, bf16[512,768]{1,0:T(8,128)(2,1)}, f32[1,768]{1,0:T(1,128)}) custom-call(bf16[512,768]{1,0:T(8,128)(2,1)} %get-tuple-element.252.tokens_ref, f32[1,768]{1,0:T(1,128)} %reshape.666.gain_one_ref.gain_ref, bf16[512,768]{1,0:T(8,128)(2,1)} %get-tuple-element.146.gradmixed_ref, ...), custom_call_target="tpu_custom_call" | custom-call | flops 10066329600 | bytes 22020096 | tf_op jit(solution)/shard_map/back_heads/pallas_call | solution.py:411
  243.0 9.3 %convolution_add_fusion.1 = f32[768,3072]{1,0:T(8,128)} fusion(f32[768,3072]{1,0:T(8,128)} %fusion.45, bf16[640,768]{1,0:T(8,128)(2,1)} %get-tuple-element.134, bf16[640,3072]{1,0:T(8,128)(2,1)S(1)} %copy-done.3), kind=kOutput, calls=%fused_computation.3 | convolution fusion | flops 3022258176 | bytes 23789568 | tf_op jit(solution)/shard_map/rd,rf->df/dot_general | solution.py:671
  252.3 8.7 %convolution_add_fusion = f32[3072,768]{1,0:T(8,128)} fusion(f32[3072,768]{1,0:T(8,128)} %fusion.46, bf16[640,3072]{1,0:T(8,128)(2,1)S(1)} %copy-done.2, bf16[640,768]{1,0:T(8,128)(2,1)S(1)} %copy-done.9), kind=kOutput, calls=%fused_computation.2 | convolution fusion | flops 3022258176 | bytes 23789568 | tf_op jit(solution)/shard_map/rf,rd->fd/dot_general | solution.py:672
  261.0 9.9 %back_rows.3 = (bf16[512,768]{1,0:T(8,128)(2,1)}, f32[512,768]{1,0:T(8,128)}, bf16[512,768]{1,0:T(8,128)(2,1)}, bf16[768,768]{1,0:T(8,128)(2,1)}, f32[768,32]{1,...) custom-call(s32[512,2]{1,0:T(8,128)} %bitcast.281, s32[512,1]{1,0:T(8,128)} %copy.141.route_ref, ...), custom_call_target="tpu_custom_call" | custom-call | flops 3825205248 | bytes 12582912 | tf_op jit(solution)/shard_map/back_rows/pallas_call | solution.py:290
  270.9 19.5 %back_heads.3 = (f32[3,4,1024]{2,1,0:T(4,128)}, bf16[3,768,768]{2,1,0:T(8,128)(2,1)}, bf16[512,768]{1,0:T(8,128)(2,1)}, f32[1,768]{1,0:T(1,128)}) custom-call(bf16[512,768]{1,0:T(8,128)(2,1)} %get-tuple-element.126.tokens_ref, f32[1,768]{1,0:T(1,128)} %reshape.666.gain_one_ref.gain_ref, bf16[512,768]{1,0:T(8,128)(2,1)} %get-tuple-element.153.gradmixed_ref, ...), custom_call_target="tpu_custom_call" | custom-call | flops 10066329600 | bytes 22020096 | tf_op jit(solution)/shard_map/back_heads/pallas_call | solution.py:411
  319.0 5.4 %collective-permute-done.17 = bf16[2,2,2,2,24,768]{5,4,0,1,2,3:T(8,128)(2,1)S(1)} collective-permute-done((bf16[2,2,2,2,24,768]{5,4,0,1,2,3:T(8,128)(2,1)S(1)}, bf16[2,2,2,2,24,768]{5,4,0,1,2,3:T(8,128)(2,1)S(1)}, u32[]{:S(2)}, u32[]{:S(2)}) %collective-permute-start.17) | collective-permute-done | bytes 589856 | tf_op jit(solution)/shard_map/ppermute | solution.py:487
  337.6 5.6 %collective-permute-done.19 = bf16[4,2,24,768]{3,2,0,1:T(8,128)(2,1)S(1)} collective-permute-done((bf16[4,2,24,768]{3,2,0,1:T(8,128)(2,1)S(1)}, bf16[4,2,24,768]{3,2,0,1:T(8,128)(2,1)S(1)}, u32[]{:S(2)}, u32[]{:S(2)}) %collective-permute-start.19) | collective-permute-done | bytes 294944 | tf_op jit(solution)/shard_map/ppermute | solution.py:487
  (226 shorter events, 113.9 us)
Async XLA Ops:
  4.4 6.5 %collective-permute-start.2 = (bf16[8,128]{1,0:T(8,128)(2,1)S(1)}, bf16[8,128]{1,0:T(8,128)(2,1)S(1)}, u32[]{:S(2)}, u32[]{:S(2)}) collective-permute-start(bf16[8,128]{1,0:T(8,128)(2,1)S(1)} %bitcast.286), channel_id=1, source_target_pairs={{0,16},{1,17},{2,18},{3,19},{4,20},{5,21},{6,22},{7,23},{8,24},{9,... | collective-permute-start | bytes 6152 | tf_op jit(solution)/shard_map/ppermute | solution.py:487
  8.5 9.6 %collective-permute-start = (bf16[4,24,768]{2,1,0:T(8,128)(2,1)}, bf16[4,24,768]{2,1,0:T(8,128)(2,1)S(1)}, u32[]{:S(2)}, u32[]{:S(2)}) collective-permute-start(bf16[4,24,768]{2,1,0:T(8,128)(2,1)} %pack.1), channel_id=1, source_target_pairs={{0,16},{1,17},{2,18},{3,19},{4,20},{5,21},{6,22},{7,23},{8,24},{9,... | collective-permute-start | bytes 442376 | tf_op jit(solution)/shard_map/ppermute | solution.py:487
  10.9 8.2 %collective-permute-start.3 = (bf16[2,8,128]{2,1,0:T(8,128)(2,1)S(1)}, bf16[2,8,128]{2,1,0:T(8,128)(2,1)S(1)}, u32[]{:S(2)}, u32[]{:S(2)}) collective-permute-start(bf16[2,8,128]{2,1,0:T(8,128)(2,1)S(1)} %pad_maximum_fusion.17), channel_id=1, source_target_pairs={{0,8},{1,9},{2,10},{3,11},{4,12},{5,13},{6,14},{7,15},{8,0},{9,1},... | collective-permute-start | bytes 12296 | tf_op jit(solution)/shard_map/ppermute | solution.py:487
  19.0 7.9 %collective-permute-start.1 = (bf16[2,4,24,768]{3,2,1,0:T(8,128)(2,1)S(1)}, bf16[2,4,24,768]{3,2,1,0:T(8,128)(2,1)S(1)}, u32[]{:S(2)}, u32[]{:S(2)}) collective-permute-start(bf16[2,4,24,768]{3,2,1,0:T(8,128)(2,1)S(1)} %pad_maximum_fusion.11), channel_id=1, source_target_pairs={{0,8},{1,9},{2,10},{3,11},{4,12},{5,13},{6,14},{7,15},{8,0},{9,1},... | collective-permute-start | bytes 884744 | tf_op jit(solution)/shard_map/ppermute | solution.py:487
  32.4 6.8 %collective-permute-start.5 = (bf16[2,2,2,24,768]{4,3,2,0,1:T(8,128)(2,1)S(1)}, bf16[2,2,2,24,768]{4,3,2,0,1:T(8,128)(2,1)S(1)}, u32[]{:S(2)}, u32[]{:S(2)}) collective-permute-start(bf16[2,2,2,24,768]{4,3,2,0,1:T(8,128)(2,1)S(1)} %get-tuple-element.211), channel_id=1, source_target_pairs={{0,2},{1,3},{2,0},{3,1},{4,6},{5,7},{6,4},{7,5},{8,10},{9,11},{10,... | collective-permute-start | bytes 884744 | tf_op jit(solution)/shard_map/ppermute | solution.py:487
  33.0 6.7 %collective-permute-start.4 = (bf16[2,2,2,24,768]{4,3,2,0,1:T(8,128)(2,1)S(1)}, bf16[2,2,2,24,768]{4,3,2,0,1:T(8,128)(2,1)S(1)}, u32[]{:S(2)}, u32[]{:S(2)}) collective-permute-start(bf16[2,2,2,24,768]{4,3,2,0,1:T(8,128)(2,1)S(1)} %get-tuple-element.212), channel_id=1, source_target_pairs={{0,4},{1,5},{2,6},{3,7},{4,0},{5,1},{6,2},{7,3},{8,12},{9,13},{10,... | collective-permute-start | bytes 884744 | tf_op jit(solution)/shard_map/ppermute | solution.py:487
  39.9 8.0 %collective-permute-start.8 = (bf16[2,2,2,2,8,128]{5,4,0,1,2,3:T(8,128)(2,1)S(1)}, bf16[2,2,2,2,8,128]{5,4,0,1,2,3:T(8,128)(2,1)S(1)}, u32[]{:S(2)}, u32[]{:S(2)}) collective-permute-start(bf16[2,2,2,2,8,128]{5,4,0,1,2,3:T(8,128)(2,1)S(1)} %pad_maximum_fusion.14), channel_id=1, source_target_pairs={{0,1},{1,0},{2,3},{3,2},{4,5},{5,4},{6,7},{7,6},{8,9},{9,8},{10,11... | collective-permute-start | bytes 98312 | tf_op jit(solution)/shard_map/ppermute | solution.py:487
  44.9 23.3 %collective-permute-start.9 = (bf16[2,2,2,2,24,768]{5,4,3,0,1,2:T(8,128)(2,1)S(1)}, bf16[2,2,2,2,24,768]{5,4,3,0,1,2:T(8,128)(2,1)}, u32[]{:S(2)}, u32[]{:S(2)}) collective-permute-start(bf16[2,2,2,2,24,768]{5,4,3,0,1,2:T(8,128)(2,1)S(1)} %get-tuple-element.104), channel_id=1, source_target_pairs={{0,2},{1,3},{2,0},{3,1},{4,6},{5,7},{6,4},{7,5},{8,10},{9,11},{10,... | collective-permute-start | bytes 1769480 | tf_op jit(solution)/shard_map/ppermute | solution.py:487
  46.4 26.2 %collective-permute-start.10 = (bf16[2,2,2,2,24,768]{5,4,3,0,1,2:T(8,128)(2,1)S(1)}, bf16[2,2,2,2,24,768]{5,4,3,0,1,2:T(8,128)(2,1)}, u32[]{:S(2)}, u32[]{:S(2)}) collective-permute-start(bf16[2,2,2,2,24,768]{5,4,3,0,1,2:T(8,128)(2,1)S(1)} %get-tuple-element.105), channel_id=1, source_target_pairs={{0,4},{1,5},{2,6},{3,7},{4,0},{5,1},{6,2},{7,3},{8,12},{9,13},{10,... | collective-permute-start | bytes 1769480 | tf_op jit(solution)/shard_map/ppermute | solution.py:487
  48.0 50.0 %all-to-all-start = ((bf16[32,40,768]{2,1,0:T(8,128)(2,1)}), bf16[32,40,768]{2,1,0:T(8,128)(2,1)S(1)}, u32[]{:S(2)}, u32[]{:S(2)}) async-start(bf16[32,40,768]{2,1,0:T(8,128)(2,1)} %bitcast.246), calls=%async_computation | async-start | bytes 3932160 | tf_op jit(solution)/shard_map/all_to_all | solution.py:482
  74.2 4.5 %collective-permute-start.12 = (bf16[2,2,2,2,2,24,768]{6,5,4,0,1,3,2:T(8,128)(2,1)S(1)}, bf16[2,2,2,2,2,24,768]{6,5,4,0,1,3,2:T(8,128)(2,1)S(1)}, u32[]{:S(2)}, u32[]{:S(2)}) collective-permute-start(bf16[2,2,2,2,2,24,768]{6,5,4,0,1,3,2:T(8,128)(2,1)S(1)} %pad_maximum_fusion.6), channel_id=1, source_target_pairs={{0,1},{1,0},{2,3},{3,2},{4,5},{5,4},{6,7},{7,6},{8,9},{9,8},{10,11... | collective-permute-start | bytes 3538952 | tf_op jit(solution)/shard_map/ppermute | solution.py:487
  98.0 29.4 %all-to-all-start.1 = ((bf16[32,40,384]{2,1,0:T(8,128)(2,1)}), bf16[32,40,384]{2,1,0:T(8,128)(2,1)S(1)}, u32[]{:S(2)}, u32[]{:S(2)}) async-start(bf16[32,40,384]{2,1,0:T(8,128)(2,1)} %bitcast.269), calls=%async_computation.1 | async-start | bytes 1966080 | tf_op jit(solution)/shard_map/all_to_all | solution.py:482
  127.4 28.7 %all-to-all-start.3 = ((bf16[32,40,384]{2,1,0:T(8,128)(2,1)}), bf16[32,40,384]{2,1,0:T(8,128)(2,1)S(1)}, u32[]{:S(2)}, u32[]{:S(2)}) async-start(bf16[32,40,384]{2,1,0:T(8,128)(2,1)} %bitcast.271), calls=%async_computation.3 | async-start | bytes 1966080 | tf_op jit(solution)/shard_map/all_to_all | solution.py:482
  157.0 50.5 %all-to-all-start.2 = ((bf16[32,40,768]{2,1,0:T(8,128)(2,1)}), bf16[32,40,768]{2,1,0:T(8,128)(2,1)S(1)}, u32[]{:S(2)}, u32[]{:S(2)}) async-start(bf16[32,40,768]{2,1,0:T(8,128)(2,1)} %bitcast.249), calls=%async_computation.2 | async-start | bytes 3932160 | tf_op jit(solution)/shard_map/all_to_all | solution.py:482
  208.8 52.2 %all-to-all-start.4 = ((bf16[32,40,768]{2,1,0:T(8,128)(2,1)}), bf16[32,40,768]{2,1,0:T(8,128)(2,1)}, u32[]{:S(2)}, u32[]{:S(2)}) async-start(bf16[32,40,768]{2,1,0:T(8,128)(2,1)} %bitcast.247), calls=%async_computation.4 | async-start | bytes 3932160 | tf_op jit(solution)/shard_map/all_to_all | solution.py:482
  293.0 4.8 %collective-permute-start.13 = (bf16[3,2,2,2,2,24,768]{6,5,0,1,2,4,3:T(8,128)(2,1)S(1)}, bf16[3,2,2,2,2,24,768]{6,5,0,1,2,4,3:T(8,128)(2,1)S(1)}, u32[]{:S(2)}, u32[]{:S(2)}) collective-permute-start(bf16[3,2,2,2,2,24,768]{6,5,0,1,2,4,3:T(8,128)(2,1)S(1)} %select_bitcast_fusion), channel_id=1, source_target_pairs={{0,1},{1,0},{2,3},{3,2},{4,5},{5,4},{6,7},{7,6},{8,9},{9,8},{10,11... | collective-permute-start | bytes 5308424 | tf_op jit(solution)/shard_map/ppermute | solution.py:487
  303.6 4.4 %collective-permute-start.22 = (bf16[1,2,2,2,32,128]{5,4,1,2,3,0:T(8,128)(2,1)S(1)}, bf16[1,2,2,2,32,128]{5,4,1,2,3,0:T(8,128)(2,1)S(1)}, u32[]{:S(2)}, u32[]{:S(2)}) collective-permute-start(bf16[1,2,2,2,32,128]{5,4,1,2,3,0:T(8,128)(2,1)S(1)} %fusion.25), channel_id=1, source_target_pairs={{0,2},{1,3},{2,0},{3,1},{4,6},{5,7},{6,4},{7,5},{8,10},{9,11},{10,... | collective-permute-start | bytes 196616 | tf_op jit(solution)/shard_map/ppermute | solution.py:487
  310.1 14.4 %collective-permute-start.17 = (bf16[2,2,2,2,24,768]{5,4,0,1,2,3:T(8,128)(2,1)S(1)}, bf16[2,2,2,2,24,768]{5,4,0,1,2,3:T(8,128)(2,1)S(1)}, u32[]{:S(2)}, u32[]{:S(2)}) collective-permute-start(bf16[2,2,2,2,24,768]{5,4,0,1,2,3:T(8,128)(2,1)S(1)} %fusion.8), channel_id=1, source_target_pairs={{0,4},{1,5},{2,6},{3,7},{4,0},{5,1},{6,2},{7,3},{8,12},{9,13},{10,... | collective-permute-start | bytes 1769480 | tf_op jit(solution)/shard_map/ppermute | solution.py:487
  314.4 13.9 %collective-permute-start.15 = (bf16[2,2,2,2,24,768]{5,4,0,1,2,3:T(8,128)(2,1)S(1)}, bf16[2,2,2,2,24,768]{5,4,0,1,2,3:T(8,128)(2,1)S(1)}, u32[]{:S(2)}, u32[]{:S(2)}) collective-permute-start(bf16[2,2,2,2,24,768]{5,4,0,1,2,3:T(8,128)(2,1)S(1)} %fusion.9), channel_id=1, source_target_pairs={{0,2},{1,3},{2,0},{3,1},{4,6},{5,7},{6,4},{7,5},{8,10},{9,11},{10,... | collective-permute-start | bytes 1769480 | tf_op jit(solution)/shard_map/ppermute | solution.py:487
  316.3 14.2 %collective-permute-start.25 = (bf16[1,32,128]{2,1,0:T(8,128)(2,1)S(1)}, bf16[1,32,128]{2,1,0:T(8,128)(2,1)S(1)}, u32[]{:S(2)}, u32[]{:S(2)}) collective-permute-start(bf16[1,32,128]{2,1,0:T(8,128)(2,1)S(1)} %fusion.36), channel_id=1, source_target_pairs={{0,16},{1,17},{2,18},{3,19},{4,20},{5,21},{6,22},{7,23},{8,24},{9,... | collective-permute-start | bytes 24584 | tf_op jit(solution)/shard_map/ppermute | solution.py:487
  324.7 8.6 %collective-permute-start.18 = (bf16[2,2,2,24,768]{4,3,0,1,2:T(8,128)(2,1)S(1)}, bf16[2,2,2,24,768]{4,3,0,1,2:T(8,128)(2,1)S(1)}, u32[]{:S(2)}, u32[]{:S(2)}) collective-permute-start(bf16[2,2,2,24,768]{4,3,0,1,2:T(8,128)(2,1)S(1)} %fusion.16), channel_id=1, source_target_pairs={{0,2},{1,3},{2,0},{3,1},{4,6},{5,7},{6,4},{7,5},{8,10},{9,11},{10,... | collective-permute-start | bytes 884744 | tf_op jit(solution)/shard_map/ppermute | solution.py:487
  328.6 6.8 %collective-permute-start.16 = (bf16[2,2,2,24,768]{4,3,0,1,2:T(8,128)(2,1)S(1)}, bf16[2,2,2,24,768]{4,3,0,1,2:T(8,128)(2,1)S(1)}, u32[]{:S(2)}, u32[]{:S(2)}) collective-permute-start(bf16[2,2,2,24,768]{4,3,0,1,2:T(8,128)(2,1)S(1)} %fusion.15), channel_id=1, source_target_pairs={{0,4},{1,5},{2,6},{3,7},{4,0},{5,1},{6,2},{7,3},{8,12},{9,13},{10,... | collective-permute-start | bytes 884744 | tf_op jit(solution)/shard_map/ppermute | solution.py:487
  335.6 7.5 %collective-permute-start.19 = (bf16[4,2,24,768]{3,2,0,1:T(8,128)(2,1)S(1)}, bf16[4,2,24,768]{3,2,0,1:T(8,128)(2,1)S(1)}, u32[]{:S(2)}, u32[]{:S(2)}) collective-permute-start(bf16[4,2,24,768]{3,2,0,1:T(8,128)(2,1)S(1)} %fusion.17), channel_id=1, source_target_pairs={{0,8},{1,9},{2,10},{3,11},{4,12},{5,13},{6,14},{7,15},{8,0},{9,1},... | collective-permute-start | bytes 884744 | tf_op jit(solution)/shard_map/ppermute | solution.py:487
  343.2 7.6 %collective-permute-start.20 = (bf16[4,24,768]{2,1,0:T(8,128)(2,1)S(1)}, bf16[4,24,768]{2,1,0:T(8,128)(2,1)S(1)}, u32[]{:S(2)}, u32[]{:S(2)}) collective-permute-start(bf16[4,24,768]{2,1,0:T(8,128)(2,1)S(1)} %fusion.18), channel_id=1, source_target_pairs={{0,16},{1,17},{2,18},{3,19},{4,20},{5,21},{6,22},{7,23},{8,24},{9,... | collective-permute-start | bytes 442376 | tf_op jit(solution)/shard_map/ppermute | solution.py:487
  (35 other events, 158.3 us)

commit v2 on v1

--- a/solution.py
+++ b/solution.py
@@ -103,8 +103,12 @@
         sent_ref[...] = (left + right).astype(bf16)
 
 
-def front_call(tokens, wq, wk, wv, wo, skewed, gain_one, gain_two, spots, slots):
-    length, width = tokens.shape
+def one_in(at, length, width):
+    return pl.BlockSpec((None, length, width), lambda *g: (at, 0, 0))
+
+
+def front_call(at, tokens, wq, wk, wv, wo, skewed, gain_one, gain_two, spots, slots):
+    length, width = tokens.shape[1:]
     part = GROUP * HEAD
     groups = HEADS // GROUP
     whole = lambda *shape: pl.BlockSpec(shape, lambda g: (0,) * len(shape))
@@ -114,7 +118,7 @@
         front_kernel,
         grid=(groups,),
         in_specs=[
-            whole(length, width), columns(width), columns(width), columns(width),
+            one_in(at, length, width), columns(width), columns(width), columns(width),
             pl.BlockSpec((part, width), lambda g: (g, 0)),
             pl.BlockSpec((GROUP, BLOCK, skewed.shape[2]), lambda g: (g, 0, 0)),
             whole(1, width), whole(1, width), whole(2, length),
@@ -130,10 +134,7 @@
         ],
         scratch_shapes=[pltpu.VMEM((length, width), bf16), pltpu.VMEM((length, width), f32)],
         compiler_params=params(60),
-        cost_estimate=pl.CostEstimate(
-            flops=2 * length * width * width * 4 + 4 * length * length * width * 4,
-            bytes_accessed=14 * MIB, transcendentals=HEADS * length * length,
-        ),
+        cost_estimate=pl.CostEstimate(flops=1000000, bytes_accessed=MIB // 4, transcendentals=0),
         name="front",
     )(tokens, wq, wk, wv, wo, skewed, gain_one, gain_two, spots)
 
@@ -151,7 +152,7 @@
 
 
 def expert_kernel(
-    own_ref, arrived_ref, raw_ref, wr_ref, rbias_ref, place_ref, placed_ref, win_ref, wout_ref,
+    mine_at, own_ref, arrived_ref, raw_ref, wr_ref, rbias_ref, place_ref, placed_ref, win_ref, wout_ref,
     sent_ref, rows_ref, active_ref, gradinner_ref, gradresult_ref, result_acc, rows_acc,
 ):
     step = pl.program_id(0)
@@ -172,7 +173,10 @@
         probs = softmax_rows(mm(rows_ref[...], wr_ref[...]) + rbias_ref[...])
         mine = lax.broadcasted_iota(jnp.int32, probs.shape, 1) == own_ref[0]
         gate = jnp.sum(jnp.where(mine, probs, 0.0), axis=-1, keepdims=True)
-        gradresult_ref[...] = (gate * raw_ref[...].astype(f32)).astype(bf16)
+        pick = (ids == place_ref[:, mine_at : mine_at + 1]).astype(bf16)
+        for at in range(0, count, unit):
+            raw = mm(pick, raw_ref[2 * at : 2 * (at + unit), :])
+            gradresult_ref[at : at + unit, :] = (gate[at : at + unit] * raw).astype(bf16)
 
     inner = mm(rows_ref[...], win_ref[...])
     grad_active = mm_nt(gradresult_ref[...], wout_ref[...])
@@ -205,19 +209,19 @@
             ).astype(bf16)
 
 
-def expert_call(own, arrived, raw, wr, rbias, place, w_in, w_out, part=1024):
-    count, width = raw.shape
+def expert_call(mine_at, own, arrived, raw, wr, rbias, place, w_in, w_out, part=1024):
+    count, width = raw.shape[0] // 2, raw.shape[1]
     hidden = w_in.shape[1]
     experts = wr.shape[1]
     whole = lambda *shape: pl.BlockSpec(shape, lambda g, own: (0,) * len(shape))
     columns = lambda n: pl.BlockSpec((n, part), lambda g, own: (0, g))
     return pl.pallas_call(
-        expert_kernel,
+        functools.partial(expert_kernel, mine_at),
         grid_spec=pltpu.PrefetchScalarGridSpec(
             num_scalar_prefetch=1,
             grid=(hidden // part,),
             in_specs=[
-                whole(2 * count, width // 2), whole(count, width), whole(width, experts),
+                whole(2 * count, width // 2), whole(2 * count, width), whole(width, experts),
                 whole(1, experts), whole(*place.shape), whole(*place.shape[::-1]),
                 columns(width), pl.BlockSpec((part, width), lambda g, own: (g, 0)),
             ],
@@ -262,7 +266,7 @@
     up = up_ref[...].astype(f32)
     hot = lax.broadcasted_iota(jnp.int32, (length, experts), 1) == route_ref[...]
     gate = jnp.sum(jnp.where(hot, router, 0.0), axis=-1, keepdims=True)
-    output_ref[...] = (resid + gate * expert_rows).astype(bf16)
+    output_ref[0] = (resid + gate * expert_rows).astype(bf16)
     grad_gate = jnp.sum(up * expert_rows, axis=-1, keepdims=True)
     grad_logits = (router * (jnp.where(hot, grad_gate, 0.0) - gate * grad_gate)).astype(bf16)
     grad_normed = mm_nt(grad_logits, wr_ref[...]) + grad_back
@@ -283,14 +287,31 @@
     gradmixed_ref[...] = mm_nt(grad_branch, wo_ref[...]).astype(bf16)
 
 
-def back_rows_call(target, route, returned, up, tokens, mixed, gain, wr, rbias, wo, prior):
-    length, width = up.shape
+def one_of(count, at, length, width):
+    spec = pl.BlockSpec((1, length, width), lambda *g: (at, 0, 0))
+    return spec, jax.ShapeDtypeStruct((count, length, width), bf16)
+
+
+def back_rows_call(
+    at, count, target, route, returned, up, tokens, mixed, gain, wr, rbias, wo, prior, output
+):
+    length, width = up.shape[1:]
     experts = wr.shape[1]
     shape = jax.ShapeDtypeStruct
+    spec, full = one_of(count, at, length, width)
+    vmem = pl.BlockSpec(memory_space=pltpu.VMEM)
+    inputs = 10 + len(prior)
     return pl.pallas_call(
         back_rows_kernel,
+        grid=(1,),
+        in_specs=[vmem] * 3
+        + [one_in(at, length, width)] * 2
+        + [vmem] * (inputs - 5)
+        + [pl.BlockSpec(memory_space=pl.ANY)] * len(output),
+        out_specs=[spec] + [vmem] * 6,
+        input_output_aliases={inputs: 0} if output else {},
         out_shape=[
-            shape((length, width), bf16), shape((length, width), f32),
+            full, shape((length, width), f32),
             shape((length, width), bf16), shape((width, width), bf16),
             shape((width, experts), f32), shape((1, width), f32), shape((1, experts), f32),
         ],
@@ -301,7 +322,7 @@
         ),
         name="back_rows",
     )(
-        target, route, returned, up, tokens, mixed, gain, wr, rbias, wo, *prior
+        target, route, returned, up, tokens, mixed, gain, wr, rbias, wo, *prior, *output
     )
 
 
@@ -309,7 +330,7 @@
     tokens_ref, gain_ref, gradmixed_ref, mixed_ref, wq_ref, wk_ref, wv_ref, q_ref, k_ref, v_ref,
     skew_ref, lse_ref, gradresid_ref, *refs,
 ):
-    prior_refs = refs[:-7]
+    prior_refs = refs[: (len(refs) - 7) // 3 * 3]
     line_ref, gw_ref, gradacts_ref, ggain_ref, normedt_ref, acc_ref, fold_ref = refs[-7:]
     step = pl.program_id(0)
     last = pl.num_programs(0) - 1
@@ -394,38 +415,42 @@
         weighted = grad_normed * gain_ref[...]
         slope = scale * scale * scale * jnp.mean(weighted * acts, axis=-1, keepdims=True)
         grad_acts = gradresid_ref[...] + (scale * weighted - acts * slope)
-        gradacts_ref[...] = grad_acts.astype(bf16)
+        gradacts_ref[0] = grad_acts.astype(bf16)
 
 
 def back_heads_call(
-    tokens, gain, grad_mixed, mixed, wq, wk, wv, q, k, v, skewed, lse, grad_resid, prior
+    at, count, tokens, gain, grad_mixed, mixed, wq, wk, wv, q, k, v, skewed, lse, grad_resid,
+    prior, grads,
 ):
-    length, width = tokens.shape
+    length, width = tokens.shape[1:]
     part = GROUP * HEAD
     groups = HEADS // GROUP
     whole = lambda *shape: pl.BlockSpec(shape, lambda g: (0,) * len(shape))
     columns = lambda size: pl.BlockSpec((size, part), lambda g: (0, g))
     shape = jax.ShapeDtypeStruct
+    spec, full = one_of(count, at, length, width)
     weights = pl.BlockSpec((3, width, part), lambda g: (0, 0, g))
     lines = pl.BlockSpec((1, GROUP, 2 * length), lambda g: (g, 0, 0))
     return pl.pallas_call(
         back_heads_kernel,
         grid=(groups,),
         in_specs=[
-            whole(length, width), whole(1, width), columns(length), columns(length),
+            one_in(at, length, width), whole(1, width), columns(length), columns(length),
             columns(width), columns(width), columns(width),
             columns(length), columns(length), columns(length),
             pl.BlockSpec((GROUP, BLOCK, skewed.shape[2]), lambda g: (g, 0, 0)),
             pl.BlockSpec((1, length, GROUP), lambda g: (g, 0, 0)), whole(length, width),
             *([weights, lines, whole(1, width)] if prior else []),
+            *([pl.BlockSpec(memory_space=pl.ANY)] * len(grads)),
         ],
         out_specs=[
             lines, weights,
-            whole(length, width), whole(1, width),
+            spec, whole(1, width),
         ],
+        input_output_aliases={13 + len(prior): 2} if grads else {},
         out_shape=[
             shape((groups, GROUP, 2 * length), f32), shape((3, width, width), bf16),
-            shape((length, width), bf16), shape((1, width), f32),
+            full, shape((1, width), f32),
         ],
         scratch_shapes=[
             pltpu.VMEM((width, length), bf16), pltpu.VMEM((length, width), f32),
@@ -439,7 +464,7 @@
         name="back_heads",
     )(
         tokens, gain, grad_mixed, mixed, wq, wk, wv, q, k, v, skewed, lse, grad_resid,
-        *prior,
+        *prior, *grads,
     )
 
 
@@ -534,6 +559,27 @@
         out.append(flat[:, at : at + size])
         at += size
     return out
+
+
+def tiles_of(shard, experts):
+    return -(-shard // 8), -(-experts // LANES) * LANES
+
+
+def small_slab(router, short, width):
+    lead, shard, experts = router.shape
+    tall, lanes = tiles_of(shard, experts)
+    router = jnp.pad(router, ((0, 0), (0, 8 * tall - shard), (0, lanes - experts)))
+    parts = [router[:, 8 * at : 8 * at + 8] for at in range(tall)]
+    parts.append(pack_rows(short, 8 * LANES).reshape(lead, 8, LANES))
+    slab = jnp.concatenate(parts, axis=2)
+    return jnp.pad(slab, ((0, 0), (0, 0), (0, width - slab.shape[2])))
+
+
+def slab_parts(slab, shard, experts, sizes):
+    tall, lanes = tiles_of(shard, experts)
+    parts = [slab[:, :, lanes * at : lanes * at + experts] for at in range(tall)]
+    short = slab[:, :, lanes * tall : lanes * tall + LANES]
+    return jnp.concatenate(parts, axis=1)[:, :shard], unpack_rows(short, sizes)
 
 
 def body(
@@ -579,28 +625,15 @@
         second = jnp.where(first >= 0, first + capacity, -1)
         return jnp.stack([first, second], axis=0)
 
-    small_parts = [w_router, gain_attn, gain_ffn, rel_bias, router_bias]
-    small = pack_rows([part.reshape(1, -1) for part in small_parts], 8 * LANES)
-    packed, small = lax.optimization_barrier(
-        (pack_call(w_query, w_key, w_value, w_output), small)
-    )
-    square, small = (packed, []), (small.reshape(8, LANES), [])
+    short = [gain_attn, gain_ffn, rel_bias, router_bias]
+    packed, short_router, *short = lax.optimization_barrier(
+        (pack_call(w_query, w_key, w_value, w_output), w_router, *short)
+    )
+    sizes = [part.size for part in short]
+    slab = small_slab(short_router[None], [part[None] for part in short], width)
+    square, small = (packed, []), (slab[0], [])
     for bit in far[::-1]:
         square, small = gather_step(square, bit), gather_step(small, bit)
-    value, ahead = lax.optimization_barrier((square[0], small[0]))
-    small = (ahead, small[1])
-    done = far[::-1]
-    value = value.reshape((2,) * len(far) + (4, -1, width))
-    low, high = ((lax.slice_in_dim(value, i, i + 2, axis=len(far)), done) for i in (0, 2))
-    for number, (one, two) in enumerate(zip(near[::-1], turned[::-1])):
-        low, high = gather_step(low, one), gather_step(high, two)
-        if number == 0:
-            for bit in near[::-1]:
-                small = gather_step(small, bit)
-            first, second, ahead = lax.optimization_barrier((low[0], high[0], small[0]))
-            low, high = (first, low[1]), (second, high[1])
-            small_all = gather_step((ahead, small[1]), 0)[0]
-
     spots = [plan(routes[at, :, 0], fill_rank[at]) for at in range(batches)]
     raw_spots = jnp.concatenate([spots[at][at] for at in range(batches)], axis=0)
     raw_ids = jnp.arange(2 * slots, dtype=jnp.int32)
@@ -609,11 +642,30 @@
         upstream_grad.reshape(batches * length, width),
         preferred_element_type=f32,
     ).astype(bf16)
-    small_all, raw_sent = lax.optimization_barrier((small_all, raw_sent))
+    value, small, raw_sent = lax.optimization_barrier((square[0], small[0], raw_sent))
+    done = far[::-1]
+    value = value.reshape((2,) * len(far) + (4, shard, width))
+    value = [lax.index_in_dim(value, i, len(far), keepdims=False) for i in range(4)]
+    low = (jnp.concatenate(value[:2] + [small], axis=-2), done)
+    high = (jnp.concatenate(value[2:], axis=-2), done)
+    for number, (one, two) in enumerate(zip(near[::-1], turned[::-1])):
+        low, high = gather_step(low, one), gather_step(high, two)
+        if number == 0:
+            first, second, raw_sent = lax.optimization_barrier((low[0], high[0], raw_sent))
+            low, high = (first, low[1]), (second, high[1])
+
     raw_arrived = exchange(raw_sent.reshape(devices, 2 * capacity, width))
 
-    wr_all, gain_one, gain_two, rel_flat, bias_all = unpack_rows(
-        small_all.reshape(devices, 1, -1), [part.size for part in small_parts]
+    first, second = lax.optimization_barrier((low[0], high[0]))
+    low, high = gather_step((first, low[1]), 0), gather_step((second, high[1]), 0)
+    low, high = (part[0].reshape(devices, -1, width) for part in (low, high))
+    wq, wk, wv, wo = (
+        part[:, i * shard : (i + 1) * shard].reshape(width, width)
+        for part in (low, high)
+        for i in range(2)
+    )
+    wr_all, (gain_one, gain_two, rel_flat, bias_all) = slab_parts(
+        low[:, 2 * shard :], shard, experts, sizes
     )
     wr_all = wr_all.reshape(width, experts)
     gain_one = gain_one.reshape(1, width).astype(f32)
@@ -630,36 +682,25 @@
     row = np.arange(count * capacity, dtype=np.int32)
     row = row + (row // capacity) * capacity
     place = jnp.asarray(np.stack([row, row + capacity], axis=1))
-    first, second, skewed, wr_all, gain_one, gain_two, bias_all = lax.optimization_barrier(
-        (low[0], high[0], skewed, wr_all, gain_one, gain_two, bias_all)
-    )
-    low, high = gather_step((first, low[1]), 0), gather_step((second, high[1]), 0)
-    wq, wk, wv, wo = (
-        lax.index_in_dim(part[0].reshape(devices, 2, -1, width), i, 1).reshape(width, width)
-        for part in (low, high)
-        for i in range(2)
-    )
-
     fronts, arrived, returned = [], [], []
+    acts = tokens
     for at in range(batches):
-        acts = tokens[at]
         if at == 1:
-            raw = raw_arrived.reshape(devices, batches, capacity, width)
-            raw = [raw[:, i].reshape(slots, width) for i in range(batches)]
-            acts, raw, targets = lax.optimization_barrier(
-                (acts, raw, [(spots[i].T, routes[i]) for i in range(batches)])
+            acts, raw_arrived, targets = lax.optimization_barrier(
+                (acts, raw_arrived, [(spots[i].T, routes[i]) for i in range(batches)])
             )
         front = front_call(
-            acts, wq, wk, wv, wo, skewed, gain_one, gain_two, spots[at], slots
+            at, acts, wq, wk, wv, wo, skewed, gain_one, gain_two, spots[at], slots
         )
         fronts.append(front)
         arrived.append(exchange(front[-1].reshape(devices, 2 * capacity, width // 2)))
     grad_in = grad_out = 0.0
     for at in range(batches):
         sent, rows, active, grad_inner, grad_result = expert_call(
+            at,
             own,
             arrived[at].reshape(2 * slots, width // 2),
-            raw[at],
+            raw_arrived.reshape(2 * slots, width),
             wr_all,
             bias_all,
             place,
@@ -674,71 +715,82 @@
         back, grad_in, grad_out = lax.optimization_barrier((back, grad_in, grad_out))
         returned.append(back)
 
-    row_parts, head_parts = [], []
-    row_prior, head_prior = [], []
+    row_prior, head_prior, outputs, grads = [], [], [], []
     for at in range(batches):
         q, k, v, mixed, lse, sent = fronts[at]
         row_part = back_rows_call(
-            *targets[at], returned[at].reshape(2 * slots, width), upstream_grad[at],
-            tokens[at], mixed, gain_two, wr_all, bias_all, wo, row_prior,
+            at, batches, *targets[at], returned[at].reshape(2 * slots, width), upstream_grad,
+            tokens, mixed, gain_two, wr_all, bias_all, wo, row_prior,
+            outputs,
         )
+        outputs = row_part[:1]
         row_prior = row_part[3:]
         head_part = back_heads_call(
-            tokens[at], gain_one, row_part[2], mixed, wq, wk, wv, q, k, v, skewed, lse,
-            row_part[1], head_prior,
+            at, batches, tokens, gain_one, row_part[2], mixed, wq, wk, wv, q, k, v, skewed, lse,
+            row_part[1], head_prior, grads,
         )
+        grads = head_part[2:3]
         head_prior = [head_part[1], head_part[0], head_part[3]]
-        row_parts.append(row_part)
-        head_parts.append(head_part)
-
-    def halved(value):
-        value = value.reshape((-1,) + (2,) * bits + (shard, width))
-        return scatter_step((value, list(range(bits))[::-1]), 0)
 
     g_output, g_router, g_gain_two, g_bias = row_prior
     g_heads, lines, g_gain_one = head_prior
-    outer, inner = halved(g_output[None]), halved(g_heads)
-    low, high = inner[0][:2], jnp.concatenate([inner[0][2:], outer[0]], axis=0)
-    low, high, g_router, g_gain_two, g_bias, lines, g_gain_one = lax.optimization_barrier(
-        (low, high, g_router, g_gain_two, g_bias, lines, g_gain_one)
-    )
-    low, high = (low, inner[1]), (high, inner[1])
-    g_rel = jnp.einsum(
-        "hn,bn->bh",
-        lines.reshape(HEADS, span),
-        bucket_hot.astype(f32),
-        precision=lax.Precision.HIGHEST,
-    )
-    short = [part.reshape(devices, -1) for part in (g_gain_one, g_gain_two, g_rel, g_bias)]
-    sizes = [part.shape[1] for part in short]
-    short_pack = pack_rows(short, 8 * LANES).reshape(devices, -1, LANES).astype(bf16)
-    lanes = -(-experts // LANES) * LANES
-    router_pack = jnp.pad(g_router.astype(bf16), ((0, 0), (0, lanes - experts)))
-    router_pack = router_pack.reshape(devices, -1, LANES)
-    small = jnp.concatenate([router_pack, short_pack], axis=1)
-    small = (small.reshape((1,) + (2,) * bits + small.shape[1:]), list(range(bits))[::-1])
-    small_bits = [0] + near + far
-    for one, two in zip(near, turned):
+    def halved(parts):
+        value = jnp.concatenate([part.astype(bf16) for part in parts], axis=1)
+        value = value.reshape((1,) + (2,) * bits + value.shape[1:])
+        return scatter_step((value, list(range(bits))[::-1]), 0)
+
+    outer = halved([g_output.reshape(devices, shard, width)])
+    g_heads = g_heads.reshape(3, devices, shard, width)
+    inner = halved(list(g_heads))
+    cut = 2 * shard
+    low = (inner[0][..., :cut, :], inner[1])
+    high = (jnp.concatenate([inner[0][..., cut:, :], outer[0]], axis=-2), inner[1])
+    for number, (one, two) in enumerate(zip(near, turned)):
         low, high = scatter_step(low, one), scatter_step(high, two)
-    held = (jnp.concatenate([low[0], high[0]], axis=0), low[1])
+        if number == 0:
+            first, second, g_router, g_gain_two, g_bias, lines, g_gain_one = (
+                lax.optimization_barrier(
+                    (low[0], high[0], g_router, g_gain_two, g_bias, lines, g_gain_one)
+                )
+            )
+            low, high = (first, low[1]), (second, high[1])
+            g_rel = jnp.einsum(
+                "hn,bn->bh",
+                lines.reshape(HEADS, span),
+                bucket_hot.astype(f32),
+                precision=lax.Precision.HIGHEST,
+            )
+            short = [
+                part.reshape(devices, -1) for part in (g_gain_one, g_gain_two, g_rel, g_bias)
+            ]
+            short_pack = pack_rows(short, 8 * LANES).reshape(devices, -1, LANES).astype(bf16)
+            lanes = -(-experts // LANES) * LANES
+            router_pack = jnp.pad(g_router.astype(bf16), ((0, 0), (0, lanes - experts)))
+            router_pack = router_pack.reshape(devices, -1, LANES)
+            small = jnp.concatenate([router_pack, short_pack], axis=1)
+            small = (small.reshape((1,) + (2,) * bits + small.shape[1:]), list(range(bits))[::-1])
+            for bit in [0] + near:
+                small = scatter_step(small, bit)
+    held = (jnp.concatenate([low[0], high[0]], axis=-2), low[1])
     for bit in far:
-        held = scatter_step(held, bit)
-    for bit in small_bits:
-        small = scatter_step(small, bit)
-    r_query, r_key, r_value, r_output = (held[0][i] for i in range(4))
+        value, ahead = lax.optimization_barrier((held[0], small[0]))
+        held = scatter_step((value, held[1]), bit)
+        small = scatter_step((ahead, small[1]), bit)
+    r_query, r_key, r_value, r_output = jnp.split(
+        held[0][0], [shard, 2 * shard, 3 * shard], axis=0
+    )
     cut = router_pack.shape[1]
     r_router = small[0][0, :cut].reshape(shard, lanes)[:, :experts]
-    tail = unpack_rows(small[0][:, cut:], sizes)
+    tail = unpack_rows(small[0][:, cut:], [part.shape[1] for part in short])
     r_gain_one, r_gain_two, r_rel, r_bias = (
         part.reshape(shape)
         for part, shape in zip(
-            tail,
-            (gain_attn.shape, gain_ffn.shape, rel_bias.shape, router_bias.shape),
+            tail, (gain_attn.shape, gain_ffn.shape, rel_bias.shape, router_bias.shape)
         )
     )
     return (
-        jnp.stack([row_part[0] for row_part in row_parts], axis=0),
-        jnp.stack([part[2] for part in head_parts], axis=0),
+        outputs[0],
+        grads[0],
         r_query,
         r_key,
         r_value,

time: 357 us -> 352 us (0.986)
  waiting for transfers between devices: 76.7 us -> 87 us
  local copies, waits for them, and re-layouts: 30.7 us -> 20.6 us
    ppermute x26 -> x23, waiting for transfers between devices: 62.8 us -> 71.4 us  [swap(): lax.ppermute(value, AXES, [(at, at ^ 1 << bit) for at in range(devices)])]
    ppermute x26 -> x23, starting transfers between devices: 33.7 us -> 26 us  [swap(): lax.ppermute(value, AXES, [(at, at ^ 1 << bit) for at in range(devices)])]
    all_to_all x5, starting transfers between devices: 20.4 us -> 24.6 us  [exchange(): return lax.all_to_all(buffer, AXES, split_axis=0, concat_axis=0, tiled=True)]
  transfers between devices with their start and end apart: 31 -> 28, of which waited for: 22 -> 21; matrix products, arithmetic and copies ran while one was open for 19% -> 17% of each run, Pallas kernels for 30% -> 31%
where the time goes in v2:
time: 352 us; the launch traced here: 348 us
  Pallas kernels  138 us (39%)
  waiting for transfers between devices  87 us (25%)
  starting transfers between devices  50.6 us (14%)
  matrix products  39.2 us (11%)
  local copies, waits for them, and re-layouts  20.6 us (6%)
  other arithmetic  10 us (3%)
    ppermute x23, waiting for transfers between devices, swap(): lax.ppermute(value, AXES, [(at, at ^ 1 << bit) for at in range(devices)])  71.4 us
    pallas_call x2, Pallas kernels, expert_call(): pl.pallas_call(functools.partial(expert_kernel, mine_at), grid_spec=pltpu...  46.5 us
    pallas_call x2, Pallas kernels, back_heads_call(): pl.pallas_call(back_heads_kernel, grid=(groups,), in_specs=[one_in(at, le...  38.3 us
    pallas_call x2, Pallas kernels, front_call(): pl.pallas_call(front_kernel, grid=(groups,), in_specs=[one_in(at, length,...  30.9 us
    ppermute x23, starting transfers between devices, swap(): lax.ppermute(value, AXES, [(at, at ^ 1 << bit) for at in range(devices)])  26 us
    all_to_all x5, starting transfers between devices, exchange(): return lax.all_to_all(buffer, AXES, split_axis=0, concat_axis=0, tiled=True)  24.6 us
    pallas_call x2, Pallas kernels, back_rows_call(): pl.pallas_call(back_rows_kernel, grid=(1,), in_specs=[vmem] * 3 + [one_in...  19.1 us
    dot_general x2, matrix products, body(): jnp.einsum('rd,rf->df', rows, grad_inner, preferred_element_type=f32)  17.8 us
  transfers between devices with their start and end apart: 28, of which 21 were waited for; matrix products, arithmetic and copies ran while one was open for 17% of the time, Pallas kernels for 31%

profile of v2, /device:TPU:0, one launch (start us, length us, event | category | flops | bytes accessed | tf_op | source)
XLA Modules:
  0.0 347.6 jit_solution(10335852044499499732)
XLA Ops:
  10.7 5.1 %fusion.1 = bf16[1280,768]{1,0:T(8,128)(2,1)} fusion(bf16[1024,768]{1,0:T(8,128)(2,1)} %bitcast.287, s32[1024]{0:T(1024)S(1)} %pad_add_fusion), kind=kOutput, calls=%fused_computation.6 | convolution fusion | flops 2015559680 | bytes 3543040 | tf_op jit(solution)/shard_map/dot_general | solution.py:640
  20.0 6.1 %collective-permute-done.1 = bf16[2,4,24,768]{3,2,1,0:T(8,128)(2,1)S(1)} collective-permute-done((bf16[2,4,24,768]{3,2,1,0:T(8,128)(2,1)S(1)}, bf16[2,4,24,768]{3,2,1,0:T(8,128)(2,1)S(1)}, u32[]{:S(2)}, u32[]{:S(2)}) %collective-permute-start.1) | collective-permute-done | bytes 294944 | tf_op jit(solution)/shard_map/ppermute | solution.py:512
  38.4 4.5 %all-to-all-start = ((bf16[32,40,768]{2,1,0:T(8,128)(2,1)}), bf16[32,40,768]{2,1,0:T(8,128)(2,1)}, u32[]{:S(2)}, u32[]{:S(2)}) async-start(bf16[32,40,768]{2,1,0:T(8,128)(2,1)} %bitcast.27), calls=%async_computation | async-start | bytes 3932160 | tf_op jit(solution)/shard_map/all_to_all | solution.py:507
  42.9 11.4 %collective-permute-done.7 = bf16[2,2,2,48,768]{4,3,0,1,2:T(8,128)(2,1)S(1)} collective-permute-done((bf16[2,2,2,48,768]{4,3,0,1,2:T(8,128)(2,1)S(1)}, bf16[2,2,2,48,768]{4,3,0,1,2:T(8,128)(2,1)S(1)}, u32[]{:S(2)}, u32[]{:S(2)}) %collective-permute-start.7) | collective-permute-done | bytes 589856 | tf_op jit(solution)/shard_map/ppermute | solution.py:512
  54.5 8.0 %collective-permute-done.6 = bf16[2,2,2,56,768]{4,3,0,1,2:T(8,128)(2,1)S(1)} collective-permute-done((bf16[2,2,2,56,768]{4,3,0,1,2:T(8,128)(2,1)S(1)}, bf16[2,2,2,56,768]{4,3,0,1,2:T(8,128)(2,1)S(1)}, u32[]{:S(2)}, u32[]{:S(2)}) %collective-permute-start.6) | collective-permute-done | bytes 688160 | tf_op jit(solution)/shard_map/ppermute | solution.py:512
  77.7 15.5 %front.3 = (bf16[512,768]{1,0:T(8,128)(2,1)}, bf16[512,768]{1,0:T(8,128)(2,1)}, bf16[512,768]{1,0:T(8,128)(2,1)}, bf16[512,768]{1,0:T(8,128)(2,1)}, f32[3,512,4]{2,1,0:T(8,128)}, /*index=5*/bf16[1280,384]{1,0:T(8,128)(2,1)}) custom-call(bf16[2,512,768]{2,1,0:T(8,128)(2,1)} %tokens_ref.10, bf16[768,768]{1,0:T(8,128)(2,1)} %bitcast.235, ...), custom_call_target="tpu_custom_call" | custom-call | flops 1000000 | bytes 262144 | tf_op jit(solution)/shard_map/front/pallas_call | solution.py:117
  93.2 5.4 %all-to-all-start.2 = ((bf16[32,40,384]{2,1,0:T(8,128)(2,1)}), bf16[32,40,384]{2,1,0:T(8,128)(2,1)}, u32[]{:S(2)}, u32[]{:S(2)}) async-start(bf16[32,40,384]{2,1,0:T(8,128)(2,1)} %bitcast.252), calls=%async_computation.2 | async-start | bytes 1966080 | tf_op jit(solution)/shard_map/all_to_all | solution.py:507
  100.4 15.4 %front.2 = (bf16[512,768]{1,0:T(8,128)(2,1)}, bf16[512,768]{1,0:T(8,128)(2,1)}, bf16[512,768]{1,0:T(8,128)(2,1)}, bf16[512,768]{1,0:T(8,128)(2,1)}, f32[3,512,4]{2,1,0:T(8,128)}, /*index=5*/bf16[1280,384]{1,0:T(8,128)(2,1)}) custom-call(bf16[2,512,768]{2,1,0:T(8,128)(2,1)} %tokens_ref.10, bf16[768,768]{1,0:T(8,128)(2,1)} %bitcast.236, ...), custom_call_target="tpu_custom_call" | custom-call | flops 1000000 | bytes 262144 | tf_op jit(solution)/shard_map/front/pallas_call | solution.py:117
  115.8 7.7 %all-to-all-done.2 = bf16[32,40,384]{2,1,0:T(8,128)(2,1)} async-done(((bf16[32,40,384]{2,1,0:T(8,128)(2,1)}), bf16[32,40,384]{2,1,0:T(8,128)(2,1)}, u32[]{:S(2)}, u32[]{:S(2)}) %all-to-all-start.2) | async-done | bytes 983072 | tf_op jit(solution)/shard_map/all_to_all | solution.py:507
  128.9 23.2 %expert.3 = (bf16[1280,768]{1,0:T(8,128)(2,1)}, bf16[640,768]{1,0:T(8,128)(2,1)}, bf16[640,3072]{1,0:T(8,128)(2,1)}, bf16[640,3072]{1,0:T(8,128)(2,1)}, bf16[640,768]{1,0:T(8,128)(2,1)}) custom-call(s32[1]{0:T(128)} %bitcast.36.own_ref, bf16[1280,384]{1,0:T(8,128)(2,1)} %bitcast.59.arrived_ref, bf16[1280,768]{1,0:T(8,128)(2,1)} %bitcast.53.raw_ref, ...), custom_call_target="tpu_custom_call" | custom-call | flops 12079595520 | bytes 20971520 | tf_op jit(solution)/shard_map/expert/pallas_call | solution.py:218
  152.3 6.1 %all-to-all-start.3 = ((bf16[32,40,768]{2,1,0:T(8,128)(2,1)}), bf16[32,40,768]{2,1,0:T(8,128)(2,1)S(1)}, u32[]{:S(2)}, u32[]{:S(2)}) async-start(bf16[32,40,768]{2,1,0:T(8,128)(2,1)} %bitcast.249), calls=%async_computation.3 | async-start | bytes 3932160 | tf_op jit(solution)/shard_map/all_to_all | solution.py:507
  158.4 8.6 %fusion.55 = f32[768,3072]{1,0:T(8,128)} fusion(bf16[640,768]{1,0:T(8,128)(2,1)S(1)} %copy-done.6, bf16[640,3072]{1,0:T(8,128)(2,1)} %get-tuple-element.120), kind=kOutput, calls=%fused_computation.175 | convolution fusion | flops 3019898880 | bytes 14352384 | tf_op jit(solution)/shard_map/rd,rf->df/dot_general | solution.py:712
  167.0 6.4 %fusion.56 = f32[3072,768]{1,0:T(8,128)} fusion(bf16[640,3072]{1,0:T(8,128)(2,1)S(1)} %copy-done.17, bf16[640,768]{1,0:T(8,128)(2,1)S(1)} %copy-done.18), kind=kOutput, calls=%fused_computation.176 | convolution fusion | flops 3019898880 | bytes 14352384 | tf_op jit(solution)/shard_map/rf,rd->fd/dot_general | solution.py:713
  173.4 23.3 %expert.2 = (bf16[1280,768]{1,0:T(8,128)(2,1)}, bf16[640,768]{1,0:T(8,128)(2,1)}, bf16[640,3072]{1,0:T(8,128)(2,1)}, bf16[640,3072]{1,0:T(8,128)(2,1)}, bf16[640,768]{1,0:T(8,128)(2,1)}) custom-call(s32[1]{0:T(128)} %bitcast.36.own_ref, bf16[1280,384]{1,0:T(8,128)(2,1)} %bitcast.52.arrived_ref, bf16[1280,768]{1,0:T(8,128)(2,1)} %bitcast.53.raw_ref, ...), custom_call_target="tpu_custom_call" | custom-call | flops 12079595520 | bytes 20971520 | tf_op jit(solution)/shard_map/expert/pallas_call | solution.py:218
  196.6 7.8 %all-to-all-done.3 = bf16[32,40,768]{2,1,0:T(8,128)(2,1)S(1)} async-done(((bf16[32,40,768]{2,1,0:T(8,128)(2,1)}), bf16[32,40,768]{2,1,0:T(8,128)(2,1)S(1)}, u32[]{:S(2)}, u32[]{:S(2)}) %all-to-all-start.3) | async-done | bytes 1966112 | tf_op jit(solution)/shard_map/all_to_all | solution.py:507
  205.7 4.6 %all-to-all-start.4 = ((bf16[32,40,768]{2,1,0:T(8,128)(2,1)}), bf16[32,40,768]{2,1,0:T(8,128)(2,1)}, u32[]{:S(2)}, u32[]{:S(2)}) async-start(bf16[32,40,768]{2,1,0:T(8,128)(2,1)} %bitcast.247), calls=%async_computation.4 | async-start | bytes 3932160 | tf_op jit(solution)/shard_map/all_to_all | solution.py:507
  212.0 9.2 %back_rows.2 = (bf16[2,512,768]{2,1,0:T(8,128)(2,1)}, f32[512,768]{1,0:T(8,128)}, bf16[512,768]{1,0:T(8,128)(2,1)}, bf16[768,768]{1,0:T(8,128)(2,1)}, f32[768,32...) custom-call(s32[512,2]{1,0:T(8,128)} %bitcast.255, s32[512,1]{1,0:T(8,128)} %copy.86.route_ref, ...), custom_call_target="tpu_custom_call" | custom-call | flops 3825205248 | bytes 12582912 | tf_op jit(solution)/shard_map/back_rows/pallas_call | solution.py:304
  221.2 18.9 %back_heads.2 = (f32[3,4,1024]{2,1,0:T(4,128)}, bf16[3,768,768]{2,1,0:T(8,128)(2,1)}, bf16[2,512,768]{2,1,0:T(8,128)(2,1)}, f32[1,768]{1,0:T(1,128)}) custom-call(bf16[2,512,768]{2,1,0:T(8,128)(2,1)} %tokens_ref.10, f32[1,768]{1,0:T(1,128)} %reshape.963.gain_one_ref.gain_ref, bf16[512,768]{1,0:T(8,128)(2,1)} %get-tuple-element.150.gradmixed_ref, ...), custom_call_target="tpu_custom_call" | custom-call | flops 10066329600 | bytes 22020096 | tf_op jit(solution)/shard_map/back_heads/pallas_call | solution.py:434
  240.1 9.3 %convolution_add_fusion.1 = f32[768,3072]{1,0:T(8,128)} fusion(f32[768,3072]{1,0:T(8,128)} %fusion.55, bf16[640,768]{1,0:T(8,128)(2,1)} %get-tuple-element.127, bf16[640,3072]{1,0:T(8,128)(2,1)S(1)} %copy-done.2), kind=kOutput, calls=%fused_computation.3 | convolution fusion | flops 3022258176 | bytes 23789568 | tf_op jit(solution)/shard_map/rd,rf->df/dot_general | solution.py:712
  249.4 8.7 %convolution_add_fusion = f32[3072,768]{1,0:T(8,128)} fusion(f32[3072,768]{1,0:T(8,128)} %fusion.56, bf16[640,3072]{1,0:T(8,128)(2,1)S(1)} %copy-done.1, bf16[640,768]{1,0:T(8,128)(2,1)S(1)} %copy-done.5), kind=kOutput, calls=%fused_computation.2 | convolution fusion | flops 3022258176 | bytes 23789568 | tf_op jit(solution)/shard_map/rf,rd->fd/dot_general | solution.py:713
  258.1 9.9 %back_rows.3 = (bf16[2,512,768]{2,1,0:T(8,128)(2,1)}, f32[512,768]{1,0:T(8,128)}, bf16[512,768]{1,0:T(8,128)(2,1)}, bf16[768,768]{1,0:T(8,128)(2,1)}, f32[768,32...) custom-call(s32[512,2]{1,0:T(8,128)} %bitcast.254, ...), custom_call_target="tpu_custom_call", output_to_operand_aliasing={{0}: (14, {})} | custom-call | flops 3825205248 | bytes 12582912 | tf_op jit(solution)/shard_map/back_rows/pallas_call | solution.py:304
  268.0 19.4 %back_heads.3 = (f32[3,4,1024]{2,1,0:T(4,128)}, bf16[3,768,768]{2,1,0:T(8,128)(2,1)}, bf16[2,512,768]{2,1,0:T(8,128)(2,1)}, f32[1,768]{1,0:T(1,128)}) custom-call(bf16[2,512,768]{2,1,0:T(8,128)(2,1)} %tokens_ref.10, f32[1,768]{1,0:T(1,128)} %reshape.963.gain_one_ref.gain_ref, ...), custom_call_target="tpu_custom_call", output_to_operand_aliasing={{2}: (16, {})} | custom-call | flops 10066329600 | bytes 22020096 | tf_op jit(solution)/shard_map/back_heads/pallas_call | solution.py:434
  298.8 11.8 %collective-permute-done.11 = bf16[1,2,2,2,48,768]{5,4,1,2,3,0:T(8,128)(2,1)S(1)} collective-permute-done((bf16[1,2,2,2,48,768]{5,4,1,2,3,0:T(8,128)(2,1)S(1)}, bf16[1,2,2,2,48,768]{5,4,1,2,3,0:T(8,128)(2,1)S(1)}, u32[]{:S(2)}, u32[]{:S(2)}) %collective-permute-start.11) | collective-permute-done | bytes 589856 | tf_op jit(solution)/shard_map/ppermute | solution.py:512
  331.4 4.9 %collective-permute-done.20 = bf16[1,2,32,128]{3,2,1,0:T(8,128)(2,1)S(1)} collective-permute-done((bf16[1,2,32,128]{3,2,1,0:T(8,128)(2,1)S(1)}, bf16[1,2,32,128]{3,2,1,0:T(8,128)(2,1)S(1)}, u32[]{:S(2)}, u32[]{:S(2)}) %collective-permute-start.20) | collective-permute-done | bytes 16416 | tf_op jit(solution)/shard_map/ppermute | solution.py:512
  (194 shorter events, 94.3 us)
Async XLA Ops:
  2.1 15.7 %collective-permute-start = (bf16[4,24,768]{2,1,0:T(8,128)(2,1)}, bf16[4,24,768]{2,1,0:T(8,128)(2,1)S(1)}, u32[]{:S(2)}, u32[]{:S(2)}) collective-permute-start(bf16[4,24,768]{2,1,0:T(8,128)(2,1)} %pack.1), channel_id=1, source_target_pairs={{0,16},{1,17},{2,18},{3,19},{4,20},{5,21},{6,22},{7,23},{8,24},{9,... | collective-permute-start | bytes 442376 | tf_op jit(solution)/shard_map/ppermute | solution.py:512
  8.3 7.5 %collective-permute-start.2 = (bf16[8,768]{1,0:T(8,128)(2,1)S(1)}, bf16[8,768]{1,0:T(8,128)(2,1)S(1)}, u32[]{:S(2)}, u32[]{:S(2)}) collective-permute-start(bf16[8,768]{1,0:T(8,128)(2,1)S(1)} %fusion.44), channel_id=1, source_target_pairs={{0,16},{1,17},{2,18},{3,19},{4,20},{5,21},{6,22},{7,23},{8,24},{9,... | collective-permute-start | bytes 36872 | tf_op jit(solution)/shard_map/ppermute | solution.py:512
  17.9 8.2 %collective-permute-start.1 = (bf16[2,4,24,768]{3,2,1,0:T(8,128)(2,1)S(1)}, bf16[2,4,24,768]{3,2,1,0:T(8,128)(2,1)S(1)}, u32[]{:S(2)}, u32[]{:S(2)}) collective-permute-start(bf16[2,4,24,768]{3,2,1,0:T(8,128)(2,1)S(1)} %pad_maximum_fusion.11), channel_id=1, source_target_pairs={{0,8},{1,9},{2,10},{3,11},{4,12},{5,13},{6,14},{7,15},{8,0},{9,1},... | collective-permute-start | bytes 884744 | tf_op jit(solution)/shard_map/ppermute | solution.py:512
  26.3 7.3 %collective-permute-start.5 = (bf16[2,2,48,768]{3,2,0,1:T(8,128)(2,1)S(1)}, bf16[2,2,48,768]{3,2,0,1:T(8,128)(2,1)S(1)}, u32[]{:S(2)}, u32[]{:S(2)}) collective-permute-start(bf16[2,2,48,768]{3,2,0,1:T(8,128)(2,1)S(1)} %pad_maximum_fusion.12), channel_id=1, source_target_pairs={{0,2},{1,3},{2,0},{3,1},{4,6},{5,7},{6,4},{7,5},{8,10},{9,11},{10,... | collective-permute-start | bytes 884744 | tf_op jit(solution)/shard_map/ppermute | solution.py:512
  27.9 8.1 %collective-permute-start.4 = (bf16[2,2,56,768]{3,2,0,1:T(8,128)(2,1)S(1)}, bf16[2,2,56,768]{3,2,0,1:T(8,128)(2,1)S(1)}, u32[]{:S(2)}, u32[]{:S(2)}) collective-permute-start(bf16[2,2,56,768]{3,2,0,1:T(8,128)(2,1)S(1)} %pad_maximum_fusion.10), channel_id=1, source_target_pairs={{0,4},{1,5},{2,6},{3,7},{4,0},{5,1},{6,2},{7,3},{8,12},{9,13},{10,... | collective-permute-start | bytes 1032200 | tf_op jit(solution)/shard_map/ppermute | solution.py:512
  36.3 18.0 %collective-permute-start.7 = (bf16[2,2,2,48,768]{4,3,0,1,2:T(8,128)(2,1)S(1)}, bf16[2,2,2,48,768]{4,3,0,1,2:T(8,128)(2,1)S(1)}, u32[]{:S(2)}, u32[]{:S(2)}) collective-permute-start(bf16[2,2,2,48,768]{4,3,0,1,2:T(8,128)(2,1)S(1)} %pad_maximum_fusion.9), channel_id=1, source_target_pairs={{0,4},{1,5},{2,6},{3,7},{4,0},{5,1},{6,2},{7,3},{8,12},{9,13},{10,... | collective-permute-start | bytes 1769480 | tf_op jit(solution)/shard_map/ppermute | solution.py:512
  37.8 24.6 %collective-permute-start.6 = (bf16[2,2,2,56,768]{4,3,0,1,2:T(8,128)(2,1)S(1)}, bf16[2,2,2,56,768]{4,3,0,1,2:T(8,128)(2,1)S(1)}, u32[]{:S(2)}, u32[]{:S(2)}) collective-permute-start(bf16[2,2,2,56,768]{4,3,0,1,2:T(8,128)(2,1)S(1)} %pad_maximum_fusion.7), channel_id=1, source_target_pairs={{0,2},{1,3},{2,0},{3,1},{4,6},{5,7},{6,4},{7,5},{8,10},{9,11},{10,... | collective-permute-start | bytes 2064392 | tf_op jit(solution)/shard_map/ppermute | solution.py:512
  38.4 54.8 %all-to-all-start = ((bf16[32,40,768]{2,1,0:T(8,128)(2,1)}), bf16[32,40,768]{2,1,0:T(8,128)(2,1)}, u32[]{:S(2)}, u32[]{:S(2)}) async-start(bf16[32,40,768]{2,1,0:T(8,128)(2,1)} %bitcast.27), calls=%async_computation | async-start | bytes 3932160 | tf_op jit(solution)/shard_map/all_to_all | solution.py:507
  62.8 6.4 %collective-permute-start.8 = (bf16[2,2,2,2,56,768]{5,4,0,1,2,3:T(8,128)(2,1)S(1)}, bf16[2,2,2,2,56,768]{5,4,0,1,2,3:T(8,128)(2,1)}, u32[]{:S(2)}, u32[]{:S(2)}) collective-permute-start(bf16[2,2,2,2,56,768]{5,4,0,1,2,3:T(8,128)(2,1)S(1)} %pad_maximum_fusion.3), channel_id=1, source_target_pairs={{0,1},{1,0},{2,3},{3,2},{4,5},{5,4},{6,7},{7,6},{8,9},{9,8},{10,11... | collective-permute-start | bytes 4128776 | tf_op jit(solution)/shard_map/ppermute | solution.py:512
  93.2 30.3 %all-to-all-start.2 = ((bf16[32,40,384]{2,1,0:T(8,128)(2,1)}), bf16[32,40,384]{2,1,0:T(8,128)(2,1)}, u32[]{:S(2)}, u32[]{:S(2)}) async-start(bf16[32,40,384]{2,1,0:T(8,128)(2,1)} %bitcast.252), calls=%async_computation.2 | async-start | bytes 1966080 | tf_op jit(solution)/shard_map/all_to_all | solution.py:507
  123.5 28.8 %all-to-all-start.1 = ((bf16[32,40,384]{2,1,0:T(8,128)(2,1)}), bf16[32,40,384]{2,1,0:T(8,128)(2,1)}, u32[]{:S(2)}, u32[]{:S(2)}) async-start(bf16[32,40,384]{2,1,0:T(8,128)(2,1)} %bitcast.251), calls=%async_computation.1 | async-start | bytes 1966080 | tf_op jit(solution)/shard_map/all_to_all | solution.py:507
  152.3 52.1 %all-to-all-start.3 = ((bf16[32,40,768]{2,1,0:T(8,128)(2,1)}), bf16[32,40,768]{2,1,0:T(8,128)(2,1)S(1)}, u32[]{:S(2)}, u32[]{:S(2)}) async-start(bf16[32,40,768]{2,1,0:T(8,128)(2,1)} %bitcast.249), calls=%async_computation.3 | async-start | bytes 3932160 | tf_op jit(solution)/shard_map/all_to_all | solution.py:507
  205.7 52.4 %all-to-all-start.4 = ((bf16[32,40,768]{2,1,0:T(8,128)(2,1)}), bf16[32,40,768]{2,1,0:T(8,128)(2,1)}, u32[]{:S(2)}, u32[]{:S(2)}) async-start(bf16[32,40,768]{2,1,0:T(8,128)(2,1)} %bitcast.247), calls=%async_computation.4 | async-start | bytes 3932160 | tf_op jit(solution)/shard_map/all_to_all | solution.py:507
  291.7 5.1 %collective-permute-start.12 = (bf16[1,2,2,2,2,24,768]{6,5,1,2,4,3,0:T(8,128)(2,1)S(1)}, bf16[1,2,2,2,2,24,768]{6,5,1,2,4,3,0:T(8,128)(2,1)S(1)}, u32[]{:S(2)}, u32[]{:S(2)}) collective-permute-start(bf16[1,2,2,2,2,24,768]{6,5,1,2,4,3,0:T(8,128)(2,1)S(1)} %select_bitcast_fusion.7), channel_id=1, source_target_pairs={{0,1},{1,0},{2,3},{3,2},{4,5},{5,4},{6,7},{7,6},{8,9},{9,8},{10,11... | collective-permute-start | bytes 1769480 | tf_op jit(solution)/shard_map/ppermute | solution.py:512
  294.9 15.7 %collective-permute-start.11 = (bf16[1,2,2,2,48,768]{5,4,1,2,3,0:T(8,128)(2,1)S(1)}, bf16[1,2,2,2,48,768]{5,4,1,2,3,0:T(8,128)(2,1)S(1)}, u32[]{:S(2)}, u32[]{:S(2)}) collective-permute-start(bf16[1,2,2,2,48,768]{5,4,1,2,3,0:T(8,128)(2,1)S(1)} %fusion.10), channel_id=1, source_target_pairs={{0,2},{1,3},{2,0},{3,1},{4,6},{5,7},{6,4},{7,5},{8,10},{9,11},{10,... | collective-permute-start | bytes 1769480 | tf_op jit(solution)/shard_map/ppermute | solution.py:512
  297.2 15.2 %collective-permute-start.13 = (bf16[1,2,2,2,48,768]{5,4,1,2,3,0:T(8,128)(2,1)S(1)}, bf16[1,2,2,2,48,768]{5,4,1,2,3,0:T(8,128)(2,1)S(1)}, u32[]{:S(2)}, u32[]{:S(2)}) collective-permute-start(bf16[1,2,2,2,48,768]{5,4,1,2,3,0:T(8,128)(2,1)S(1)} %fusion.11), channel_id=1, source_target_pairs={{0,4},{1,5},{2,6},{3,7},{4,0},{5,1},{6,2},{7,3},{8,12},{9,13},{10,... | collective-permute-start | bytes 1769480 | tf_op jit(solution)/shard_map/ppermute | solution.py:512
  315.0 5.0 %collective-permute-start.17 = (bf16[1,2,2,2,32,128]{5,4,1,2,3,0:T(8,128)(2,1)S(1)}, bf16[1,2,2,2,32,128]{5,4,1,2,3,0:T(8,128)(2,1)S(1)}, u32[]{:S(2)}, u32[]{:S(2)}) collective-permute-start(bf16[1,2,2,2,32,128]{5,4,1,2,3,0:T(8,128)(2,1)S(1)} %fusion.26), channel_id=1, source_target_pairs={{0,2},{1,3},{2,0},{3,1},{4,6},{5,7},{6,4},{7,5},{8,10},{9,11},{10,... | collective-permute-start | bytes 196616 | tf_op jit(solution)/shard_map/ppermute | solution.py:512
  316.0 9.6 %collective-permute-start.15 = (bf16[1,2,2,48,768]{4,3,1,2,0:T(8,128)(2,1)S(1)}, bf16[1,2,2,48,768]{4,3,1,2,0:T(8,128)(2,1)S(1)}, u32[]{:S(2)}, u32[]{:S(2)}) collective-permute-start(bf16[1,2,2,48,768]{4,3,1,2,0:T(8,128)(2,1)S(1)} %fusion.17), channel_id=1, source_target_pairs={{0,2},{1,3},{2,0},{3,1},{4,6},{5,7},{6,4},{7,5},{8,10},{9,11},{10,... | collective-permute-start | bytes 884744 | tf_op jit(solution)/shard_map/ppermute | solution.py:512
  320.1 4.4 %collective-permute-start.18 = (bf16[1,2,2,32,128]{4,3,1,2,0:T(8,128)(2,1)S(1)}, bf16[1,2,2,32,128]{4,3,1,2,0:T(8,128)(2,1)S(1)}, u32[]{:S(2)}, u32[]{:S(2)}) collective-permute-start(bf16[1,2,2,32,128]{4,3,1,2,0:T(8,128)(2,1)S(1)} %fusion.33), channel_id=1, source_target_pairs={{0,4},{1,5},{2,6},{3,7},{4,0},{5,1},{6,2},{7,3},{8,12},{9,13},{10,... | collective-permute-start | bytes 98312 | tf_op jit(solution)/shard_map/ppermute | solution.py:512
  321.7 7.4 %collective-permute-start.14 = (bf16[1,2,2,48,768]{4,3,1,2,0:T(8,128)(2,1)S(1)}, bf16[1,2,2,48,768]{4,3,1,2,0:T(8,128)(2,1)S(1)}, u32[]{:S(2)}, u32[]{:S(2)}) collective-permute-start(bf16[1,2,2,48,768]{4,3,1,2,0:T(8,128)(2,1)S(1)} %fusion.16), channel_id=1, source_target_pairs={{0,4},{1,5},{2,6},{3,7},{4,0},{5,1},{6,2},{7,3},{8,12},{9,13},{10,... | collective-permute-start | bytes 884744 | tf_op jit(solution)/shard_map/ppermute | solution.py:512
  329.3 7.0 %collective-permute-start.19 = (bf16[1,2,96,768]{3,2,1,0:T(8,128)(2,1)S(1)}, bf16[1,2,96,768]{3,2,1,0:T(8,128)(2,1)S(1)}, u32[]{:S(2)}, u32[]{:S(2)}) collective-permute-start(bf16[1,2,96,768]{3,2,1,0:T(8,128)(2,1)S(1)} %fusion.18), channel_id=1, source_target_pairs={{0,8},{1,9},{2,10},{3,11},{4,12},{5,13},{6,14},{7,15},{8,0},{9,1},... | collective-permute-start | bytes 884744 | tf_op jit(solution)/shard_map/ppermute | solution.py:512
  330.8 5.4 %collective-permute-start.20 = (bf16[1,2,32,128]{3,2,1,0:T(8,128)(2,1)S(1)}, bf16[1,2,32,128]{3,2,1,0:T(8,128)(2,1)S(1)}, u32[]{:S(2)}, u32[]{:S(2)}) collective-permute-start(bf16[1,2,32,128]{3,2,1,0:T(8,128)(2,1)S(1)} %fusion.40), channel_id=1, source_target_pairs={{0,8},{1,9},{2,10},{3,11},{4,12},{5,13},{6,14},{7,15},{8,0},{9,1},... | collective-permute-start | bytes 49160 | tf_op jit(solution)/shard_map/ppermute | solution.py:512
  336.4 5.0 %collective-permute-start.22 = (bf16[1,32,128]{2,1,0:T(8,128)(2,1)S(1)}, bf16[1,32,128]{2,1,0:T(8,128)(2,1)S(1)}, u32[]{:S(2)}, u32[]{:S(2)}) collective-permute-start(bf16[1,32,128]{2,1,0:T(8,128)(2,1)S(1)} %fusion.45), channel_id=1, source_target_pairs={{0,16},{1,17},{2,18},{3,19},{4,20},{5,21},{6,22},{7,23},{8,24},{9,... | collective-permute-start | bytes 24584 | tf_op jit(solution)/shard_map/ppermute | solution.py:512
  339.0 7.7 %collective-permute-start.21 = (bf16[1,96,768]{2,1,0:T(8,128)(2,1)S(1)}, bf16[1,96,768]{2,1,0:T(8,128)(2,1)S(1)}, u32[]{:S(2)}, u32[]{:S(2)}) collective-permute-start(bf16[1,96,768]{2,1,0:T(8,128)(2,1)S(1)} %fusion.19), channel_id=1, source_target_pairs={{0,16},{1,17},{2,18},{3,19},{4,20},{5,21},{6,22},{7,23},{8,24},{9,... | collective-permute-start | bytes 442376 | tf_op jit(solution)/shard_map/ppermute | solution.py:512
  (23 other events, 137.2 us)

commit v3 on v2

--- a/solution.py
+++ b/solution.py
@@ -686,8 +686,9 @@
     acts = tokens
     for at in range(batches):
         if at == 1:
-            acts, raw_arrived, targets = lax.optimization_barrier(
-                (acts, raw_arrived, [(spots[i].T, routes[i]) for i in range(batches)])
+            targets = [(spots[i].T, routes[i]) for i in range(batches)]
+            acts, raw_arrived, targets, place, wr_all, bias_all = lax.optimization_barrier(
+                (acts, raw_arrived, targets, place, wr_all, bias_all)
             )
         front = front_call(
             at, acts, wq, wk, wv, wo, skewed, gain_one, gain_two, spots[at], slots
@@ -768,20 +769,16 @@
             router_pack = jnp.pad(g_router.astype(bf16), ((0, 0), (0, lanes - experts)))
             router_pack = router_pack.reshape(devices, -1, LANES)
             small = jnp.concatenate([router_pack, short_pack], axis=1)
-            small = (small.reshape((1,) + (2,) * bits + small.shape[1:]), list(range(bits))[::-1])
-            for bit in [0] + near:
-                small = scatter_step(small, bit)
+            small = jnp.sum(exchange(small).astype(f32), axis=0)
     held = (jnp.concatenate([low[0], high[0]], axis=-2), low[1])
     for bit in far:
-        value, ahead = lax.optimization_barrier((held[0], small[0]))
-        held = scatter_step((value, held[1]), bit)
-        small = scatter_step((ahead, small[1]), bit)
+        held = scatter_step(held, bit)
     r_query, r_key, r_value, r_output = jnp.split(
         held[0][0], [shard, 2 * shard, 3 * shard], axis=0
     )
     cut = router_pack.shape[1]
-    r_router = small[0][0, :cut].reshape(shard, lanes)[:, :experts]
-    tail = unpack_rows(small[0][:, cut:], [part.shape[1] for part in short])
+    r_router = small[:cut].reshape(shard, lanes)[:, :experts]
+    tail = unpack_rows(small[None, cut:], [part.shape[1] for part in short])
     r_gain_one, r_gain_two, r_rel, r_bias = (
         part.reshape(shape)
         for part, shape in zip(

time: 352 us -> 351 us (level)
  waiting for transfers between devices: 87 us -> 78.7 us
    ppermute x23 -> x18, waiting for transfers between devices: 71.4 us -> 58.5 us  [swap(): lax.ppermute(value, AXES, [(at, at ^ 1 << bit) for at in range(devices)])]
    all_to_all x5 -> x6, waiting for transfers between devices: 15.6 us -> 20.2 us  [exchange(): return lax.all_to_all(buffer, AXES, split_axis=0, concat_axis=0, tiled=True)]
    all_to_all x5 -> x6, starting transfers between devices: 24.6 us -> 28.1 us  [exchange(): return lax.all_to_all(buffer, AXES, split_axis=0, concat_axis=0, tiled=True)]
    ppermute x23 -> x18, starting transfers between devices: 26 us -> 22.8 us  [swap(): lax.ppermute(value, AXES, [(at, at ^ 1 << bit) for at in range(devices)])]
  transfers between devices with their start and end apart: 28 -> 24, of which waited for: 21 -> 16; matrix products, arithmetic and copies ran while one was open for 17% -> 19% of each run, Pallas kernels for 31% -> 31%
where the time goes in v3:
time: 351 us; the launch traced here: 346 us
  Pallas kernels  138 us (39%)
  waiting for transfers between devices  78.7 us (22%)
  starting transfers between devices  50.9 us (15%)
  matrix products  40.9 us (12%)
  local copies, waits for them, and re-layouts  22.2 us (6%)
  other arithmetic  13.1 us (4%)
    ppermute x18, waiting for transfers between devices, swap(): lax.ppermute(value, AXES, [(at, at ^ 1 << bit) for at in range(devices)])  58.5 us
    pallas_call x2, Pallas kernels, expert_call(): pl.pallas_call(functools.partial(expert_kernel, mine_at), grid_spec=pltpu...  47 us
    pallas_call x2, Pallas kernels, back_heads_call(): pl.pallas_call(back_heads_kernel, grid=(groups,), in_specs=[one_in(at, le...  38.4 us
    pallas_call x2, Pallas kernels, front_call(): pl.pallas_call(front_kernel, grid=(groups,), in_specs=[one_in(at, length,...  30.8 us
    all_to_all x6, starting transfers between devices, exchange(): return lax.all_to_all(buffer, AXES, split_axis=0, concat_axis=0, tiled=True)  28.1 us
    ppermute x18, starting transfers between devices, swap(): lax.ppermute(value, AXES, [(at, at ^ 1 << bit) for at in range(devices)])  22.8 us
    all_to_all x6, waiting for transfers between devices, exchange(): return lax.all_to_all(buffer, AXES, split_axis=0, concat_axis=0, tiled=True)  20.2 us
    dot_general x2, matrix products, body(): jnp.einsum('rd,rf->df', rows, grad_inner, preferred_element_type=f32)  19.5 us
  transfers between devices with their start and end apart: 24, of which 16 were waited for; matrix products, arithmetic and copies ran while one was open for 19% of the time, Pallas kernels for 31%

profile of v3, /device:TPU:0, one launch (start us, length us, event | category | flops | bytes accessed | tf_op | source)
XLA Modules:
  0.0 346.5 jit_solution(2892124665597723856)
XLA Ops:
  10.7 5.1 %fusion.1 = bf16[1280,768]{1,0:T(8,128)(2,1)} fusion(bf16[1024,768]{1,0:T(8,128)(2,1)} %bitcast.267, s32[1024]{0:T(1024)S(1)} %pad_add_fusion), kind=kOutput, calls=%fused_computation.6 | convolution fusion | flops 2015559680 | bytes 3543040 | tf_op jit(solution)/shard_map/dot_general | solution.py:640
  20.0 6.1 %collective-permute-done.1 = bf16[2,4,24,768]{3,2,1,0:T(8,128)(2,1)S(1)} collective-permute-done((bf16[2,4,24,768]{3,2,1,0:T(8,128)(2,1)S(1)}, bf16[2,4,24,768]{3,2,1,0:T(8,128)(2,1)S(1)}, u32[]{:S(2)}, u32[]{:S(2)}) %collective-permute-start.1) | collective-permute-done | bytes 294944 | tf_op jit(solution)/shard_map/ppermute | solution.py:512
  42.9 11.4 %collective-permute-done.7 = bf16[2,2,2,48,768]{4,3,0,1,2:T(8,128)(2,1)S(1)} collective-permute-done((bf16[2,2,2,48,768]{4,3,0,1,2:T(8,128)(2,1)S(1)}, bf16[2,2,2,48,768]{4,3,0,1,2:T(8,128)(2,1)S(1)}, u32[]{:S(2)}, u32[]{:S(2)}) %collective-permute-start.7) | collective-permute-done | bytes 589856 | tf_op jit(solution)/shard_map/ppermute | solution.py:512
  54.5 8.0 %collective-permute-done.6 = bf16[2,2,2,56,768]{4,3,0,1,2:T(8,128)(2,1)S(1)} collective-permute-done((bf16[2,2,2,56,768]{4,3,0,1,2:T(8,128)(2,1)S(1)}, bf16[2,2,2,56,768]{4,3,0,1,2:T(8,128)(2,1)S(1)}, u32[]{:S(2)}, u32[]{:S(2)}) %collective-permute-start.6) | collective-permute-done | bytes 688160 | tf_op jit(solution)/shard_map/ppermute | solution.py:512
  77.7 15.5 %front.3 = (bf16[512,768]{1,0:T(8,128)(2,1)}, bf16[512,768]{1,0:T(8,128)(2,1)}, bf16[512,768]{1,0:T(8,128)(2,1)}, bf16[512,768]{1,0:T(8,128)(2,1)}, f32[3,512,4]{2,1,0:T(8,128)}, /*index=5*/bf16[1280,384]{1,0:T(8,128)(2,1)}) custom-call(bf16[2,512,768]{2,1,0:T(8,128)(2,1)} %tokens_ref.10, bf16[768,768]{1,0:T(8,128)(2,1)} %bitcast.209, ...), custom_call_target="tpu_custom_call" | custom-call | flops 1000000 | bytes 262144 | tf_op jit(solution)/shard_map/front/pallas_call | solution.py:117
  93.2 5.4 %all-to-all-start.2 = ((bf16[32,40,384]{2,1,0:T(8,128)(2,1)}), bf16[32,40,384]{2,1,0:T(8,128)(2,1)}, u32[]{:S(2)}, u32[]{:S(2)}) async-start(bf16[32,40,384]{2,1,0:T(8,128)(2,1)} %bitcast.225), calls=%async_computation.2 | async-start | bytes 1966080 | tf_op jit(solution)/shard_map/all_to_all | solution.py:507
  101.8 15.3 %front.2 = (bf16[512,768]{1,0:T(8,128)(2,1)}, bf16[512,768]{1,0:T(8,128)(2,1)}, bf16[512,768]{1,0:T(8,128)(2,1)}, bf16[512,768]{1,0:T(8,128)(2,1)}, f32[3,512,4]{2,1,0:T(8,128)}, /*index=5*/bf16[1280,384]{1,0:T(8,128)(2,1)}) custom-call(bf16[2,512,768]{2,1,0:T(8,128)(2,1)} %tokens_ref.10, bf16[768,768]{1,0:T(8,128)(2,1)} %bitcast.210, ...), custom_call_target="tpu_custom_call" | custom-call | flops 1000000 | bytes 262144 | tf_op jit(solution)/shard_map/front/pallas_call | solution.py:117
  117.2 6.3 %all-to-all-done.2 = bf16[32,40,384]{2,1,0:T(8,128)(2,1)} async-done(((bf16[32,40,384]{2,1,0:T(8,128)(2,1)}), bf16[32,40,384]{2,1,0:T(8,128)(2,1)}, u32[]{:S(2)}, u32[]{:S(2)}) %all-to-all-start.2) | async-done | bytes 983072 | tf_op jit(solution)/shard_map/all_to_all | solution.py:507
  128.1 23.2 %expert.3 = (bf16[1280,768]{1,0:T(8,128)(2,1)}, bf16[640,768]{1,0:T(8,128)(2,1)}, bf16[640,3072]{1,0:T(8,128)(2,1)}, bf16[640,3072]{1,0:T(8,128)(2,1)}, bf16[640,768]{1,0:T(8,128)(2,1)}) custom-call(s32[1]{0:T(128)} %bitcast.44.own_ref, bf16[1280,384]{1,0:T(8,128)(2,1)} %bitcast.59.arrived_ref, bf16[1280,768]{1,0:T(8,128)(2,1)} %bitcast.54.raw_ref, ...), custom_call_target="tpu_custom_call" | custom-call | flops 12079595520 | bytes 20971520 | tf_op jit(solution)/shard_map/expert/pallas_call | solution.py:218
  153.1 5.4 %all-to-all-start.3 = ((bf16[32,40,768]{2,1,0:T(8,128)(2,1)}), bf16[32,40,768]{2,1,0:T(8,128)(2,1)S(1)}, u32[]{:S(2)}, u32[]{:S(2)}) async-start(bf16[32,40,768]{2,1,0:T(8,128)(2,1)} %bitcast.223), calls=%async_computation.3 | async-start | bytes 3932160 | tf_op jit(solution)/shard_map/all_to_all | solution.py:507
  158.5 10.2 %fusion.51 = f32[768,3072]{1,0:T(8,128)} fusion(bf16[640,768]{1,0:T(8,128)(2,1)} %get-tuple-element.121, bf16[640,3072]{1,0:T(8,128)(2,1)} %get-tuple-element.122), kind=kOutput, calls=%fused_computation.161 | convolution fusion | flops 3019898880 | bytes 14352384 | tf_op jit(solution)/shard_map/rd,rf->df/dot_general | solution.py:713
  168.7 6.4 %fusion.52 = f32[3072,768]{1,0:T(8,128)} fusion(bf16[640,3072]{1,0:T(8,128)(2,1)S(1)} %copy-done.18, bf16[640,768]{1,0:T(8,128)(2,1)S(1)} %copy-done.19), kind=kOutput, calls=%fused_computation.162 | convolution fusion | flops 3019898880 | bytes 14352384 | tf_op jit(solution)/shard_map/rf,rd->fd/dot_general | solution.py:714
  175.1 23.7 %expert.2 = (bf16[1280,768]{1,0:T(8,128)(2,1)}, bf16[640,768]{1,0:T(8,128)(2,1)}, bf16[640,3072]{1,0:T(8,128)(2,1)}, bf16[640,3072]{1,0:T(8,128)(2,1)}, bf16[640,768]{1,0:T(8,128)(2,1)}) custom-call(s32[1]{0:T(128)} %bitcast.44.own_ref, bf16[1280,384]{1,0:T(8,128)(2,1)} %bitcast.226, bf16[1280,768]{1,0:T(8,128)(2,1)} %bitcast.54.raw_ref, ...), custom_call_target="tpu_custom_call" | custom-call | flops 12079595520 | bytes 20971520 | tf_op jit(solution)/shard_map/expert/pallas_call | solution.py:218
  198.8 5.7 %all-to-all-done.3 = bf16[32,40,768]{2,1,0:T(8,128)(2,1)S(1)} async-done(((bf16[32,40,768]{2,1,0:T(8,128)(2,1)}), bf16[32,40,768]{2,1,0:T(8,128)(2,1)S(1)}, u32[]{:S(2)}, u32[]{:S(2)}) %all-to-all-start.3) | async-done | bytes 1966112 | tf_op jit(solution)/shard_map/all_to_all | solution.py:507
  211.9 9.2 %back_rows.2 = (bf16[2,512,768]{2,1,0:T(8,128)(2,1)}, f32[512,768]{1,0:T(8,128)}, bf16[512,768]{1,0:T(8,128)(2,1)}, bf16[768,768]{1,0:T(8,128)(2,1)}, f32[768,32...) custom-call(s32[512,2]{1,0:T(8,128)} %bitcast.230, s32[512,1]{1,0:T(8,128)} %copy.114.route_ref, ...), custom_call_target="tpu_custom_call" | custom-call | flops 3825205248 | bytes 12582912 | tf_op jit(solution)/shard_map/back_rows/pallas_call | solution.py:304
  221.1 18.9 %back_heads.2 = (f32[3,4,1024]{2,1,0:T(4,128)}, bf16[3,768,768]{2,1,0:T(8,128)(2,1)}, bf16[2,512,768]{2,1,0:T(8,128)(2,1)}, f32[1,768]{1,0:T(1,128)}) custom-call(bf16[2,512,768]{2,1,0:T(8,128)(2,1)} %tokens_ref.10, f32[1,768]{1,0:T(1,128)} %reshape.703.gain_one_ref.gain_ref, bf16[512,768]{1,0:T(8,128)(2,1)} %get-tuple-element.152.gradmixed_ref, ...), custom_call_target="tpu_custom_call" | custom-call | flops 10066329600 | bytes 22020096 | tf_op jit(solution)/shard_map/back_heads/pallas_call | solution.py:434
  240.0 9.3 %convolution_add_fusion.1 = f32[768,3072]{1,0:T(8,128)} fusion(f32[768,3072]{1,0:T(8,128)} %fusion.51, bf16[640,768]{1,0:T(8,128)(2,1)} %get-tuple-element.129, bf16[640,3072]{1,0:T(8,128)(2,1)S(1)} %copy-done.2), kind=kOutput, calls=%fused_computation.3 | convolution fusion | flops 3022258176 | bytes 23789568 | tf_op jit(solution)/shard_map/rd,rf->df/dot_general | solution.py:713
  249.3 8.7 %convolution_add_fusion = f32[3072,768]{1,0:T(8,128)} fusion(f32[3072,768]{1,0:T(8,128)} %fusion.52, bf16[640,3072]{1,0:T(8,128)(2,1)S(1)} %copy-done.1, bf16[640,768]{1,0:T(8,128)(2,1)S(1)} %copy-done.5), kind=kOutput, calls=%fused_computation.2 | convolution fusion | flops 3022258176 | bytes 23789568 | tf_op jit(solution)/shard_map/rf,rd->fd/dot_general | solution.py:714
  258.0 9.9 %back_rows.3 = (bf16[2,512,768]{2,1,0:T(8,128)(2,1)}, f32[512,768]{1,0:T(8,128)}, bf16[512,768]{1,0:T(8,128)(2,1)}, bf16[768,768]{1,0:T(8,128)(2,1)}, f32[768,32...) custom-call(s32[512,2]{1,0:T(8,128)} %bitcast.229, ...), custom_call_target="tpu_custom_call", output_to_operand_aliasing={{0}: (14, {})} | custom-call | flops 3825205248 | bytes 12582912 | tf_op jit(solution)/shard_map/back_rows/pallas_call | solution.py:304
  267.9 19.5 %back_heads.3 = (f32[3,4,1024]{2,1,0:T(4,128)}, bf16[3,768,768]{2,1,0:T(8,128)(2,1)}, bf16[2,512,768]{2,1,0:T(8,128)(2,1)}, f32[1,768]{1,0:T(1,128)}) custom-call(bf16[2,512,768]{2,1,0:T(8,128)(2,1)} %tokens_ref.10, f32[1,768]{1,0:T(1,128)} %reshape.703.gain_one_ref.gain_ref, ...), custom_call_target="tpu_custom_call", output_to_operand_aliasing={{2}: (16, {})} | custom-call | flops 10066329600 | bytes 22020096 | tf_op jit(solution)/shard_map/back_heads/pallas_call | solution.py:434
  298.8 11.8 %collective-permute-done.11 = bf16[1,2,2,2,48,768]{5,4,1,2,3,0:T(8,128)(2,1)S(1)} collective-permute-done((bf16[1,2,2,2,48,768]{5,4,1,2,3,0:T(8,128)(2,1)S(1)}, bf16[1,2,2,2,48,768]{5,4,1,2,3,0:T(8,128)(2,1)S(1)}, u32[]{:S(2)}, u32[]{:S(2)}) %collective-permute-start.11) | collective-permute-done | bytes 589856 | tf_op jit(solution)/shard_map/ppermute | solution.py:512
  317.8 4.6 %all-to-all-start.5 = ((bf16[32,32,128]{2,1,0:T(8,128)(2,1)}), bf16[32,32,128]{2,1,0:T(8,128)(2,1)S(1)}, u32[]{:S(2)}, u32[]{:S(2)}) async-start(bf16[32,32,128]{2,1,0:T(8,128)(2,1)} %pad_maximum_fusion.13), calls=%async_computation.5 | async-start | bytes 524288 | tf_op jit(solution)/shard_map/all_to_all | solution.py:507
  325.5 7.4 %all-to-all-done.5 = bf16[32,32,128]{2,1,0:T(8,128)(2,1)S(1)} async-done(((bf16[32,32,128]{2,1,0:T(8,128)(2,1)}), bf16[32,32,128]{2,1,0:T(8,128)(2,1)S(1)}, u32[]{:S(2)}, u32[]{:S(2)}) %all-to-all-start.5) | async-done | bytes 262176 | tf_op jit(solution)/shard_map/all_to_all | solution.py:507
  339.0 6.4 %collective-permute-done.17 = bf16[1,96,768]{2,1,0:T(8,128)(2,1)S(1)} collective-permute-done((bf16[1,96,768]{2,1,0:T(8,128)(2,1)S(1)}, bf16[1,96,768]{2,1,0:T(8,128)(2,1)S(1)}, u32[]{:S(2)}, u32[]{:S(2)}) %collective-permute-start.17) | collective-permute-done | bytes 147488 | tf_op jit(solution)/shard_map/ppermute | solution.py:512
  (177 shorter events, 90.8 us)
Async XLA Ops:
  2.1 15.7 %collective-permute-start = (bf16[4,24,768]{2,1,0:T(8,128)(2,1)}, bf16[4,24,768]{2,1,0:T(8,128)(2,1)S(1)}, u32[]{:S(2)}, u32[]{:S(2)}) collective-permute-start(bf16[4,24,768]{2,1,0:T(8,128)(2,1)} %pack.1), channel_id=1, source_target_pairs={{0,16},{1,17},{2,18},{3,19},{4,20},{5,21},{6,22},{7,23},{8,24},{9,... | collective-permute-start | bytes 442376 | tf_op jit(solution)/shard_map/ppermute | solution.py:512
  8.3 7.5 %collective-permute-start.2 = (bf16[8,768]{1,0:T(8,128)(2,1)S(1)}, bf16[8,768]{1,0:T(8,128)(2,1)S(1)}, u32[]{:S(2)}, u32[]{:S(2)}) collective-permute-start(bf16[8,768]{1,0:T(8,128)(2,1)S(1)} %fusion.41), channel_id=1, source_target_pairs={{0,16},{1,17},{2,18},{3,19},{4,20},{5,21},{6,22},{7,23},{8,24},{9,... | collective-permute-start | bytes 36872 | tf_op jit(solution)/shard_map/ppermute | solution.py:512
  15.9 4.1 %collective-permute-start.3 = (bf16[2,8,768]{2,1,0:T(8,128)(2,1)S(1)}, bf16[2,8,768]{2,1,0:T(8,128)(2,1)S(1)}, u32[]{:S(2)}, u32[]{:S(2)}) collective-permute-start(bf16[2,8,768]{2,1,0:T(8,128)(2,1)S(1)} %pad_maximum_fusion.16), channel_id=1, source_target_pairs={{0,8},{1,9},{2,10},{3,11},{4,12},{5,13},{6,14},{7,15},{8,0},{9,1},... | collective-permute-start | bytes 73736 | tf_op jit(solution)/shard_map/ppermute | solution.py:512
  17.9 8.2 %collective-permute-start.1 = (bf16[2,4,24,768]{3,2,1,0:T(8,128)(2,1)S(1)}, bf16[2,4,24,768]{3,2,1,0:T(8,128)(2,1)S(1)}, u32[]{:S(2)}, u32[]{:S(2)}) collective-permute-start(bf16[2,4,24,768]{3,2,1,0:T(8,128)(2,1)S(1)} %pad_maximum_fusion.11), channel_id=1, source_target_pairs={{0,8},{1,9},{2,10},{3,11},{4,12},{5,13},{6,14},{7,15},{8,0},{9,1},... | collective-permute-start | bytes 884744 | tf_op jit(solution)/shard_map/ppermute | solution.py:512
  26.3 7.3 %collective-permute-start.5 = (bf16[2,2,48,768]{3,2,0,1:T(8,128)(2,1)S(1)}, bf16[2,2,48,768]{3,2,0,1:T(8,128)(2,1)S(1)}, u32[]{:S(2)}, u32[]{:S(2)}) collective-permute-start(bf16[2,2,48,768]{3,2,0,1:T(8,128)(2,1)S(1)} %pad_maximum_fusion.12), channel_id=1, source_target_pairs={{0,2},{1,3},{2,0},{3,1},{4,6},{5,7},{6,4},{7,5},{8,10},{9,11},{10,... | collective-permute-start | bytes 884744 | tf_op jit(solution)/shard_map/ppermute | solution.py:512
  27.9 8.1 %collective-permute-start.4 = (bf16[2,2,56,768]{3,2,0,1:T(8,128)(2,1)S(1)}, bf16[2,2,56,768]{3,2,0,1:T(8,128)(2,1)S(1)}, u32[]{:S(2)}, u32[]{:S(2)}) collective-permute-start(bf16[2,2,56,768]{3,2,0,1:T(8,128)(2,1)S(1)} %pad_maximum_fusion.10), channel_id=1, source_target_pairs={{0,4},{1,5},{2,6},{3,7},{4,0},{5,1},{6,2},{7,3},{8,12},{9,13},{10,... | collective-permute-start | bytes 1032200 | tf_op jit(solution)/shard_map/ppermute | solution.py:512
  36.3 18.0 %collective-permute-start.7 = (bf16[2,2,2,48,768]{4,3,0,1,2:T(8,128)(2,1)S(1)}, bf16[2,2,2,48,768]{4,3,0,1,2:T(8,128)(2,1)S(1)}, u32[]{:S(2)}, u32[]{:S(2)}) collective-permute-start(bf16[2,2,2,48,768]{4,3,0,1,2:T(8,128)(2,1)S(1)} %pad_maximum_fusion.9), channel_id=1, source_target_pairs={{0,4},{1,5},{2,6},{3,7},{4,0},{5,1},{6,2},{7,3},{8,12},{9,13},{10,... | collective-permute-start | bytes 1769480 | tf_op jit(solution)/shard_map/ppermute | solution.py:512
  37.8 24.6 %collective-permute-start.6 = (bf16[2,2,2,56,768]{4,3,0,1,2:T(8,128)(2,1)S(1)}, bf16[2,2,2,56,768]{4,3,0,1,2:T(8,128)(2,1)S(1)}, u32[]{:S(2)}, u32[]{:S(2)}) collective-permute-start(bf16[2,2,2,56,768]{4,3,0,1,2:T(8,128)(2,1)S(1)} %pad_maximum_fusion.6), channel_id=1, source_target_pairs={{0,2},{1,3},{2,0},{3,1},{4,6},{5,7},{6,4},{7,5},{8,10},{9,11},{10,... | collective-permute-start | bytes 2064392 | tf_op jit(solution)/shard_map/ppermute | solution.py:512
  38.4 54.8 %all-to-all-start = ((bf16[32,40,768]{2,1,0:T(8,128)(2,1)}), bf16[32,40,768]{2,1,0:T(8,128)(2,1)}, u32[]{:S(2)}, u32[]{:S(2)}) async-start(bf16[32,40,768]{2,1,0:T(8,128)(2,1)} %bitcast.27), calls=%async_computation | async-start | bytes 3932160 | tf_op jit(solution)/shard_map/all_to_all | solution.py:507
  62.7 3.0 collective-permute-start.9
  62.8 6.4 %collective-permute-start.8 = (bf16[2,2,2,2,56,768]{5,4,0,1,2,3:T(8,128)(2,1)S(1)}, bf16[2,2,2,2,56,768]{5,4,0,1,2,3:T(8,128)(2,1)}, u32[]{:S(2)}, u32[]{:S(2)}) collective-permute-start(bf16[2,2,2,2,56,768]{5,4,0,1,2,3:T(8,128)(2,1)S(1)} %pad_maximum_fusion.3), channel_id=1, source_target_pairs={{0,1},{1,0},{2,3},{3,2},{4,5},{5,4},{6,7},{7,6},{8,9},{9,8},{10,11... | collective-permute-start | bytes 4128776 | tf_op jit(solution)/shard_map/ppermute | solution.py:512
  93.2 30.3 %all-to-all-start.2 = ((bf16[32,40,384]{2,1,0:T(8,128)(2,1)}), bf16[32,40,384]{2,1,0:T(8,128)(2,1)}, u32[]{:S(2)}, u32[]{:S(2)}) async-start(bf16[32,40,384]{2,1,0:T(8,128)(2,1)} %bitcast.225), calls=%async_computation.2 | async-start | bytes 1966080 | tf_op jit(solution)/shard_map/all_to_all | solution.py:507
  123.5 28.7 %all-to-all-start.1 = ((bf16[32,40,384]{2,1,0:T(8,128)(2,1)}), bf16[32,40,384]{2,1,0:T(8,128)(2,1)S(1)}, u32[]{:S(2)}, u32[]{:S(2)}) async-start(bf16[32,40,384]{2,1,0:T(8,128)(2,1)} %bitcast.227), calls=%async_computation.1 | async-start | bytes 1966080 | tf_op jit(solution)/shard_map/all_to_all | solution.py:507
  153.1 51.4 %all-to-all-start.3 = ((bf16[32,40,768]{2,1,0:T(8,128)(2,1)}), bf16[32,40,768]{2,1,0:T(8,128)(2,1)S(1)}, u32[]{:S(2)}, u32[]{:S(2)}) async-start(bf16[32,40,768]{2,1,0:T(8,128)(2,1)} %bitcast.223), calls=%async_computation.3 | async-start | bytes 3932160 | tf_op jit(solution)/shard_map/all_to_all | solution.py:507
  205.8 52.2 %all-to-all-start.4 = ((bf16[32,40,768]{2,1,0:T(8,128)(2,1)}), bf16[32,40,768]{2,1,0:T(8,128)(2,1)}, u32[]{:S(2)}, u32[]{:S(2)}) async-start(bf16[32,40,768]{2,1,0:T(8,128)(2,1)} %bitcast.221), calls=%async_computation.4 | async-start | bytes 3932160 | tf_op jit(solution)/shard_map/all_to_all | solution.py:507
  290.4 3.8 %collective-permute-start.10 = (bf16[1,2,2,2,2,72,768]{6,5,1,2,4,3,0:T(8,128)(2,1)S(1)}, bf16[1,2,2,2,2,72,768]{6,5,1,2,4,3,0:T(8,128)(2,1)S(1)}, u32[]{:S(2)}, u32[]{:S(2)}) collective-permute-start(bf16[1,2,2,2,2,72,768]{6,5,1,2,4,3,0:T(8,128)(2,1)S(1)} %select_bitcast_fusion), channel_id=1, source_target_pairs={{0,1},{1,0},{2,3},{3,2},{4,5},{5,4},{6,7},{7,6},{8,9},{9,8},{10,11... | collective-permute-start | bytes 5308424 | tf_op jit(solution)/shard_map/ppermute | solution.py:512
  291.7 5.1 %collective-permute-start.12 = (bf16[1,2,2,2,2,24,768]{6,5,1,2,4,3,0:T(8,128)(2,1)S(1)}, bf16[1,2,2,2,2,24,768]{6,5,1,2,4,3,0:T(8,128)(2,1)S(1)}, u32[]{:S(2)}, u32[]{:S(2)}) collective-permute-start(bf16[1,2,2,2,2,24,768]{6,5,1,2,4,3,0:T(8,128)(2,1)S(1)} %select_bitcast_fusion.7), channel_id=1, source_target_pairs={{0,1},{1,0},{2,3},{3,2},{4,5},{5,4},{6,7},{7,6},{8,9},{9,8},{10,11... | collective-permute-start | bytes 1769480 | tf_op jit(solution)/shard_map/ppermute | solution.py:512
  294.9 15.7 %collective-permute-start.11 = (bf16[1,2,2,2,48,768]{5,4,1,2,3,0:T(8,128)(2,1)S(1)}, bf16[1,2,2,2,48,768]{5,4,1,2,3,0:T(8,128)(2,1)S(1)}, u32[]{:S(2)}, u32[]{:S(2)}) collective-permute-start(bf16[1,2,2,2,48,768]{5,4,1,2,3,0:T(8,128)(2,1)S(1)} %fusion.10), channel_id=1, source_target_pairs={{0,2},{1,3},{2,0},{3,1},{4,6},{5,7},{6,4},{7,5},{8,10},{9,11},{10,... | collective-permute-start | bytes 1769480 | tf_op jit(solution)/shard_map/ppermute | solution.py:512
  297.2 15.2 %collective-permute-start.13 = (bf16[1,2,2,2,48,768]{5,4,1,2,3,0:T(8,128)(2,1)S(1)}, bf16[1,2,2,2,48,768]{5,4,1,2,3,0:T(8,128)(2,1)S(1)}, u32[]{:S(2)}, u32[]{:S(2)}) collective-permute-start(bf16[1,2,2,2,48,768]{5,4,1,2,3,0:T(8,128)(2,1)S(1)} %fusion.11), channel_id=1, source_target_pairs={{0,4},{1,5},{2,6},{3,7},{4,0},{5,1},{6,2},{7,3},{8,12},{9,13},{10,... | collective-permute-start | bytes 1769480 | tf_op jit(solution)/shard_map/ppermute | solution.py:512
  313.4 9.1 %collective-permute-start.15 = (bf16[1,2,2,48,768]{4,3,1,2,0:T(8,128)(2,1)}, bf16[1,2,2,48,768]{4,3,1,2,0:T(8,128)(2,1)}, u32[]{:S(2)}, u32[]{:S(2)}) collective-permute-start(bf16[1,2,2,48,768]{4,3,1,2,0:T(8,128)(2,1)} %fusion.18), channel_id=1, source_target_pairs={{0,2},{1,3},{2,0},{3,1},{4,6},{5,7},{6,4},{7,5},{8,10},{9,11},{10,... | collective-permute-start | bytes 884744 | tf_op jit(solution)/shard_map/ppermute | solution.py:512
  314.5 9.0 %collective-permute-start.14 = (bf16[1,2,2,48,768]{4,3,1,2,0:T(8,128)(2,1)}, bf16[1,2,2,48,768]{4,3,1,2,0:T(8,128)(2,1)S(1)}, u32[]{:S(2)}, u32[]{:S(2)}) collective-permute-start(bf16[1,2,2,48,768]{4,3,1,2,0:T(8,128)(2,1)} %fusion.17), channel_id=1, source_target_pairs={{0,4},{1,5},{2,6},{3,7},{4,0},{5,1},{6,2},{7,3},{8,12},{9,13},{10,... | collective-permute-start | bytes 884744 | tf_op jit(solution)/shard_map/ppermute | solution.py:512
  317.8 15.1 %all-to-all-start.5 = ((bf16[32,32,128]{2,1,0:T(8,128)(2,1)}), bf16[32,32,128]{2,1,0:T(8,128)(2,1)S(1)}, u32[]{:S(2)}, u32[]{:S(2)}) async-start(bf16[32,32,128]{2,1,0:T(8,128)(2,1)} %pad_maximum_fusion.13), calls=%async_computation.5 | async-start | bytes 524288 | tf_op jit(solution)/shard_map/all_to_all | solution.py:507
  323.7 12.2 %collective-permute-start.16 = (bf16[1,2,96,768]{3,2,1,0:T(8,128)(2,1)S(1)}, bf16[1,2,96,768]{3,2,1,0:T(8,128)(2,1)S(1)}, u32[]{:S(2)}, u32[]{:S(2)}) collective-permute-start(bf16[1,2,96,768]{3,2,1,0:T(8,128)(2,1)S(1)} %fusion.19), channel_id=1, source_target_pairs={{0,8},{1,9},{2,10},{3,11},{4,12},{5,13},{6,14},{7,15},{8,0},{9,1},... | collective-permute-start | bytes 884744 | tf_op jit(solution)/shard_map/ppermute | solution.py:512
  336.0 9.5 %collective-permute-start.17 = (bf16[1,96,768]{2,1,0:T(8,128)(2,1)S(1)}, bf16[1,96,768]{2,1,0:T(8,128)(2,1)S(1)}, u32[]{:S(2)}, u32[]{:S(2)}) collective-permute-start(bf16[1,96,768]{2,1,0:T(8,128)(2,1)S(1)} %fusion.20), channel_id=1, source_target_pairs={{0,16},{1,17},{2,18},{3,19},{4,20},{5,21},{6,22},{7,23},{8,24},{9,... | collective-permute-start | bytes 442376 | tf_op jit(solution)/shard_map/ppermute | solution.py:512
  (20 other events, 142.7 us)

commit v4 on v3

--- a/solution.py
+++ b/solution.py
@@ -534,14 +534,18 @@
     return held[0].reshape((-1,) + value.shape)
 
 
-def scatter_step(held, bit):
-    value, left = held
+def halves(value, left, bit):
     place = 1 + left.index(bit)
     low = lax.index_in_dim(value, 0, place, keepdims=False)
     high = lax.index_in_dim(value, 1, place, keepdims=False)
     upper = own_bit(bit)
-    sent = jnp.where(upper, low, high).astype(bf16)
-    value = jnp.where(upper, high, low).astype(f32) + swap(sent, bit).astype(f32)
+    return jnp.where(upper, low, high).astype(bf16), jnp.where(upper, high, low).astype(f32)
+
+
+def scatter_step(held, bit):
+    value, left = held
+    sent, kept = halves(value, left, bit)
+    value = kept + swap(sent, bit).astype(f32)
     return value, [other for other in left if other != bit]
 
 
@@ -769,12 +773,18 @@
             router_pack = jnp.pad(g_router.astype(bf16), ((0, 0), (0, lanes - experts)))
             router_pack = router_pack.reshape(devices, -1, LANES)
             small = jnp.concatenate([router_pack, short_pack], axis=1)
-            small = jnp.sum(exchange(small).astype(f32), axis=0)
+            small = exchange(small)
     held = (jnp.concatenate([low[0], high[0]], axis=-2), low[1])
-    for bit in far:
+    for bit in far[:-1]:
         held = scatter_step(held, bit)
+    value, left = held
+    sent, value = halves(value, left, far[-1])
+    theirs = swap(sent, far[-1])
+    theirs, small = lax.optimization_barrier((theirs, small))
+    total = (value + theirs.astype(f32))[0]
+    small = jnp.sum(small.astype(f32), axis=0)
     r_query, r_key, r_value, r_output = jnp.split(
-        held[0][0], [shard, 2 * shard, 3 * shard], axis=0
+        total, [shard, 2 * shard, 3 * shard], axis=0
     )
     cut = router_pack.shape[1]
     r_router = small[:cut].reshape(shard, lanes)[:, :experts]

time: 351 us -> 354 us (level)
  waiting for transfers between devices: 78.7 us -> 82.4 us
    all_to_all x6, waiting for transfers between devices: 20.2 us -> 23.9 us  [exchange(): return lax.all_to_all(buffer, AXES, split_axis=0, concat_axis=0, tiled=True)]
  transfers between devices with their start and end apart: 24 -> 24, of which waited for: 16 -> 17; matrix products, arithmetic and copies ran while one was open for 19% -> 18% of each run, Pallas kernels for 31% -> 31%
where the time goes in v4:
time: 354 us; the launch traced here: 350 us
  Pallas kernels  138 us (39%)
  waiting for transfers between devices  82.4 us (23%)
  starting transfers between devices  50.9 us (14%)
  matrix products  40.9 us (12%)
  local copies, waits for them, and re-layouts  22.2 us (6%)
  other arithmetic  12.4 us (4%)
    ppermute x18, waiting for transfers between devices, swap(): lax.ppermute(value, AXES, [(at, at ^ 1 << bit) for at in range(devices)])  58.6 us
    pallas_call x2, Pallas kernels, expert_call(): pl.pallas_call(functools.partial(expert_kernel, mine_at), grid_spec=pltpu...  47 us
    pallas_call x2, Pallas kernels, back_heads_call(): pl.pallas_call(back_heads_kernel, grid=(groups,), in_specs=[one_in(at, le...  38.4 us
    pallas_call x2, Pallas kernels, front_call(): pl.pallas_call(front_kernel, grid=(groups,), in_specs=[one_in(at, length,...  30.8 us
    all_to_all x6, starting transfers between devices, exchange(): return lax.all_to_all(buffer, AXES, split_axis=0, concat_axis=0, tiled=True)  28.1 us
    all_to_all x6, waiting for transfers between devices, exchange(): return lax.all_to_all(buffer, AXES, split_axis=0, concat_axis=0, tiled=True)  23.9 us
    ppermute x18, starting transfers between devices, swap(): lax.ppermute(value, AXES, [(at, at ^ 1 << bit) for at in range(devices)])  22.8 us
    dot_general x2, matrix products, body(): jnp.einsum('rd,rf->df', rows, grad_inner, preferred_element_type=f32)  19.5 us
  transfers between devices with their start and end apart: 24, of which 17 were waited for; matrix products, arithmetic and copies ran while one was open for 18% of the time, Pallas kernels for 31%

profile of v4, /device:TPU:0, one launch (start us, length us, event | category | flops | bytes accessed | tf_op | source)
XLA Modules:
  0.0 349.5 jit_solution(2607493718753024324)
XLA Ops:
  10.7 5.1 %fusion.1 = bf16[1280,768]{1,0:T(8,128)(2,1)} fusion(bf16[1024,768]{1,0:T(8,128)(2,1)} %bitcast.267, s32[1024]{0:T(1024)S(1)} %pad_add_fusion), kind=kOutput, calls=%fused_computation.6 | convolution fusion | flops 2015559680 | bytes 3543040 | tf_op jit(solution)/shard_map/dot_general | solution.py:644
  20.0 6.1 %collective-permute-done.1 = bf16[2,4,24,768]{3,2,1,0:T(8,128)(2,1)S(1)} collective-permute-done((bf16[2,4,24,768]{3,2,1,0:T(8,128)(2,1)S(1)}, bf16[2,4,24,768]{3,2,1,0:T(8,128)(2,1)S(1)}, u32[]{:S(2)}, u32[]{:S(2)}) %collective-permute-start.1) | collective-permute-done | bytes 294944 | tf_op jit(solution)/shard_map/ppermute | solution.py:512
  42.9 11.4 %collective-permute-done.7 = bf16[2,2,2,48,768]{4,3,0,1,2:T(8,128)(2,1)S(1)} collective-permute-done((bf16[2,2,2,48,768]{4,3,0,1,2:T(8,128)(2,1)S(1)}, bf16[2,2,2,48,768]{4,3,0,1,2:T(8,128)(2,1)S(1)}, u32[]{:S(2)}, u32[]{:S(2)}) %collective-permute-start.7) | collective-permute-done | bytes 589856 | tf_op jit(solution)/shard_map/ppermute | solution.py:512
  54.5 8.0 %collective-permute-done.6 = bf16[2,2,2,56,768]{4,3,0,1,2:T(8,128)(2,1)S(1)} collective-permute-done((bf16[2,2,2,56,768]{4,3,0,1,2:T(8,128)(2,1)S(1)}, bf16[2,2,2,56,768]{4,3,0,1,2:T(8,128)(2,1)S(1)}, u32[]{:S(2)}, u32[]{:S(2)}) %collective-permute-start.6) | collective-permute-done | bytes 688160 | tf_op jit(solution)/shard_map/ppermute | solution.py:512
  77.7 15.5 %front.3 = (bf16[512,768]{1,0:T(8,128)(2,1)}, bf16[512,768]{1,0:T(8,128)(2,1)}, bf16[512,768]{1,0:T(8,128)(2,1)}, bf16[512,768]{1,0:T(8,128)(2,1)}, f32[3,512,4]{2,1,0:T(8,128)}, /*index=5*/bf16[1280,384]{1,0:T(8,128)(2,1)}) custom-call(bf16[2,512,768]{2,1,0:T(8,128)(2,1)} %tokens_ref.10, bf16[768,768]{1,0:T(8,128)(2,1)} %bitcast.209, ...), custom_call_target="tpu_custom_call" | custom-call | flops 1000000 | bytes 262144 | tf_op jit(solution)/shard_map/front/pallas_call | solution.py:117
  93.2 5.4 %all-to-all-start.2 = ((bf16[32,40,384]{2,1,0:T(8,128)(2,1)}), bf16[32,40,384]{2,1,0:T(8,128)(2,1)}, u32[]{:S(2)}, u32[]{:S(2)}) async-start(bf16[32,40,384]{2,1,0:T(8,128)(2,1)} %bitcast.225), calls=%async_computation.2 | async-start | bytes 1966080 | tf_op jit(solution)/shard_map/all_to_all | solution.py:507
  101.8 15.3 %front.2 = (bf16[512,768]{1,0:T(8,128)(2,1)}, bf16[512,768]{1,0:T(8,128)(2,1)}, bf16[512,768]{1,0:T(8,128)(2,1)}, bf16[512,768]{1,0:T(8,128)(2,1)}, f32[3,512,4]{2,1,0:T(8,128)}, /*index=5*/bf16[1280,384]{1,0:T(8,128)(2,1)}) custom-call(bf16[2,512,768]{2,1,0:T(8,128)(2,1)} %tokens_ref.10, bf16[768,768]{1,0:T(8,128)(2,1)} %bitcast.210, ...), custom_call_target="tpu_custom_call" | custom-call | flops 1000000 | bytes 262144 | tf_op jit(solution)/shard_map/front/pallas_call | solution.py:117
  117.2 6.3 %all-to-all-done.2 = bf16[32,40,384]{2,1,0:T(8,128)(2,1)} async-done(((bf16[32,40,384]{2,1,0:T(8,128)(2,1)}), bf16[32,40,384]{2,1,0:T(8,128)(2,1)}, u32[]{:S(2)}, u32[]{:S(2)}) %all-to-all-start.2) | async-done | bytes 983072 | tf_op jit(solution)/shard_map/all_to_all | solution.py:507
  128.1 23.2 %expert.3 = (bf16[1280,768]{1,0:T(8,128)(2,1)}, bf16[640,768]{1,0:T(8,128)(2,1)}, bf16[640,3072]{1,0:T(8,128)(2,1)}, bf16[640,3072]{1,0:T(8,128)(2,1)}, bf16[640,768]{1,0:T(8,128)(2,1)}) custom-call(s32[1]{0:T(128)} %bitcast.44.own_ref, bf16[1280,384]{1,0:T(8,128)(2,1)} %bitcast.59.arrived_ref, bf16[1280,768]{1,0:T(8,128)(2,1)} %bitcast.54.raw_ref, ...), custom_call_target="tpu_custom_call" | custom-call | flops 12079595520 | bytes 20971520 | tf_op jit(solution)/shard_map/expert/pallas_call | solution.py:218
  153.1 5.4 %all-to-all-start.3 = ((bf16[32,40,768]{2,1,0:T(8,128)(2,1)}), bf16[32,40,768]{2,1,0:T(8,128)(2,1)S(1)}, u32[]{:S(2)}, u32[]{:S(2)}) async-start(bf16[32,40,768]{2,1,0:T(8,128)(2,1)} %bitcast.223), calls=%async_computation.3 | async-start | bytes 3932160 | tf_op jit(solution)/shard_map/all_to_all | solution.py:507
  158.5 10.2 %fusion.51 = f32[768,3072]{1,0:T(8,128)} fusion(bf16[640,768]{1,0:T(8,128)(2,1)} %get-tuple-element.123, bf16[640,3072]{1,0:T(8,128)(2,1)} %get-tuple-element.124), kind=kOutput, calls=%fused_computation.161 | convolution fusion | flops 3019898880 | bytes 14352384 | tf_op jit(solution)/shard_map/rd,rf->df/dot_general | solution.py:717
  168.7 6.4 %fusion.52 = f32[3072,768]{1,0:T(8,128)} fusion(bf16[640,3072]{1,0:T(8,128)(2,1)S(1)} %copy-done.18, bf16[640,768]{1,0:T(8,128)(2,1)S(1)} %copy-done.19), kind=kOutput, calls=%fused_computation.162 | convolution fusion | flops 3019898880 | bytes 14352384 | tf_op jit(solution)/shard_map/rf,rd->fd/dot_general | solution.py:718
  175.1 23.7 %expert.2 = (bf16[1280,768]{1,0:T(8,128)(2,1)}, bf16[640,768]{1,0:T(8,128)(2,1)}, bf16[640,3072]{1,0:T(8,128)(2,1)}, bf16[640,3072]{1,0:T(8,128)(2,1)}, bf16[640,768]{1,0:T(8,128)(2,1)}) custom-call(s32[1]{0:T(128)} %bitcast.44.own_ref, bf16[1280,384]{1,0:T(8,128)(2,1)} %bitcast.226, bf16[1280,768]{1,0:T(8,128)(2,1)} %bitcast.54.raw_ref, ...), custom_call_target="tpu_custom_call" | custom-call | flops 12079595520 | bytes 20971520 | tf_op jit(solution)/shard_map/expert/pallas_call | solution.py:218
  198.8 5.7 %all-to-all-done.3 = bf16[32,40,768]{2,1,0:T(8,128)(2,1)S(1)} async-done(((bf16[32,40,768]{2,1,0:T(8,128)(2,1)}), bf16[32,40,768]{2,1,0:T(8,128)(2,1)S(1)}, u32[]{:S(2)}, u32[]{:S(2)}) %all-to-all-start.3) | async-done | bytes 1966112 | tf_op jit(solution)/shard_map/all_to_all | solution.py:507
  211.9 9.2 %back_rows.2 = (bf16[2,512,768]{2,1,0:T(8,128)(2,1)}, f32[512,768]{1,0:T(8,128)}, bf16[512,768]{1,0:T(8,128)(2,1)}, bf16[768,768]{1,0:T(8,128)(2,1)}, f32[768,32...) custom-call(s32[512,2]{1,0:T(8,128)} %bitcast.230, s32[512,1]{1,0:T(8,128)} %copy.114.route_ref, ...), custom_call_target="tpu_custom_call" | custom-call | flops 3825205248 | bytes 12582912 | tf_op jit(solution)/shard_map/back_rows/pallas_call | solution.py:304
  221.1 18.9 %back_heads.2 = (f32[3,4,1024]{2,1,0:T(4,128)}, bf16[3,768,768]{2,1,0:T(8,128)(2,1)}, bf16[2,512,768]{2,1,0:T(8,128)(2,1)}, f32[1,768]{1,0:T(1,128)}) custom-call(bf16[2,512,768]{2,1,0:T(8,128)(2,1)} %tokens_ref.10, f32[1,768]{1,0:T(1,128)} %reshape.703.gain_one_ref.gain_ref, bf16[512,768]{1,0:T(8,128)(2,1)} %get-tuple-element.154.gradmixed_ref, ...), custom_call_target="tpu_custom_call" | custom-call | flops 10066329600 | bytes 22020096 | tf_op jit(solution)/shard_map/back_heads/pallas_call | solution.py:434
  240.0 9.3 %convolution_add_fusion.1 = f32[768,3072]{1,0:T(8,128)} fusion(f32[768,3072]{1,0:T(8,128)} %fusion.51, bf16[640,768]{1,0:T(8,128)(2,1)} %get-tuple-element.131, bf16[640,3072]{1,0:T(8,128)(2,1)S(1)} %copy-done.2), kind=kOutput, calls=%fused_computation.3 | convolution fusion | flops 3022258176 | bytes 23789568 | tf_op jit(solution)/shard_map/rd,rf->df/dot_general | solution.py:717
  249.3 8.7 %convolution_add_fusion = f32[3072,768]{1,0:T(8,128)} fusion(f32[3072,768]{1,0:T(8,128)} %fusion.52, bf16[640,3072]{1,0:T(8,128)(2,1)S(1)} %copy-done.1, bf16[640,768]{1,0:T(8,128)(2,1)S(1)} %copy-done.5), kind=kOutput, calls=%fused_computation.2 | convolution fusion | flops 3022258176 | bytes 23789568 | tf_op jit(solution)/shard_map/rf,rd->fd/dot_general | solution.py:718
  258.0 9.9 %back_rows.3 = (bf16[2,512,768]{2,1,0:T(8,128)(2,1)}, f32[512,768]{1,0:T(8,128)}, bf16[512,768]{1,0:T(8,128)(2,1)}, bf16[768,768]{1,0:T(8,128)(2,1)}, f32[768,32...) custom-call(s32[512,2]{1,0:T(8,128)} %bitcast.229, ...), custom_call_target="tpu_custom_call", output_to_operand_aliasing={{0}: (14, {})} | custom-call | flops 3825205248 | bytes 12582912 | tf_op jit(solution)/shard_map/back_rows/pallas_call | solution.py:304
  267.9 19.5 %back_heads.3 = (f32[3,4,1024]{2,1,0:T(4,128)}, bf16[3,768,768]{2,1,0:T(8,128)(2,1)}, bf16[2,512,768]{2,1,0:T(8,128)(2,1)}, f32[1,768]{1,0:T(1,128)}) custom-call(bf16[2,512,768]{2,1,0:T(8,128)(2,1)} %tokens_ref.10, f32[1,768]{1,0:T(1,128)} %reshape.703.gain_one_ref.gain_ref, ...), custom_call_target="tpu_custom_call", output_to_operand_aliasing={{2}: (16, {})} | custom-call | flops 10066329600 | bytes 22020096 | tf_op jit(solution)/shard_map/back_heads/pallas_call | solution.py:434
  298.8 11.8 %collective-permute-done.11 = bf16[1,2,2,2,48,768]{5,4,1,2,3,0:T(8,128)(2,1)S(1)} collective-permute-done((bf16[1,2,2,2,48,768]{5,4,1,2,3,0:T(8,128)(2,1)S(1)}, bf16[1,2,2,2,48,768]{5,4,1,2,3,0:T(8,128)(2,1)S(1)}, u32[]{:S(2)}, u32[]{:S(2)}) %collective-permute-start.11) | collective-permute-done | bytes 589856 | tf_op jit(solution)/shard_map/ppermute | solution.py:512
  316.1 4.6 %collective-permute-done.15 = bf16[1,2,2,48,768]{4,3,1,2,0:T(8,128)(2,1)S(1)} collective-permute-done((bf16[1,2,2,48,768]{4,3,1,2,0:T(8,128)(2,1)S(1)}, bf16[1,2,2,48,768]{4,3,1,2,0:T(8,128)(2,1)S(1)}, u32[]{:S(2)}, u32[]{:S(2)}) %collective-permute-start.15) | collective-permute-done | bytes 294944 | tf_op jit(solution)/shard_map/ppermute | solution.py:512
  325.7 4.6 %all-to-all-start.5 = ((bf16[32,32,128]{2,1,0:T(8,128)(2,1)}), bf16[32,32,128]{2,1,0:T(8,128)(2,1)S(1)}, u32[]{:S(2)}, u32[]{:S(2)}) async-start(bf16[32,32,128]{2,1,0:T(8,128)(2,1)} %pad_maximum_fusion.13), calls=%async_computation.5 | async-start | bytes 524288 | tf_op jit(solution)/shard_map/all_to_all | solution.py:507
  333.3 11.1 %all-to-all-done.5 = bf16[32,32,128]{2,1,0:T(8,128)(2,1)S(1)} async-done(((bf16[32,32,128]{2,1,0:T(8,128)(2,1)}), bf16[32,32,128]{2,1,0:T(8,128)(2,1)S(1)}, u32[]{:S(2)}, u32[]{:S(2)}) %all-to-all-start.5) | async-done | bytes 262176 | tf_op jit(solution)/shard_map/all_to_all | solution.py:507
  (177 shorter events, 91.9 us)
Async XLA Ops:
  2.1 15.7 %collective-permute-start = (bf16[4,24,768]{2,1,0:T(8,128)(2,1)}, bf16[4,24,768]{2,1,0:T(8,128)(2,1)S(1)}, u32[]{:S(2)}, u32[]{:S(2)}) collective-permute-start(bf16[4,24,768]{2,1,0:T(8,128)(2,1)} %pack.1), channel_id=1, source_target_pairs={{0,16},{1,17},{2,18},{3,19},{4,20},{5,21},{6,22},{7,23},{8,24},{9,... | collective-permute-start | bytes 442376 | tf_op jit(solution)/shard_map/ppermute | solution.py:512
  8.3 7.5 %collective-permute-start.2 = (bf16[8,768]{1,0:T(8,128)(2,1)S(1)}, bf16[8,768]{1,0:T(8,128)(2,1)S(1)}, u32[]{:S(2)}, u32[]{:S(2)}) collective-permute-start(bf16[8,768]{1,0:T(8,128)(2,1)S(1)} %fusion.41), channel_id=1, source_target_pairs={{0,16},{1,17},{2,18},{3,19},{4,20},{5,21},{6,22},{7,23},{8,24},{9,... | collective-permute-start | bytes 36872 | tf_op jit(solution)/shard_map/ppermute | solution.py:512
  15.9 4.1 %collective-permute-start.3 = (bf16[2,8,768]{2,1,0:T(8,128)(2,1)S(1)}, bf16[2,8,768]{2,1,0:T(8,128)(2,1)S(1)}, u32[]{:S(2)}, u32[]{:S(2)}) collective-permute-start(bf16[2,8,768]{2,1,0:T(8,128)(2,1)S(1)} %pad_maximum_fusion.16), channel_id=1, source_target_pairs={{0,8},{1,9},{2,10},{3,11},{4,12},{5,13},{6,14},{7,15},{8,0},{9,1},... | collective-permute-start | bytes 73736 | tf_op jit(solution)/shard_map/ppermute | solution.py:512
  17.9 8.2 %collective-permute-start.1 = (bf16[2,4,24,768]{3,2,1,0:T(8,128)(2,1)S(1)}, bf16[2,4,24,768]{3,2,1,0:T(8,128)(2,1)S(1)}, u32[]{:S(2)}, u32[]{:S(2)}) collective-permute-start(bf16[2,4,24,768]{3,2,1,0:T(8,128)(2,1)S(1)} %pad_maximum_fusion.11), channel_id=1, source_target_pairs={{0,8},{1,9},{2,10},{3,11},{4,12},{5,13},{6,14},{7,15},{8,0},{9,1},... | collective-permute-start | bytes 884744 | tf_op jit(solution)/shard_map/ppermute | solution.py:512
  26.3 7.3 %collective-permute-start.5 = (bf16[2,2,48,768]{3,2,0,1:T(8,128)(2,1)S(1)}, bf16[2,2,48,768]{3,2,0,1:T(8,128)(2,1)S(1)}, u32[]{:S(2)}, u32[]{:S(2)}) collective-permute-start(bf16[2,2,48,768]{3,2,0,1:T(8,128)(2,1)S(1)} %pad_maximum_fusion.12), channel_id=1, source_target_pairs={{0,2},{1,3},{2,0},{3,1},{4,6},{5,7},{6,4},{7,5},{8,10},{9,11},{10,... | collective-permute-start | bytes 884744 | tf_op jit(solution)/shard_map/ppermute | solution.py:512
  27.9 8.1 %collective-permute-start.4 = (bf16[2,2,56,768]{3,2,0,1:T(8,128)(2,1)S(1)}, bf16[2,2,56,768]{3,2,0,1:T(8,128)(2,1)S(1)}, u32[]{:S(2)}, u32[]{:S(2)}) collective-permute-start(bf16[2,2,56,768]{3,2,0,1:T(8,128)(2,1)S(1)} %pad_maximum_fusion.10), channel_id=1, source_target_pairs={{0,4},{1,5},{2,6},{3,7},{4,0},{5,1},{6,2},{7,3},{8,12},{9,13},{10,... | collective-permute-start | bytes 1032200 | tf_op jit(solution)/shard_map/ppermute | solution.py:512
  36.3 18.0 %collective-permute-start.7 = (bf16[2,2,2,48,768]{4,3,0,1,2:T(8,128)(2,1)S(1)}, bf16[2,2,2,48,768]{4,3,0,1,2:T(8,128)(2,1)S(1)}, u32[]{:S(2)}, u32[]{:S(2)}) collective-permute-start(bf16[2,2,2,48,768]{4,3,0,1,2:T(8,128)(2,1)S(1)} %pad_maximum_fusion.9), channel_id=1, source_target_pairs={{0,4},{1,5},{2,6},{3,7},{4,0},{5,1},{6,2},{7,3},{8,12},{9,13},{10,... | collective-permute-start | bytes 1769480 | tf_op jit(solution)/shard_map/ppermute | solution.py:512
  37.8 24.6 %collective-permute-start.6 = (bf16[2,2,2,56,768]{4,3,0,1,2:T(8,128)(2,1)S(1)}, bf16[2,2,2,56,768]{4,3,0,1,2:T(8,128)(2,1)S(1)}, u32[]{:S(2)}, u32[]{:S(2)}) collective-permute-start(bf16[2,2,2,56,768]{4,3,0,1,2:T(8,128)(2,1)S(1)} %pad_maximum_fusion.6), channel_id=1, source_target_pairs={{0,2},{1,3},{2,0},{3,1},{4,6},{5,7},{6,4},{7,5},{8,10},{9,11},{10,... | collective-permute-start | bytes 2064392 | tf_op jit(solution)/shard_map/ppermute | solution.py:512
  38.4 54.8 %all-to-all-start = ((bf16[32,40,768]{2,1,0:T(8,128)(2,1)}), bf16[32,40,768]{2,1,0:T(8,128)(2,1)}, u32[]{:S(2)}, u32[]{:S(2)}) async-start(bf16[32,40,768]{2,1,0:T(8,128)(2,1)} %bitcast.27), calls=%async_computation | async-start | bytes 3932160 | tf_op jit(solution)/shard_map/all_to_all | solution.py:507
  62.7 3.0 collective-permute-start.9
  62.8 6.4 %collective-permute-start.8 = (bf16[2,2,2,2,56,768]{5,4,0,1,2,3:T(8,128)(2,1)S(1)}, bf16[2,2,2,2,56,768]{5,4,0,1,2,3:T(8,128)(2,1)}, u32[]{:S(2)}, u32[]{:S(2)}) collective-permute-start(bf16[2,2,2,2,56,768]{5,4,0,1,2,3:T(8,128)(2,1)S(1)} %pad_maximum_fusion.3), channel_id=1, source_target_pairs={{0,1},{1,0},{2,3},{3,2},{4,5},{5,4},{6,7},{7,6},{8,9},{9,8},{10,11... | collective-permute-start | bytes 4128776 | tf_op jit(solution)/shard_map/ppermute | solution.py:512
  93.2 30.3 %all-to-all-start.2 = ((bf16[32,40,384]{2,1,0:T(8,128)(2,1)}), bf16[32,40,384]{2,1,0:T(8,128)(2,1)}, u32[]{:S(2)}, u32[]{:S(2)}) async-start(bf16[32,40,384]{2,1,0:T(8,128)(2,1)} %bitcast.225), calls=%async_computation.2 | async-start | bytes 1966080 | tf_op jit(solution)/shard_map/all_to_all | solution.py:507
  123.5 28.7 %all-to-all-start.1 = ((bf16[32,40,384]{2,1,0:T(8,128)(2,1)}), bf16[32,40,384]{2,1,0:T(8,128)(2,1)S(1)}, u32[]{:S(2)}, u32[]{:S(2)}) async-start(bf16[32,40,384]{2,1,0:T(8,128)(2,1)} %bitcast.227), calls=%async_computation.1 | async-start | bytes 1966080 | tf_op jit(solution)/shard_map/all_to_all | solution.py:507
  153.1 51.4 %all-to-all-start.3 = ((bf16[32,40,768]{2,1,0:T(8,128)(2,1)}), bf16[32,40,768]{2,1,0:T(8,128)(2,1)S(1)}, u32[]{:S(2)}, u32[]{:S(2)}) async-start(bf16[32,40,768]{2,1,0:T(8,128)(2,1)} %bitcast.223), calls=%async_computation.3 | async-start | bytes 3932160 | tf_op jit(solution)/shard_map/all_to_all | solution.py:507
  205.8 52.2 %all-to-all-start.4 = ((bf16[32,40,768]{2,1,0:T(8,128)(2,1)}), bf16[32,40,768]{2,1,0:T(8,128)(2,1)}, u32[]{:S(2)}, u32[]{:S(2)}) async-start(bf16[32,40,768]{2,1,0:T(8,128)(2,1)} %bitcast.221), calls=%async_computation.4 | async-start | bytes 3932160 | tf_op jit(solution)/shard_map/all_to_all | solution.py:507
  290.4 3.8 %collective-permute-start.10 = (bf16[1,2,2,2,2,72,768]{6,5,1,2,4,3,0:T(8,128)(2,1)S(1)}, bf16[1,2,2,2,2,72,768]{6,5,1,2,4,3,0:T(8,128)(2,1)S(1)}, u32[]{:S(2)}, u32[]{:S(2)}) collective-permute-start(bf16[1,2,2,2,2,72,768]{6,5,1,2,4,3,0:T(8,128)(2,1)S(1)} %select_bitcast_fusion), channel_id=1, source_target_pairs={{0,1},{1,0},{2,3},{3,2},{4,5},{5,4},{6,7},{7,6},{8,9},{9,8},{10,11... | collective-permute-start | bytes 5308424 | tf_op jit(solution)/shard_map/ppermute | solution.py:512
  291.7 5.1 %collective-permute-start.12 = (bf16[1,2,2,2,2,24,768]{6,5,1,2,4,3,0:T(8,128)(2,1)S(1)}, bf16[1,2,2,2,2,24,768]{6,5,1,2,4,3,0:T(8,128)(2,1)S(1)}, u32[]{:S(2)}, u32[]{:S(2)}) collective-permute-start(bf16[1,2,2,2,2,24,768]{6,5,1,2,4,3,0:T(8,128)(2,1)S(1)} %select_bitcast_fusion.7), channel_id=1, source_target_pairs={{0,1},{1,0},{2,3},{3,2},{4,5},{5,4},{6,7},{7,6},{8,9},{9,8},{10,11... | collective-permute-start | bytes 1769480 | tf_op jit(solution)/shard_map/ppermute | solution.py:512
  294.9 15.7 %collective-permute-start.11 = (bf16[1,2,2,2,48,768]{5,4,1,2,3,0:T(8,128)(2,1)S(1)}, bf16[1,2,2,2,48,768]{5,4,1,2,3,0:T(8,128)(2,1)S(1)}, u32[]{:S(2)}, u32[]{:S(2)}) collective-permute-start(bf16[1,2,2,2,48,768]{5,4,1,2,3,0:T(8,128)(2,1)S(1)} %fusion.10), channel_id=1, source_target_pairs={{0,2},{1,3},{2,0},{3,1},{4,6},{5,7},{6,4},{7,5},{8,10},{9,11},{10,... | collective-permute-start | bytes 1769480 | tf_op jit(solution)/shard_map/ppermute | solution.py:512
  297.2 15.2 %collective-permute-start.13 = (bf16[1,2,2,2,48,768]{5,4,1,2,3,0:T(8,128)(2,1)S(1)}, bf16[1,2,2,2,48,768]{5,4,1,2,3,0:T(8,128)(2,1)S(1)}, u32[]{:S(2)}, u32[]{:S(2)}) collective-permute-start(bf16[1,2,2,2,48,768]{5,4,1,2,3,0:T(8,128)(2,1)S(1)} %fusion.11), channel_id=1, source_target_pairs={{0,4},{1,5},{2,6},{3,7},{4,0},{5,1},{6,2},{7,3},{8,12},{9,13},{10,... | collective-permute-start | bytes 1769480 | tf_op jit(solution)/shard_map/ppermute | solution.py:512
  312.7 8.0 %collective-permute-start.15 = (bf16[1,2,2,48,768]{4,3,1,2,0:T(8,128)(2,1)S(1)}, bf16[1,2,2,48,768]{4,3,1,2,0:T(8,128)(2,1)S(1)}, u32[]{:S(2)}, u32[]{:S(2)}) collective-permute-start(bf16[1,2,2,48,768]{4,3,1,2,0:T(8,128)(2,1)S(1)} %fusion.18), channel_id=1, source_target_pairs={{0,2},{1,3},{2,0},{3,1},{4,6},{5,7},{6,4},{7,5},{8,10},{9,11},{10,... | collective-permute-start | bytes 884744 | tf_op jit(solution)/shard_map/ppermute | solution.py:512
  313.9 8.2 %collective-permute-start.14 = (bf16[1,2,2,48,768]{4,3,1,2,0:T(8,128)(2,1)}, bf16[1,2,2,48,768]{4,3,1,2,0:T(8,128)(2,1)}, u32[]{:S(2)}, u32[]{:S(2)}) collective-permute-start(bf16[1,2,2,48,768]{4,3,1,2,0:T(8,128)(2,1)} %fusion.17), channel_id=1, source_target_pairs={{0,4},{1,5},{2,6},{3,7},{4,0},{5,1},{6,2},{7,3},{8,12},{9,13},{10,... | collective-permute-start | bytes 884744 | tf_op jit(solution)/shard_map/ppermute | solution.py:512
  323.2 7.2 %collective-permute-start.16 = (bf16[1,2,96,768]{3,2,1,0:T(8,128)(2,1)S(1)}, bf16[1,2,96,768]{3,2,1,0:T(8,128)(2,1)S(1)}, u32[]{:S(2)}, u32[]{:S(2)}) collective-permute-start(bf16[1,2,96,768]{3,2,1,0:T(8,128)(2,1)S(1)} %fusion.19), channel_id=1, source_target_pairs={{0,8},{1,9},{2,10},{3,11},{4,12},{5,13},{6,14},{7,15},{8,0},{9,1},... | collective-permute-start | bytes 884744 | tf_op jit(solution)/shard_map/ppermute | solution.py:512
  325.7 18.6 %all-to-all-start.5 = ((bf16[32,32,128]{2,1,0:T(8,128)(2,1)}), bf16[32,32,128]{2,1,0:T(8,128)(2,1)S(1)}, u32[]{:S(2)}, u32[]{:S(2)}) async-start(bf16[32,32,128]{2,1,0:T(8,128)(2,1)} %pad_maximum_fusion.13), calls=%async_computation.5 | async-start | bytes 524288 | tf_op jit(solution)/shard_map/all_to_all | solution.py:507
  330.5 15.6 %collective-permute-start.17 = (bf16[1,96,768]{2,1,0:T(8,128)(2,1)S(1)}, bf16[1,96,768]{2,1,0:T(8,128)(2,1)S(1)}, u32[]{:S(2)}, u32[]{:S(2)}) collective-permute-start(bf16[1,96,768]{2,1,0:T(8,128)(2,1)S(1)} %fusion.20), channel_id=1, source_target_pairs={{0,16},{1,17},{2,18},{3,19},{4,20},{5,21},{6,22},{7,23},{8,24},{9,... | collective-permute-start | bytes 442376 | tf_op jit(solution)/shard_map/ppermute | solution.py:512
  (20 other events, 140.2 us)

commit v5 on v3

--- a/solution.py
+++ b/solution.py
@@ -315,7 +315,7 @@
             shape((length, width), bf16), shape((width, width), bf16),
             shape((width, experts), f32), shape((1, width), f32), shape((1, experts), f32),
         ],
-        compiler_params=params(60),
+        compiler_params=params(44),
         cost_estimate=pl.CostEstimate(
             flops=2 * length * width * (3 * width + 2 * returned.shape[0]),
             bytes_accessed=12 * MIB, transcendentals=0,

time: 351 us -> 366 us (1.043)
  local copies, waits for them, and re-layouts: 22.2 us -> 34.5 us
  Pallas kernels: 138 us -> 134 us
    unnamed x42 -> x74, local copies, waits for them, and re-layouts: 4.51 us -> 18.9 us
    pallas_call x2, Pallas kernels: 19.1 us -> 14.8 us  [back_rows_call(): pl.pallas_call(back_rows_kernel, grid=(1,), in_specs=[vmem] * 3 + [one_in...]
  transfers between devices with their start and end apart: 24 -> 24, of which waited for: 16 -> 16; matrix products, arithmetic and copies ran while one was open for 19% -> 19% of each run, Pallas kernels for 31% -> 29%
where the time goes in v5:
time: 366 us; the launch traced here: 360 us
  Pallas kernels  134 us (37%)
  waiting for transfers between devices  81 us (22%)
  starting transfers between devices  50.7 us (14%)
  matrix products  44.5 us (12%)
  local copies, waits for them, and re-layouts  34.5 us (9%)
  other arithmetic  13.1 us (4%)
    ppermute x18, waiting for transfers between devices, swap(): lax.ppermute(value, AXES, [(at, at ^ 1 << bit) for at in range(devices)])  59.4 us
    pallas_call x2, Pallas kernels, expert_call(): pl.pallas_call(functools.partial(expert_kernel, mine_at), grid_spec=pltpu...  46.9 us
    pallas_call x2, Pallas kernels, back_heads_call(): pl.pallas_call(back_heads_kernel, grid=(groups,), in_specs=[one_in(at, le...  38.4 us
    pallas_call x2, Pallas kernels, front_call(): pl.pallas_call(front_kernel, grid=(groups,), in_specs=[one_in(at, length,...  30.8 us
    all_to_all x6, starting transfers between devices, exchange(): return lax.all_to_all(buffer, AXES, split_axis=0, concat_axis=0, tiled=True)  28.1 us
    dot_general x2, matrix products, body(): jnp.einsum('rd,rf->df', rows, grad_inner, preferred_element_type=f32)  23.1 us
    ppermute x18, starting transfers between devices, swap(): lax.ppermute(value, AXES, [(at, at ^ 1 << bit) for at in range(devices)])  22.6 us
    all_to_all x6, waiting for transfers between devices, exchange(): return lax.all_to_all(buffer, AXES, split_axis=0, concat_axis=0, tiled=True)  21.7 us
  transfers between devices with their start and end apart: 24, of which 16 were waited for; matrix products, arithmetic and copies ran while one was open for 19% of the time, Pallas kernels for 29%

profile of v5, /device:TPU:0, one launch (start us, length us, event | category | flops | bytes accessed | tf_op | source)
XLA Modules:
  0.0 360.4 jit_solution(11114883963036562705)
XLA Ops:
  10.7 5.1 %fusion.1 = bf16[1280,768]{1,0:T(8,128)(2,1)} fusion(bf16[1024,768]{1,0:T(8,128)(2,1)} %bitcast.211, s32[1024]{0:T(1024)S(1)} %pad_add_fusion), kind=kOutput, calls=%fused_computation.6 | convolution fusion | flops 2015559680 | bytes 3543040 | tf_op jit(solution)/shard_map/dot_general | solution.py:640
  20.0 6.1 %collective-permute-done.1 = bf16[2,4,24,768]{3,2,1,0:T(8,128)(2,1)S(1)} collective-permute-done((bf16[2,4,24,768]{3,2,1,0:T(8,128)(2,1)S(1)}, bf16[2,4,24,768]{3,2,1,0:T(8,128)(2,1)S(1)}, u32[]{:S(2)}, u32[]{:S(2)}) %collective-permute-start.1) | collective-permute-done | bytes 294944 | tf_op jit(solution)/shard_map/ppermute | solution.py:512
  42.9 11.4 %collective-permute-done.7 = bf16[2,2,2,48,768]{4,3,0,1,2:T(8,128)(2,1)S(1)} collective-permute-done((bf16[2,2,2,48,768]{4,3,0,1,2:T(8,128)(2,1)S(1)}, bf16[2,2,2,48,768]{4,3,0,1,2:T(8,128)(2,1)S(1)}, u32[]{:S(2)}, u32[]{:S(2)}) %collective-permute-start.7) | collective-permute-done | bytes 589856 | tf_op jit(solution)/shard_map/ppermute | solution.py:512
  54.5 8.0 %collective-permute-done.6 = bf16[2,2,2,56,768]{4,3,0,1,2:T(8,128)(2,1)S(1)} collective-permute-done((bf16[2,2,2,56,768]{4,3,0,1,2:T(8,128)(2,1)S(1)}, bf16[2,2,2,56,768]{4,3,0,1,2:T(8,128)(2,1)S(1)}, u32[]{:S(2)}, u32[]{:S(2)}) %collective-permute-start.6) | collective-permute-done | bytes 688160 | tf_op jit(solution)/shard_map/ppermute | solution.py:512
  77.7 15.5 %front.3 = (bf16[512,768]{1,0:T(8,128)(2,1)}, bf16[512,768]{1,0:T(8,128)(2,1)}, bf16[512,768]{1,0:T(8,128)(2,1)}, bf16[512,768]{1,0:T(8,128)(2,1)}, f32[3,512,4]{2,1,0:T(8,128)}, /*index=5*/bf16[1280,384]{1,0:T(8,128)(2,1)}) custom-call(bf16[2,512,768]{2,1,0:T(8,128)(2,1)} %tokens_ref.10, bf16[768,768]{1,0:T(8,128)(2,1)} %bitcast.221, ...), custom_call_target="tpu_custom_call" | custom-call | flops 1000000 | bytes 262144 | tf_op jit(solution)/shard_map/front/pallas_call | solution.py:117
  93.2 5.4 %all-to-all-start.2 = ((bf16[32,40,384]{2,1,0:T(8,128)(2,1)}), bf16[32,40,384]{2,1,0:T(8,128)(2,1)}, u32[]{:S(2)}, u32[]{:S(2)}) async-start(bf16[32,40,384]{2,1,0:T(8,128)(2,1)} %bitcast.236), calls=%async_computation.2 | async-start | bytes 1966080 | tf_op jit(solution)/shard_map/all_to_all | solution.py:507
  100.4 15.3 %front.2 = (bf16[512,768]{1,0:T(8,128)(2,1)}, bf16[512,768]{1,0:T(8,128)(2,1)}, bf16[512,768]{1,0:T(8,128)(2,1)}, bf16[512,768]{1,0:T(8,128)(2,1)}, f32[3,512,4]{2,1,0:T(8,128)}, /*index=5*/bf16[1280,384]{1,0:T(8,128)(2,1)}) custom-call(bf16[2,512,768]{2,1,0:T(8,128)(2,1)} %tokens_ref.10, bf16[768,768]{1,0:T(8,128)(2,1)} %bitcast.222, ...), custom_call_target="tpu_custom_call" | custom-call | flops 1000000 | bytes 262144 | tf_op jit(solution)/shard_map/front/pallas_call | solution.py:117
  115.8 7.7 %all-to-all-done.2 = bf16[32,40,384]{2,1,0:T(8,128)(2,1)} async-done(((bf16[32,40,384]{2,1,0:T(8,128)(2,1)}), bf16[32,40,384]{2,1,0:T(8,128)(2,1)}, u32[]{:S(2)}, u32[]{:S(2)}) %all-to-all-start.2) | async-done | bytes 983072 | tf_op jit(solution)/shard_map/all_to_all | solution.py:507
  128.1 23.2 %expert.3 = (bf16[1280,768]{1,0:T(8,128)(2,1)}, bf16[640,768]{1,0:T(8,128)(2,1)}, bf16[640,3072]{1,0:T(8,128)(2,1)}, bf16[640,3072]{1,0:T(8,128)(2,1)}, bf16[640,768]{1,0:T(8,128)(2,1)}) custom-call(s32[1]{0:T(128)} %bitcast.44.own_ref, bf16[1280,384]{1,0:T(8,128)(2,1)} %bitcast.59.arrived_ref, bf16[1280,768]{1,0:T(8,128)(2,1)} %bitcast.54.raw_ref, ...), custom_call_target="tpu_custom_call" | custom-call | flops 12079595520 | bytes 20971520 | tf_op jit(solution)/shard_map/expert/pallas_call | solution.py:218
  153.1 5.4 %all-to-all-start.3 = ((bf16[32,40,768]{2,1,0:T(8,128)(2,1)}), bf16[32,40,768]{2,1,0:T(8,128)(2,1)S(1)}, u32[]{:S(2)}, u32[]{:S(2)}) async-start(bf16[32,40,768]{2,1,0:T(8,128)(2,1)} %bitcast.235), calls=%async_computation.3 | async-start | bytes 3932160 | tf_op jit(solution)/shard_map/all_to_all | solution.py:507
  158.5 10.2 %fusion.51 = f32[768,3072]{1,0:T(8,128)} fusion(bf16[640,768]{1,0:T(8,128)(2,1)} %get-tuple-element.121, bf16[640,3072]{1,0:T(8,128)(2,1)} %get-tuple-element.122), kind=kOutput, calls=%fused_computation.161 | convolution fusion | flops 3019898880 | bytes 14352384 | tf_op jit(solution)/shard_map/rd,rf->df/dot_general | solution.py:713
  168.7 6.4 %fusion.52 = f32[3072,768]{1,0:T(8,128)} fusion(bf16[640,3072]{1,0:T(8,128)(2,1)S(1)} %copy-done.34, bf16[640,768]{1,0:T(8,128)(2,1)S(1)} %copy-done.35), kind=kOutput, calls=%fused_computation.162 | convolution fusion | flops 3019898880 | bytes 14352384 | tf_op jit(solution)/shard_map/rf,rd->fd/dot_general | solution.py:714
  175.1 23.7 %expert.2 = (bf16[1280,768]{1,0:T(8,128)(2,1)}, bf16[640,768]{1,0:T(8,128)(2,1)}, bf16[640,3072]{1,0:T(8,128)(2,1)}, bf16[640,3072]{1,0:T(8,128)(2,1)}, bf16[640,768]{1,0:T(8,128)(2,1)}) custom-call(s32[1]{0:T(128)} %bitcast.44.own_ref, bf16[1280,384]{1,0:T(8,128)(2,1)} %bitcast.237, bf16[1280,768]{1,0:T(8,128)(2,1)} %bitcast.54.raw_ref, ...), custom_call_target="tpu_custom_call" | custom-call | flops 12079595520 | bytes 20971520 | tf_op jit(solution)/shard_map/expert/pallas_call | solution.py:218
  198.7 5.8 %all-to-all-done.3 = bf16[32,40,768]{2,1,0:T(8,128)(2,1)S(1)} async-done(((bf16[32,40,768]{2,1,0:T(8,128)(2,1)}), bf16[32,40,768]{2,1,0:T(8,128)(2,1)S(1)}, u32[]{:S(2)}, u32[]{:S(2)}) %all-to-all-start.3) | async-done | bytes 1966112 | tf_op jit(solution)/shard_map/all_to_all | solution.py:507
  215.5 7.0 %back_rows.2 = (bf16[2,512,768]{2,1,0:T(8,128)(2,1)}, f32[512,768]{1,0:T(8,128)S(1)}, bf16[512,768]{1,0:T(8,128)(2,1)S(1)}, bf16[768,768]{1,0:T(8,128)(2,1)S(1)}...) custom-call(s32[512,2]{1,0:T(8,128)S(1)} %bitcast.202, s32[512,1]{1,0:T(8,128)S(1)} %copy-done.3, ...), custom_call_target="tpu_custom_call" | custom-call | flops 3825205248 | bytes 12582912 | tf_op jit(solution)/shard_map/back_rows/pallas_call | solution.py:304
  226.4 18.9 %back_heads.2 = (f32[3,4,1024]{2,1,0:T(4,128)}, bf16[3,768,768]{2,1,0:T(8,128)(2,1)}, bf16[2,512,768]{2,1,0:T(8,128)(2,1)}, f32[1,768]{1,0:T(1,128)}) custom-call(bf16[2,512,768]{2,1,0:T(8,128)(2,1)} %tokens_ref.10, f32[1,768]{1,0:T(1,128)} %reshape.703.gain_one_ref.gain_ref, bf16[512,768]{1,0:T(8,128)(2,1)} %copy-done.19, ...), custom_call_target="tpu_custom_call" | custom-call | flops 10066329600 | bytes 22020096 | tf_op jit(solution)/shard_map/back_heads/pallas_call | solution.py:434
  245.4 12.9 %convolution_add_fusion.1 = f32[768,3072]{1,0:T(8,128)} fusion(f32[768,3072]{1,0:T(8,128)} %fusion.51, bf16[640,768]{1,0:T(8,128)(2,1)} %get-tuple-element.129, bf16[640,3072]{1,0:T(8,128)(2,1)} %get-tuple-element.130), kind=kOutput, calls=%fused_computation.3 | convolution fusion | flops 3022258176 | bytes 23789568 | tf_op jit(solution)/shard_map/rd,rf->df/dot_general | solution.py:713
  258.3 8.7 %convolution_add_fusion = f32[3072,768]{1,0:T(8,128)} fusion(f32[3072,768]{1,0:T(8,128)} %fusion.52, bf16[640,3072]{1,0:T(8,128)(2,1)S(1)} %copy-done.20, bf16[640,768]{1,0:T(8,128)(2,1)S(1)} %copy-done.22), kind=kOutput, calls=%fused_computation.2 | convolution fusion | flops 3022258176 | bytes 23789568 | tf_op jit(solution)/shard_map/rf,rd->fd/dot_general | solution.py:714
  271.9 7.8 %back_rows.3 = (bf16[2,512,768]{2,1,0:T(8,128)(2,1)}, f32[512,768]{1,0:T(8,128)S(1)}, bf16[512,768]{1,0:T(8,128)(2,1)S(1)}, bf16[768,768]{1,0:T(8,128)(2,1)S(1)}...) custom-call(s32[512,2]{1,0:T(8,128)S(1)} %bitcast.201, ...), custom_call_target="tpu_custom_call", output_to_operand_aliasing={{0}: (14, {})} | custom-call | flops 3825205248 | bytes 12582912 | tf_op jit(solution)/shard_map/back_rows/pallas_call | solution.py:304
  281.7 19.4 %back_heads.3 = (f32[3,4,1024]{2,1,0:T(4,128)}, bf16[3,768,768]{2,1,0:T(8,128)(2,1)}, bf16[2,512,768]{2,1,0:T(8,128)(2,1)}, f32[1,768]{1,0:T(1,128)}) custom-call(bf16[2,512,768]{2,1,0:T(8,128)(2,1)} %tokens_ref.10, f32[1,768]{1,0:T(1,128)} %reshape.703.gain_one_ref.gain_ref, bf16[512,768]{1,0:T(8,128)(2,1)} %copy-done.15, ...), custom_call_target="tpu_custom_call", output_to_operand_aliasing={{2}: (16, {})} | custom-call | flops 10066329600 | bytes 22020096 | tf_op jit(solution)/shard_map/back_heads/pallas_call | solution.py:434
  312.5 11.8 %collective-permute-done.11 = bf16[1,2,2,2,48,768]{5,4,1,2,3,0:T(8,128)(2,1)S(1)} collective-permute-done((bf16[1,2,2,2,48,768]{5,4,1,2,3,0:T(8,128)(2,1)S(1)}, bf16[1,2,2,2,48,768]{5,4,1,2,3,0:T(8,128)(2,1)S(1)}, u32[]{:S(2)}, u32[]{:S(2)}) %collective-permute-start.11) | collective-permute-done | bytes 589856 | tf_op jit(solution)/shard_map/ppermute | solution.py:512
  331.6 4.6 %all-to-all-start.5 = ((bf16[32,32,128]{2,1,0:T(8,128)(2,1)}), bf16[32,32,128]{2,1,0:T(8,128)(2,1)S(1)}, u32[]{:S(2)}, u32[]{:S(2)}) async-start(bf16[32,32,128]{2,1,0:T(8,128)(2,1)} %pad_maximum_fusion.13), calls=%async_computation.5 | async-start | bytes 524288 | tf_op jit(solution)/shard_map/all_to_all | solution.py:507
  339.3 7.4 %all-to-all-done.5 = bf16[32,32,128]{2,1,0:T(8,128)(2,1)S(1)} async-done(((bf16[32,32,128]{2,1,0:T(8,128)(2,1)}), bf16[32,32,128]{2,1,0:T(8,128)(2,1)S(1)}, u32[]{:S(2)}, u32[]{:S(2)}) %all-to-all-start.5) | async-done | bytes 262176 | tf_op jit(solution)/shard_map/all_to_all | solution.py:507
  352.8 6.4 %collective-permute-done.17 = bf16[1,96,768]{2,1,0:T(8,128)(2,1)S(1)} collective-permute-done((bf16[1,96,768]{2,1,0:T(8,128)(2,1)S(1)}, bf16[1,96,768]{2,1,0:T(8,128)(2,1)S(1)}, u32[]{:S(2)}, u32[]{:S(2)}) %collective-permute-start.17) | collective-permute-done | bytes 147488 | tf_op jit(solution)/shard_map/ppermute | solution.py:512
  (209 shorter events, 103.7 us)
Async XLA Ops:
  2.1 15.7 %collective-permute-start = (bf16[4,24,768]{2,1,0:T(8,128)(2,1)}, bf16[4,24,768]{2,1,0:T(8,128)(2,1)S(1)}, u32[]{:S(2)}, u32[]{:S(2)}) collective-permute-start(bf16[4,24,768]{2,1,0:T(8,128)(2,1)} %pack.1), channel_id=1, source_target_pairs={{0,16},{1,17},{2,18},{3,19},{4,20},{5,21},{6,22},{7,23},{8,24},{9,... | collective-permute-start | bytes 442376 | tf_op jit(solution)/shard_map/ppermute | solution.py:512
  8.3 7.5 %collective-permute-start.2 = (bf16[8,768]{1,0:T(8,128)(2,1)S(1)}, bf16[8,768]{1,0:T(8,128)(2,1)S(1)}, u32[]{:S(2)}, u32[]{:S(2)}) collective-permute-start(bf16[8,768]{1,0:T(8,128)(2,1)S(1)} %fusion.41), channel_id=1, source_target_pairs={{0,16},{1,17},{2,18},{3,19},{4,20},{5,21},{6,22},{7,23},{8,24},{9,... | collective-permute-start | bytes 36872 | tf_op jit(solution)/shard_map/ppermute | solution.py:512
  15.9 4.1 %collective-permute-start.3 = (bf16[2,8,768]{2,1,0:T(8,128)(2,1)S(1)}, bf16[2,8,768]{2,1,0:T(8,128)(2,1)S(1)}, u32[]{:S(2)}, u32[]{:S(2)}) collective-permute-start(bf16[2,8,768]{2,1,0:T(8,128)(2,1)S(1)} %pad_maximum_fusion.16), channel_id=1, source_target_pairs={{0,8},{1,9},{2,10},{3,11},{4,12},{5,13},{6,14},{7,15},{8,0},{9,1},... | collective-permute-start | bytes 73736 | tf_op jit(solution)/shard_map/ppermute | solution.py:512
  17.9 8.2 %collective-permute-start.1 = (bf16[2,4,24,768]{3,2,1,0:T(8,128)(2,1)S(1)}, bf16[2,4,24,768]{3,2,1,0:T(8,128)(2,1)S(1)}, u32[]{:S(2)}, u32[]{:S(2)}) collective-permute-start(bf16[2,4,24,768]{3,2,1,0:T(8,128)(2,1)S(1)} %pad_maximum_fusion.11), channel_id=1, source_target_pairs={{0,8},{1,9},{2,10},{3,11},{4,12},{5,13},{6,14},{7,15},{8,0},{9,1},... | collective-permute-start | bytes 884744 | tf_op jit(solution)/shard_map/ppermute | solution.py:512
  26.3 7.3 %collective-permute-start.5 = (bf16[2,2,48,768]{3,2,0,1:T(8,128)(2,1)S(1)}, bf16[2,2,48,768]{3,2,0,1:T(8,128)(2,1)S(1)}, u32[]{:S(2)}, u32[]{:S(2)}) collective-permute-start(bf16[2,2,48,768]{3,2,0,1:T(8,128)(2,1)S(1)} %pad_maximum_fusion.12), channel_id=1, source_target_pairs={{0,2},{1,3},{2,0},{3,1},{4,6},{5,7},{6,4},{7,5},{8,10},{9,11},{10,... | collective-permute-start | bytes 884744 | tf_op jit(solution)/shard_map/ppermute | solution.py:512
  27.9 8.1 %collective-permute-start.4 = (bf16[2,2,56,768]{3,2,0,1:T(8,128)(2,1)S(1)}, bf16[2,2,56,768]{3,2,0,1:T(8,128)(2,1)S(1)}, u32[]{:S(2)}, u32[]{:S(2)}) collective-permute-start(bf16[2,2,56,768]{3,2,0,1:T(8,128)(2,1)S(1)} %pad_maximum_fusion.10), channel_id=1, source_target_pairs={{0,4},{1,5},{2,6},{3,7},{4,0},{5,1},{6,2},{7,3},{8,12},{9,13},{10,... | collective-permute-start | bytes 1032200 | tf_op jit(solution)/shard_map/ppermute | solution.py:512
  36.3 18.0 %collective-permute-start.7 = (bf16[2,2,2,48,768]{4,3,0,1,2:T(8,128)(2,1)S(1)}, bf16[2,2,2,48,768]{4,3,0,1,2:T(8,128)(2,1)S(1)}, u32[]{:S(2)}, u32[]{:S(2)}) collective-permute-start(bf16[2,2,2,48,768]{4,3,0,1,2:T(8,128)(2,1)S(1)} %pad_maximum_fusion.9), channel_id=1, source_target_pairs={{0,4},{1,5},{2,6},{3,7},{4,0},{5,1},{6,2},{7,3},{8,12},{9,13},{10,... | collective-permute-start | bytes 1769480 | tf_op jit(solution)/shard_map/ppermute | solution.py:512
  37.8 24.6 %collective-permute-start.6 = (bf16[2,2,2,56,768]{4,3,0,1,2:T(8,128)(2,1)S(1)}, bf16[2,2,2,56,768]{4,3,0,1,2:T(8,128)(2,1)S(1)}, u32[]{:S(2)}, u32[]{:S(2)}) collective-permute-start(bf16[2,2,2,56,768]{4,3,0,1,2:T(8,128)(2,1)S(1)} %pad_maximum_fusion.6), channel_id=1, source_target_pairs={{0,2},{1,3},{2,0},{3,1},{4,6},{5,7},{6,4},{7,5},{8,10},{9,11},{10,... | collective-permute-start | bytes 2064392 | tf_op jit(solution)/shard_map/ppermute | solution.py:512
  38.4 54.8 %all-to-all-start = ((bf16[32,40,768]{2,1,0:T(8,128)(2,1)}), bf16[32,40,768]{2,1,0:T(8,128)(2,1)}, u32[]{:S(2)}, u32[]{:S(2)}) async-start(bf16[32,40,768]{2,1,0:T(8,128)(2,1)} %bitcast.27), calls=%async_computation | async-start | bytes 3932160 | tf_op jit(solution)/shard_map/all_to_all | solution.py:507
  62.7 3.0 collective-permute-start.9
  62.8 6.5 %collective-permute-start.8 = (bf16[2,2,2,2,56,768]{5,4,0,1,2,3:T(8,128)(2,1)S(1)}, bf16[2,2,2,2,56,768]{5,4,0,1,2,3:T(8,128)(2,1)}, u32[]{:S(2)}, u32[]{:S(2)}) collective-permute-start(bf16[2,2,2,2,56,768]{5,4,0,1,2,3:T(8,128)(2,1)S(1)} %pad_maximum_fusion.3), channel_id=1, source_target_pairs={{0,1},{1,0},{2,3},{3,2},{4,5},{5,4},{6,7},{7,6},{8,9},{9,8},{10,11... | collective-permute-start | bytes 4128776 | tf_op jit(solution)/shard_map/ppermute | solution.py:512
  93.2 30.2 %all-to-all-start.2 = ((bf16[32,40,384]{2,1,0:T(8,128)(2,1)}), bf16[32,40,384]{2,1,0:T(8,128)(2,1)}, u32[]{:S(2)}, u32[]{:S(2)}) async-start(bf16[32,40,384]{2,1,0:T(8,128)(2,1)} %bitcast.236), calls=%async_computation.2 | async-start | bytes 1966080 | tf_op jit(solution)/shard_map/all_to_all | solution.py:507
  123.5 28.7 %all-to-all-start.1 = ((bf16[32,40,384]{2,1,0:T(8,128)(2,1)}), bf16[32,40,384]{2,1,0:T(8,128)(2,1)S(1)}, u32[]{:S(2)}, u32[]{:S(2)}) async-start(bf16[32,40,384]{2,1,0:T(8,128)(2,1)} %bitcast.238), calls=%async_computation.1 | async-start | bytes 1966080 | tf_op jit(solution)/shard_map/all_to_all | solution.py:507
  153.1 51.4 %all-to-all-start.3 = ((bf16[32,40,768]{2,1,0:T(8,128)(2,1)}), bf16[32,40,768]{2,1,0:T(8,128)(2,1)S(1)}, u32[]{:S(2)}, u32[]{:S(2)}) async-start(bf16[32,40,768]{2,1,0:T(8,128)(2,1)} %bitcast.235), calls=%async_computation.3 | async-start | bytes 3932160 | tf_op jit(solution)/shard_map/all_to_all | solution.py:507
  205.8 61.3 %all-to-all-start.4 = ((bf16[32,40,768]{2,1,0:T(8,128)(2,1)}), bf16[32,40,768]{2,1,0:T(8,128)(2,1)}, u32[]{:S(2)}, u32[]{:S(2)}) async-start(bf16[32,40,768]{2,1,0:T(8,128)(2,1)} %bitcast.233), calls=%async_computation.4 | async-start | bytes 3932160 | tf_op jit(solution)/shard_map/all_to_all | solution.py:507
  304.2 3.8 %collective-permute-start.10 = (bf16[1,2,2,2,2,72,768]{6,5,1,2,4,3,0:T(8,128)(2,1)S(1)}, bf16[1,2,2,2,2,72,768]{6,5,1,2,4,3,0:T(8,128)(2,1)S(1)}, u32[]{:S(2)}, u32[]{:S(2)}) collective-permute-start(bf16[1,2,2,2,2,72,768]{6,5,1,2,4,3,0:T(8,128)(2,1)S(1)} %select_bitcast_fusion), channel_id=1, source_target_pairs={{0,1},{1,0},{2,3},{3,2},{4,5},{5,4},{6,7},{7,6},{8,9},{9,8},{10,11... | collective-permute-start | bytes 5308424 | tf_op jit(solution)/shard_map/ppermute | solution.py:512
  304.8 5.8 %collective-permute-start.12 = (bf16[1,2,2,2,2,24,768]{6,5,1,2,4,3,0:T(8,128)(2,1)S(1)}, bf16[1,2,2,2,2,24,768]{6,5,1,2,4,3,0:T(8,128)(2,1)S(1)}, u32[]{:S(2)}, u32[]{:S(2)}) collective-permute-start(bf16[1,2,2,2,2,24,768]{6,5,1,2,4,3,0:T(8,128)(2,1)S(1)} %select_bitcast_fusion.7), channel_id=1, source_target_pairs={{0,1},{1,0},{2,3},{3,2},{4,5},{5,4},{6,7},{7,6},{8,9},{9,8},{10,11... | collective-permute-start | bytes 1769480 | tf_op jit(solution)/shard_map/ppermute | solution.py:512
  308.6 15.6 %collective-permute-start.11 = (bf16[1,2,2,2,48,768]{5,4,1,2,3,0:T(8,128)(2,1)S(1)}, bf16[1,2,2,2,48,768]{5,4,1,2,3,0:T(8,128)(2,1)S(1)}, u32[]{:S(2)}, u32[]{:S(2)}) collective-permute-start(bf16[1,2,2,2,48,768]{5,4,1,2,3,0:T(8,128)(2,1)S(1)} %fusion.10), channel_id=1, source_target_pairs={{0,2},{1,3},{2,0},{3,1},{4,6},{5,7},{6,4},{7,5},{8,10},{9,11},{10,... | collective-permute-start | bytes 1769480 | tf_op jit(solution)/shard_map/ppermute | solution.py:512
  311.0 15.2 %collective-permute-start.13 = (bf16[1,2,2,2,48,768]{5,4,1,2,3,0:T(8,128)(2,1)S(1)}, bf16[1,2,2,2,48,768]{5,4,1,2,3,0:T(8,128)(2,1)S(1)}, u32[]{:S(2)}, u32[]{:S(2)}) collective-permute-start(bf16[1,2,2,2,48,768]{5,4,1,2,3,0:T(8,128)(2,1)S(1)} %fusion.11), channel_id=1, source_target_pairs={{0,4},{1,5},{2,6},{3,7},{4,0},{5,1},{6,2},{7,3},{8,12},{9,13},{10,... | collective-permute-start | bytes 1769480 | tf_op jit(solution)/shard_map/ppermute | solution.py:512
  327.2 9.0 %collective-permute-start.15 = (bf16[1,2,2,48,768]{4,3,1,2,0:T(8,128)(2,1)}, bf16[1,2,2,48,768]{4,3,1,2,0:T(8,128)(2,1)}, u32[]{:S(2)}, u32[]{:S(2)}) collective-permute-start(bf16[1,2,2,48,768]{4,3,1,2,0:T(8,128)(2,1)} %fusion.18), channel_id=1, source_target_pairs={{0,2},{1,3},{2,0},{3,1},{4,6},{5,7},{6,4},{7,5},{8,10},{9,11},{10,... | collective-permute-start | bytes 884744 | tf_op jit(solution)/shard_map/ppermute | solution.py:512
  328.3 9.0 %collective-permute-start.14 = (bf16[1,2,2,48,768]{4,3,1,2,0:T(8,128)(2,1)}, bf16[1,2,2,48,768]{4,3,1,2,0:T(8,128)(2,1)S(1)}, u32[]{:S(2)}, u32[]{:S(2)}) collective-permute-start(bf16[1,2,2,48,768]{4,3,1,2,0:T(8,128)(2,1)} %fusion.17), channel_id=1, source_target_pairs={{0,4},{1,5},{2,6},{3,7},{4,0},{5,1},{6,2},{7,3},{8,12},{9,13},{10,... | collective-permute-start | bytes 884744 | tf_op jit(solution)/shard_map/ppermute | solution.py:512
  331.6 15.1 %all-to-all-start.5 = ((bf16[32,32,128]{2,1,0:T(8,128)(2,1)}), bf16[32,32,128]{2,1,0:T(8,128)(2,1)S(1)}, u32[]{:S(2)}, u32[]{:S(2)}) async-start(bf16[32,32,128]{2,1,0:T(8,128)(2,1)} %pad_maximum_fusion.13), calls=%async_computation.5 | async-start | bytes 524288 | tf_op jit(solution)/shard_map/all_to_all | solution.py:507
  337.4 12.2 %collective-permute-start.16 = (bf16[1,2,96,768]{3,2,1,0:T(8,128)(2,1)S(1)}, bf16[1,2,96,768]{3,2,1,0:T(8,128)(2,1)S(1)}, u32[]{:S(2)}, u32[]{:S(2)}) collective-permute-start(bf16[1,2,96,768]{3,2,1,0:T(8,128)(2,1)S(1)} %fusion.19), channel_id=1, source_target_pairs={{0,8},{1,9},{2,10},{3,11},{4,12},{5,13},{6,14},{7,15},{8,0},{9,1},... | collective-permute-start | bytes 884744 | tf_op jit(solution)/shard_map/ppermute | solution.py:512
  349.7 9.5 %collective-permute-start.17 = (bf16[1,96,768]{2,1,0:T(8,128)(2,1)S(1)}, bf16[1,96,768]{2,1,0:T(8,128)(2,1)S(1)}, u32[]{:S(2)}, u32[]{:S(2)}) collective-permute-start(bf16[1,96,768]{2,1,0:T(8,128)(2,1)S(1)} %fusion.20), channel_id=1, source_target_pairs={{0,16},{1,17},{2,18},{3,19},{4,20},{5,21},{6,22},{7,23},{8,24},{9,... | collective-permute-start | bytes 442376 | tf_op jit(solution)/shard_map/ppermute | solution.py:512
  (36 other events, 175.4 us)
